TPU v7x, 128 devices: a whole 4x4x4 slice. The times are simulated.
128 devices in a mesh: member: 4 (over z_hi, core), space: 32 (over y, x, z_lo).
Axes of the slice: x: 4, y: 4, z: 4 (z_hi: 2, z_lo: 2; z = z_hi * 2 + z_lo), core: 2. Of those that a mesh axis runs over, the one named last changes fastest.
Arguments:
- hidden: bfloat16 [16, 2048, 1024], P('member', 'space')
- grid_state: bfloat16 [16384, 1024], P('space'), may hold values from -6 to 6
- project_weight: bfloat16 [1024, 1024], replicated, may hold values from -0.1875 to 0.1875
- node_weight: bfloat16 [1024, 1024], replicated, may hold values from -0.1875 to 0.1875
- output_weight: bfloat16 [1024, 100], replicated, may hold values from -0.1875 to 0.1875
- prior_state: float32 [100, 16384], P(None, 'space'), may hold values from -6 to 6
- target: float32 [100, 16384], P(None, 'space'), may hold values from -6 to 6
- area_weight: float32 [16384], P('space'), as said below
- variable_weight: float32 [100], replicated, may hold values from 0.3 to 3
- edge_source: int32 [65536], P('space'), may hold values from 0 to 95, as said below
- edge_target: int32 [65536], P('space'), may hold values from 0 to 511, as said below
- edge_count: int32 [32], P('space'), may hold values from 1024 to 2048, as said below
- send_index: int32 [64, 16], P('space'), may hold values from 0 to 63, as said below
Outputs:
- grad_hidden: bfloat16 [16, 2048, 1024], P('member', 'space')
- grad_project: float32 [1024, 1024], P('space')
- grad_node: float32 [1024, 1024], P('space')
- grad_output: float32 [1024, 100], P('space')
- crps_loss: float32 [], replicated
Inputs may be any that keep to these rules, and one draw needn't show every extreme that they name: `edge_count`: within each shard, live slots come first and their points never fall; every point has 2 to 4 live edges; in every draw one shard has 4 for every point and another has 2 for every point. `edge_source`: rows 64 and above only in live slots; rows from 64 to 79 never in shard 0, rows from 80 on never in the last shard; slots past the live count hold 0. `edge_target`: slots past the live count hold 511. `send_index`: each row holds distinct, increasing nodes; row 2s lies among the first 32 nodes of shard s, row 2s+1 among its last 32. `area_weight`: Positive.
All inputs are finite; a program needn't handle non-finite values.
Results may differ from a plain program's by a relative error of at most 0.012.
The roundings to bfloat16 on the way count: a program that leaves them out, or rounds other values in their place, can miss the bound.
Values may be sent and summed in bfloat16 or wider, within the bound.
No kernel may reach another device: no remote copies, remote signals or barrier semaphores. Data moves between devices by JAX's collectives and lax.ppermute only.
A program may use at most 256 MiB of HBM per device.

v0:
```python
import jax
import jax.numpy as jnp
from jax import lax
from jax.sharding import PartitionSpec as P

SQRT_TWO_PI = 0.7978845608028654
CUBIC = 0.044715
ALPHA = 0.95
SOFT_EDGE = 0.05


def with_halo(block, sides, width):
    for axis, dim in sides:
        count = lax.axis_size(axis)
        forward = [(i, i + 1) for i in range(count - 1)]
        backward = [(target, source) for source, target in forward]
        low = lax.ppermute(
            lax.slice_in_dim(block, block.shape[dim] - width, None, axis=dim), axis, forward
        )
        high = lax.ppermute(lax.slice_in_dim(block, 0, width, axis=dim), axis, backward)
        block = jnp.concatenate([low, block, high], axis=dim)
    return block


def gelu_tanh(value):
    tanh_arg = SQRT_TWO_PI * (value + CUBIC * value * value * value)
    return 0.5 * value * (1.0 + jnp.tanh(tanh_arg))


def gelu_slope(value):
    tanh_arg = SQRT_TWO_PI * (value + CUBIC * value * value * value)
    tangent = jnp.tanh(tanh_arg)
    return 0.5 * (1.0 + tangent) + 0.5 * value * (1.0 - tangent * tangent) * SQRT_TWO_PI * (
        1.0 + 3.0 * CUBIC * value * value
    )


def soft_abs(value):
    return jnp.sqrt(value * value + SOFT_EDGE * SOFT_EDGE) - SOFT_EDGE


def soft_sign(value):
    return value / jnp.sqrt(value * value + SOFT_EDGE * SOFT_EDGE)


def crps_terms(own_preds, ensemble_preds, truth_rows, weight_map):
    member_count = ensemble_preds.shape[0]
    fairness = 1.0 - (1.0 - ALPHA) / member_count
    spread = own_preds[:, None] - ensemble_preds[None]
    pair_abs = jnp.sum(soft_abs(spread), axis=1)
    pair_sign = jnp.sum(soft_sign(spread), axis=1)
    misfit = own_preds - truth_rows[None]
    partial_sum = jnp.sum(
        weight_map[None]
        * (
            soft_abs(misfit) / member_count
            - fairness / (2.0 * member_count * (member_count - 1)) * pair_abs
        )
    )
    gradient = weight_map[None] * (soft_sign(misfit) - fairness / (member_count - 1) * pair_sign)
    return (gradient, partial_sum)


def shards(
    hidden,
    grid_state,
    project_weight,
    node_weight,
    output_weight,
    prior_state,
    target,
    area_weight,
    variable_weight,
    edge_source,
    edge_target,
    edge_count,
    send_index,
):
    members, own_nodes, model_width = hidden.shape
    points = grid_state.shape[0]
    send_rows = send_index.shape[1]
    variables = output_weight.shape[1]
    live_mask = (jnp.arange(edge_source.shape[0], dtype=jnp.int32) < edge_count[0]).astype(
        jnp.float32
    )[:, None]
    grid_edge = grid_state[edge_target].astype(jnp.float32)
    packed = jnp.stack([hidden[:, send_index[0]], hidden[:, send_index[1]]])
    rim_rows = with_halo(packed, (("space", 0),), 1)
    source_rows = jnp.concatenate([hidden, rim_rows[0], rim_rows[3]], axis=1)
    projected = jnp.einsum(
        "mnh,hk->mnk", source_rows, project_weight, preferred_element_type=jnp.float32
    ).astype(jnp.bfloat16)
    pre_act = projected[:, edge_source].astype(jnp.float32) + grid_edge[None]

    def point_sums(edge_values):
        return jax.ops.segment_sum(
            edge_values, edge_target, num_segments=points, indices_are_sorted=True
        )

    summed = jax.vmap(point_sums)(gelu_tanh(pre_act) * live_mask[None]).astype(jnp.bfloat16)
    node_pre = jnp.einsum("mgh,hk->mgk", summed, node_weight, preferred_element_type=jnp.float32)
    node_out = gelu_tanh(node_pre).astype(jnp.bfloat16)
    pred = prior_state[None] + jnp.einsum(
        "mgh,hv->mvg", node_out, output_weight, preferred_element_type=jnp.float32
    )
    weight_map = variable_weight[:, None] * area_weight[None, :]
    ensemble_preds = lax.all_gather(pred, "member", axis=0, tiled=True)
    gradient, partial_sum = crps_terms(pred, ensemble_preds, target, weight_map)
    grad_pred = gradient.astype(jnp.bfloat16)
    node_grad = jnp.einsum(
        "mvg,hv->mgh", grad_pred, output_weight, preferred_element_type=jnp.float32
    )
    node_pre_grad = (node_grad * gelu_slope(node_pre)).astype(jnp.bfloat16)
    summed_grad = jnp.einsum(
        "mgk,hk->mgh", node_pre_grad, node_weight, preferred_element_type=jnp.float32
    )
    table_rows = projected.shape[1]
    row_table = (jnp.arange(table_rows, dtype=jnp.int32)[:, None] == edge_source[None, :]).astype(
        jnp.float32
    )
    edge_grad = summed_grad[:, edge_target] * gelu_slope(pre_act) * live_mask[None]
    table_grad = jnp.einsum(
        "re,mek->mrk",
        row_table,
        edge_grad,
        precision=lax.Precision.HIGHEST,
        preferred_element_type=jnp.float32,
    )
    back_rows = jnp.stack(
        [table_grad[:, own_nodes : own_nodes + send_rows], table_grad[:, own_nodes + send_rows :]]
    )
    back_rim = with_halo(back_rows.astype(jnp.bfloat16), (("space", 0),), 1).astype(back_rows.dtype)
    own_grad = (
        table_grad[:, :own_nodes]
        .at[:, send_index[0]]
        .add(back_rim[0])
        .at[:, send_index[1]]
        .add(back_rim[3])
    )
    projected_grad = own_grad.astype(jnp.bfloat16)
    grad_hidden = jnp.einsum(
        "mnk,hk->mnh", projected_grad, project_weight, preferred_element_type=jnp.float32
    ).astype(jnp.bfloat16)
    project_term = jnp.einsum(
        "mnh,mnk->hk", hidden, projected_grad, preferred_element_type=jnp.float32
    )
    node_term = jnp.einsum("mgh,mgk->hk", summed, node_pre_grad, preferred_element_type=jnp.float32)
    output_term = jnp.einsum("mgh,mvg->hv", node_out, grad_pred, preferred_element_type=jnp.float32)
    space_count = lax.axis_size("space")
    total_points = points * space_count
    share_rows = model_width // space_count
    project_sum, node_sum, output_sum, loss_sum = lax.psum(
        (project_term, node_term, output_term, partial_sum), ("member", "space")
    )
    first_row = lax.axis_index("space") * share_rows
    project_sum = lax.dynamic_slice_in_dim(project_sum, first_row, share_rows, 0)
    node_sum = lax.dynamic_slice_in_dim(node_sum, first_row, share_rows, 0)
    output_sum = lax.dynamic_slice_in_dim(output_sum, first_row, share_rows, 0)
    crps_loss = loss_sum / (total_points * variables)
    return (
        grad_hidden,
        project_sum / total_points,
        node_sum / total_points,
        output_sum / total_points,
        crps_loss,
    )


def solution(mesh):
    placed = (
        P("member", "space", None),
        P("space", None),
        P(),
        P(),
        P(),
        P(None, "space"),
        P(None, "space"),
        P("space"),
        P(),
        P("space"),
        P("space"),
        P("space"),
        P("space", None),
    )
    return jax.shard_map(
        shards,
        mesh=mesh,
        in_specs=placed,
        out_specs=(
            P("member", "space", None),
            P("space", None),
            P("space", None),
            P("space", None),
            P(),
        ),
        check_vma=False,
    )
```

profile of v0, /device:TPU:1, one launch (start us, length us, event | category | flops | bytes accessed | tf_op | source)
XLA Modules:
  0.0 858.9 jit_solution(10837654683752665959)
XLA Ops:
  7.2 0.0 copy-start
  7.2 0.0 all-gather.2.cloned.1.call-start
  7.2 0.9 fusion.69
  8.1 1.7 gather_fusion
  9.8 5.0 collective-permute-start
  14.9 1.7 gather_fusion.1
  16.6 1.3 collective-permute-start.1
  17.9 0.7 fusion.66
  18.6 0.7 fusion.67
  19.3 9.6 %gather_fusion.3 = bf16[2048,1024]{1,0:T(8,128)(2,1)} fusion(bf16[512,1024]{1,0:T(8,128)(2,1)S(1)} %copy-done.2, s32[2048]{0:T(1024)S(1)} %fusion.67), kind=kCustom, calls=%fused_computation.3 | custom fusion | bytes 8396800 | tf_op jit(solution)/shard_map/gather | solution.py:86
  28.9 6.6 convert_element_type.45
  36.2 0.0 collective-permute-done
  36.2 0.0 collective-permute-done.1
  36.2 2.0 fusion.47
  38.2 0.6 copy.72
  38.8 30.4 %gather_fusion.2 = bf16[2048,4,1024]{2,1,0:T(4,128)(2,1)} fusion(bf16[4,96,1024]{2,0,1:T(4,128)(2,1)S(1)} %copy.72, s32[2048]{0:T(1024)S(1)} %fusion.66), kind=kCustom, calls=%fused_computation.2 | custom fusion | bytes 33562624 | tf_op jit(solution)/shard_map/gather | solution.py:93
  69.2 25.6 %fusion.10 = f32[2048,4,1024]{2,0,1:T(8,128)} fusion(f32[2048,1024]{1,0:T(8,128)} %convert_element_type.45, f32[2048]{0:T(1024)S(1)} %fusion.68, bf16[2048,4,1024]{2,1,0:T(4,128)(2,1)} %gather_fusion.2), kind=kLoop, calls=%fused_computation.22 | loop fusion | flops 92274688 | bytes 58728448 | tf_op jit(solution)/shard_map/mul | solution.py:100
  94.9 37.9 %copy.74 = f32[2048,4,1024]{2,1,0:T(4,128)} copy(f32[2048,4,1024]{2,0,1:T(8,128)} %fusion.10) | data formatting | bytes 67108864 | tf_op jit(solution)/shard_map/mul | solution.py:100
  132.8 5.4 broadcast_in_dim.8
  138.2 296.4 %scatter_fusion = f32[4,512,1024]{2,0,1:T(4,128)} fusion(f32[4,512,1024]{2,0,1:T(4,128)} %broadcast_in_dim.8, s32[2048]{0:T(1024)S(1)} %copy-done.12, f32[2048,4,1024]{2,1,0:T(4,128)} %copy.74), kind=kCustom, calls=%fused_computation.5 | custom fusion | flops 8388608 | bytes 100671488 | tf_op jit(solution)/shard_map/vmap()/scatter-add | solution.py:96
  434.5 7.4 convert_element_type.47
  442.0 7.6 copy.84
  449.6 10.9 %multiply_convert_fusion = (bf16[4,512,1024]{2,1,0:T(8,128)(2,1)S(1)}, f32[4,512,1024]{2,1,0:T(8,128)}) fusion(bf16[4,512,1024]{1,2,0:T(8,128)(2,1)} %copy.84, bf16[1024,1024]{1,0:T(8,128)(2,1)S(1)} %copy-done), kind=kOutput, calls=%fused_computation.50 | convolution fusion | flops 4313841664 | bytes 18874368 | tf_op jit(solution)/shard_map/mgh,hk->mgk/dot_general | solution.py:101
  460.5 2.0 copy-done.3
  462.6 2.4 fusion.50
  464.9 0.0 all-gather.2.cloned.1.call-update
  465.0 0.0 all-reduce.3.cloned.1.call-start
  465.0 0.8 broadcast_multiply_fusion
  465.8 40.9 %all-gather.2.cloned.1.call-done = f32[16,100,512]{2,1,0:T(8,128)} async-done(((f32[4,100,512]{2,1,0:T(8,128)}), f32[16,100,512]{2,1,0:T(8,128)}) %all-gather.2.cloned.1.call-update) | async-done | bytes 3276816 | tf_op jit(solution)/shard_map/all_gather | solution.py:107
  506.7 3.9 copy.76
  510.6 16.4 %fusion.28 = (f32[4,100,512]{2,1,0:T(8,128)S(1)}, f32[4,100,512]{2,1,0:T(8,128)S(1)}) fusion(f32[16,100,512]{2,0,1:T(8,128)S(1)} %copy.76, f32[4,100,512]{2,1,0:T(8,128)} %fusion.50), kind=kLoop, calls=%fused_computation.40 | loop fusion | flops 22528000 | bytes 5734400 | tf_op jit(solution)/shard_map/reduce_sum | solution.py:50
  527.0 2.2 multiply_reduce_fusion
  529.2 7.7 fusion.35
  537.0 6.1 convolution_bitcast_fusion
  543.1 7.2 fusion.36
  550.3 12.0 %copy.77 = f32[4,512,1024]{2,0,1:T(4,128)} copy(f32[4,512,1024]{2,1,0:T(8,128)} %fusion.36) | data formatting | bytes 16777216 | tf_op jit(solution)/shard_map/mgk,hk->mgh/dot_general | solution.py:114
  562.3 43.6 %gather_fusion.4 = f32[2048,4,1024]{2,1,0:T(4,128)} fusion(f32[4,512,1024]{2,0,1:T(4,128)} %copy.77, s32[2048]{0:T(1024)S(1)} %fusion.67), kind=kCustom, calls=%fused_computation.4 | custom fusion | bytes 67117056 | tf_op jit(solution)/shard_map/gather | solution.py:121
  605.9 56.8 %fusion.77 = (bf16[4,96,1024]{2,1,0:T(8,128)(2,1)S(1)}, f32[4,96,1024]{2,1,0:T(8,128)S(1)}) fusion(s32[2048]{0:T(1024)S(1)} %copy-done.13, f32[2048,4,1024]{2,1,0:T(4,128)} %gather_fusion.4, f32[2048,1024]{1,0:T(8,128)} %convert_element_type.45, f32[2048]{0:T(1024)S(1)} %fusion.68, bf16[2048,4,1024]{2,1,0:T(4,128)(2,1)} %gather_fusion.2), kind=kOutput, calls=%fused_computation.111 | convolution fusion | flops 9840427008 | bytes 61095936 | tf_op jit(solution)/shard_map/re,mek->mrk/dot_general | solution.py:122
  662.7 0.0 copy-start.17
  662.7 0.0 copy-start.15
  662.7 0.0 copy-start.7
  662.8 2.4 collective-permute-start.2
  665.2 1.3 collective-permute-start.3
  666.5 2.1 convolution_bitcast_fusion.3
  668.6 0.1 slice.44
  668.6 0.7 copy.79
  669.3 0.0 collective-permute-done.2
  669.3 3.1 collective-permute-done.3
  672.5 0.2 copy.80
  672.7 0.2 copy.81
  672.9 1.3 scatter_fusion.1
  674.2 1.3 scatter_fusion.2
  675.5 0.2 convert_element_type.52
  675.7 0.0 copy-start.1
  675.8 2.7 convolution_bitcast_fusion.1
  678.5 0.0 all-reduce.3.cloned.1.call-update
  678.5 67.9 %psum.31 = f32[]{:T(128)} all-reduce(f32[]{:T(128)} %get-tuple-element.35), channel_id=1, replica_groups=mesh['member'=4,'space'=32] {'member','space'}, use_global_device_ids=true, to_apply=%region_9.0 | all-reduce | flops 1 | bytes 8 | tf_op jit(solution)/shard_map/psum | solution.py:152
  747.1 3.1 fusion.51
  750.2 95.0 %all-reduce.3.cloned.1.call-done = (f32[1024,1024]{0,1:T(8,128)}, f32[1024,1024]{0,1:T(8,128)}, f32[1024,100]{1,0:T(8,128)}) async-done(((f32[1024,1024]{0,1:T(8,128)}, f32[1024,1024]{0,1:T(8,128)}, f32[1024,100]{1,0:T(8,128)}), (f32[1024,1024]{0,1:T(8,128)}, f32[1024,1024]{0,1:T(8,128)}, f32[1024,100]{1,0:T(8,128)})) %all-reduce.3.cloned.1.call-update) | async-done | bytes 8798224 | tf_op jit(solution)/shard_map/psum | solution.py:152
  845.2 1.2 dynamic-slice_multiply_fusion
  846.5 0.8 copy.88
  847.3 1.2 dynamic-slice_multiply_fusion.1
  848.6 0.8 copy.87
  849.4 1.3 dynamic-slice_multiply_fusion.2
  (40 shorter events, 0.1 us)
Async XLA Ops:
  7.2 442.4 %copy-start = (bf16[1024,1024]{1,0:T(8,128)(2,1)S(1)}, bf16[1024,1024]{1,0:T(8,128)(2,1)}, u32[]{:S(2)}) copy-start(bf16[1024,1024]{1,0:T(8,128)(2,1)} %param.16) | copy-start | bytes 6291460
  7.2 12.1 %copy-start.2 = (bf16[512,1024]{1,0:T(8,128)(2,1)S(1)}, bf16[512,1024]{1,0:T(8,128)(2,1)}, u32[]{:S(2)}) copy-start(bf16[512,1024]{1,0:T(8,128)(2,1)} %param.14) | copy-start | bytes 3145732
  7.2 499.5 %all-gather.2.cloned.1.call-start = ((), (), s32[]{:S(2)}) async-start(), calls=%async_computation | async-start | bytes 4259840 | tf_op jit(solution)/shard_map/all_gather | solution.py:107
  8.1 6.7 copy-start.14
  8.1 6.7 copy-start.16
  9.8 26.4 %collective-permute-start = (bf16[1,4,16,1024]{3,2,1,0:T(8,128)(2,1)S(1)}, bf16[1,4,16,1024]{3,2,1,0:T(8,128)(2,1)}, u32[]{:S(2)}, u32[]{:S(2)}) collective-permute-start(bf16[1,4,16,1024]{3,2,1,0:T(8,128)(2,1)S(1)} %bitcast.116), channel_id=1, source_target_pairs={{0,1},{1,2},{2,3},{3,4},{4,5},{5,6},{6,7},{7,8},{8,9},{9,10},{10,1... | collective-permute-start | bytes 393224 | tf_op jit(solution)/shard_map/ppermute | solution.py:17
  16.6 19.7 %collective-permute-start.1 = (bf16[1,4,16,1024]{3,2,1,0:T(8,128)(2,1)S(1)}, bf16[1,4,16,1024]{3,2,1,0:T(8,128)(2,1)}, u32[]{:S(2)}, u32[]{:S(2)}) collective-permute-start(bf16[1,4,16,1024]{3,2,1,0:T(8,128)(2,1)S(1)} %bitcast.117), channel_id=1, source_target_pairs={{1,0},{2,1},{3,2},{4,3},{5,4},{6,5},{7,6},{8,7},{9,8},{10,9},{11,1... | collective-permute-start | bytes 393224 | tf_op jit(solution)/shard_map/ppermute | solution.py:20
  28.9 7.3 copy-start.6
  28.9 7.3 copy-start.20
  132.8 5.4 copy-start.12
  449.6 13.0 %copy-start.10 = (f32[100,512]{1,0:T(8,128)S(1)}, f32[100,512]{1,0:T(8,128)}, u32[]{:S(2)}) copy-start(f32[100,512]{1,0:T(8,128)} %param.18) | copy-start | bytes 614404
  449.6 13.0 %copy-start.11 = (bf16[1024,100]{0,1:T(8,128)(2,1)S(1)}, bf16[1024,100]{0,1:T(8,128)(2,1)}, u32[]{:S(2)}) copy-start(bf16[1024,100]{0,1:T(8,128)(2,1)} %param.17) | copy-start | bytes 614404
  460.5 2.1 copy-start.3
  460.5 4.5 copy-start.18
  460.5 4.5 copy-start.19
  464.9 62.1 %copy-start.5 = (f32[4,100,512]{2,1,0:T(8,128)S(1)}, f32[4,100,512]{2,1,0:T(8,128)}, u32[]{:S(2)}) copy-start(f32[4,100,512]{2,1,0:T(8,128)} %fusion.50) | copy-start | bytes 2457604
  465.0 380.3 %all-reduce.3.cloned.1.call-start = ((), (), s32[]{:S(2)}) async-start(), calls=%async_computation.1 | async-start | bytes 17825792 | tf_op jit(solution)/shard_map/psum | solution.py:152
  506.7 20.3 %copy-start.9 = (f32[100,512]{1,0:T(8,128)S(1)}, f32[100,512]{1,0:T(8,128)}, u32[]{:S(2)}) copy-start(f32[100,512]{1,0:T(8,128)} %broadcast_multiply_fusion) | copy-start | bytes 614404
  529.2 7.7 copy-start.8
  562.3 43.6 %copy-start.13 = (s32[2048]{0:T(1024)S(1)}, s32[2048]{0:T(1024)}, u32[]{:S(2)}) copy-start(s32[2048]{0:T(1024)} %param.22) | copy-start | bytes 24580
  605.9 60.6 %copy-start.4 = (bf16[4,512,1024]{2,1,0:T(8,128)(2,1)S(1)}, bf16[4,512,1024]{2,1,0:T(8,128)(2,1)}, u32[]{:S(2)}) copy-start(bf16[4,512,1024]{2,1,0:T(8,128)(2,1)} %copy-done.3) | copy-start | bytes 12582916
  662.7 10.2 %copy-start.17 = (s32[16]{0:T(128)S(1)}, s32[16]{0:T(128)}, u32[]{:S(2)}) copy-start(s32[16]{0:T(128)} %copy-done.16) | copy-start | bytes 196
  662.7 11.5 %copy-start.15 = (s32[16]{0:T(128)S(1)}, s32[16]{0:T(128)}, u32[]{:S(2)}) copy-start(s32[16]{0:T(128)} %copy-done.14) | copy-start | bytes 196
  662.7 13.0 %copy-start.7 = (bf16[4,64,1024]{2,1,0:T(8,128)(2,1)S(1)}, bf16[4,64,1024]{2,1,0:T(8,128)(2,1)}, u32[]{:S(2)}) copy-start(bf16[4,64,1024]{2,1,0:T(8,128)(2,1)} %param.13) | copy-start | bytes 1572868
  662.8 6.6 collective-permute-start.2
  665.2 7.3 collective-permute-start.3
  675.7 175.0 %copy-start.1 = (bf16[1024,1024]{1,0:T(8,128)(2,1)S(1)}, bf16[1024,1024]{1,0:T(8,128)(2,1)}, u32[]{:S(2)}) copy-start(bf16[1024,1024]{1,0:T(8,128)(2,1)} %param.16) | copy-start | bytes 6291460
Sparse Core Ops, SparseCore 0:
  465.1 41.6 all-gather.1
  678.6 166.5 all-reduce.2
where the time goes:
time: 872 us; the launch traced here: 859 us
  other arithmetic  364 us (42%)
  local copies, waits for them, and re-layouts  159 us (18%)
  waiting for transfers between devices  139 us (16%)
  matrix products  101 us (12%)
  blocking collectives  67.9 us (8%)
  between operations  17 us (2%)
  starting transfers between devices  10.1 us (1%)
    scatter-add x1, other arithmetic, point_sums(): jax.ops.segment_sum(edge_values, edge_target, num_segments=points, indice...  296 us
    psum x1, waiting for transfers between devices, shards(): lax.psum((project_term, node_term, output_term, partial_sum), ('member',...  95 us
    psum x1, blocking collectives, shards(): lax.psum((project_term, node_term, output_term, partial_sum), ('member',...  67.9 us
    dot_general x1, matrix products, shards(): jnp.einsum('re,mek->mrk', row_table, edge_grad, precision=lax.Precision.H...  56.8 us
    gather x1, local copies, waits for them, and re-layouts, shards(): summed_grad[:, edge_target] * gelu_slope(pre_act) * live_mask[None]  43.6 us
    all_gather x1, waiting for transfers between devices, shards(): ensemble_preds = lax.all_gather(pred, 'member', axis=0, tiled=True)  40.9 us
    mul x1, local copies, waits for them, and re-layouts, shards(): gelu_tanh(pre_act) * live_mask[None]  37.9 us
    gather x1, local copies, waits for them, and re-layouts, shards(): pre_act = projected[:, edge_source].astype(jnp.float32) + grid_edge[None]  30.4 us
  transfers between devices with their start and end apart: 6, of which 3 were waited for; matrix products, arithmetic and copies ran while one was open for 3% of the time, Pallas kernels for 0%

commit v1 on v0

v1 whole, which is shorter than its diff:
```python
import functools

import jax
import jax.numpy as jnp
from jax import lax
from jax.experimental import pallas as pl
from jax.experimental.pallas import tpu as pltpu
from jax.sharding import PartitionSpec as P

SQRT_TWO_PI = 0.7978845608028654
CUBIC = 0.044715
ALPHA = 0.95
SOFT_EDGE = 0.05
DEGREE = 4
TABLE = 128
EMPTY = -64.0
CHUNK = 128
TILE = 256
VMEM_LIMIT = 56 * 1024 * 1024


def tanh_of(u):
    s = u * u
    return s, jnp.tanh(u * (SQRT_TWO_PI + (SQRT_TWO_PI * CUBIC) * s))


def gelu_twice(u):
    _, t = tanh_of(u)
    return u + u * t


def slope_twice(u):
    s, t = tanh_of(u)
    q = u * (SQRT_TWO_PI + (3.0 * SQRT_TWO_PI * CUBIC) * s)
    return (1.0 + t) * (1.0 + (1.0 - t) * q)


def dot(left, right):
    return lax.dot_general(
        left, right, (((1,), (0,)), ((), ())), preferred_element_type=jnp.float32
    )


def dot_nt(left, right):
    return lax.dot_general(
        left, right, (((1,), (1,)), ((), ())), preferred_element_type=jnp.float32
    )


def forward_kernel(
    rows_ref, project_ref, pick_ref, grid_ref, node_ref, output_ref, prior_ref,
    pred_ref, summed_ref, out_ref, comb_ref,
):
    members, table_rows, width = rows_ref.shape

    @pl.when(pl.program_id(0) == 0)
    def _():
        for m in range(members):
            comb_ref[m, :table_rows] = dot(rows_ref[m], project_ref[...]).astype(jnp.bfloat16)
            comb_ref[m, table_rows:TABLE] = jnp.full(
                (TABLE - table_rows, width), EMPTY, jnp.bfloat16
            )

    for m in range(members):
        comb_ref[m, TABLE:] = grid_ref[...]
    pick = pick_ref[0]
    for m in range(members):
        for h in range(0, width, TILE):
            u = dot(pick, comb_ref[m, :, h : h + TILE])
            twice = jnp.sum(gelu_twice(u).reshape(DEGREE, CHUNK, TILE), axis=0)
            summed_ref[m, :, h : h + TILE] = (0.5 * twice).astype(jnp.bfloat16)
    summed = summed_ref[...].reshape(members * CHUNK, width)
    for h in range(0, width, TILE):
        u = dot(summed, node_ref[:, h : h + TILE])
        value = (0.5 * gelu_twice(u)).astype(jnp.bfloat16)
        out_ref[:, :, h : h + TILE] = value.reshape(members, CHUNK, TILE)
    for m in range(members):
        pred_ref[m] = prior_ref[...] + dot_nt(output_ref[...], out_ref[m])[: prior_ref.shape[0]]


def slope_kernel(comb_ref, pick_ref, grid_ref, summed_ref, node_ref, edge_ref, point_ref, both_ref):
    members, _, width = comb_ref.shape
    pick = pick_ref[0]
    for m in range(members):
        both_ref[m, :TABLE] = comb_ref[m]
        both_ref[m, TABLE:] = grid_ref[...]
    for m in range(members):
        for h in range(0, width, TILE):
            u = dot(pick, both_ref[m, :, h : h + TILE])
            value = (0.5 * slope_twice(u)).astype(jnp.bfloat16)
            edge_ref[m, :, :, h : h + TILE] = value.reshape(DEGREE, CHUNK, TILE)
    summed = summed_ref[...].reshape(members * CHUNK, width)
    for h in range(0, width, TILE):
        u = dot(summed, node_ref[:, h : h + TILE])
        value = (0.5 * slope_twice(u)).astype(jnp.bfloat16)
        point_ref[:, :, h : h + TILE] = value.reshape(members, CHUNK, TILE)


def loss_kernel(
    own_ref, all_ref, truth_ref, area_ref, variable_ref, slope_ref, output_ref,
    grad_ref, pre_ref, loss_ref,
):
    members, variables, _ = own_ref.shape
    width = output_ref.shape[1]
    everyone = all_ref.shape[0]
    fairness = 1.0 - (1.0 - ALPHA) / everyone
    weight = variable_ref[...] * area_ref[...]
    truth = truth_ref[...]
    edge = SOFT_EDGE * SOFT_EDGE
    terms = jnp.zeros((variables, CHUNK), jnp.float32)
    grads = []
    for j in range(members):
        own = own_ref[j]
        pair_abs = jnp.full((variables, CHUNK), -everyone * SOFT_EDGE, jnp.float32)
        pair_sign = jnp.zeros((variables, CHUNK), jnp.float32)
        for k in range(everyone):
            d = own - all_ref[k]
            square = d * d + edge
            r = lax.rsqrt(square)
            pair_abs = pair_abs + square * r
            pair_sign = pair_sign + d * r
        d = own - truth
        square = d * d + edge
        r = lax.rsqrt(square)
        terms = terms + weight * (
            (square * r - SOFT_EDGE) / everyone
            - fairness / (2.0 * everyone * (everyone - 1)) * pair_abs
        )
        gradient = weight * (d * r - fairness / (everyone - 1) * pair_sign)
        grad_ref[j] = gradient.astype(jnp.bfloat16)
        padded = jnp.concatenate(
            [gradient, jnp.zeros((TABLE - variables, CHUNK), jnp.float32)], axis=0
        )
        grads.append(padded.T.astype(jnp.bfloat16))

    @pl.when(pl.program_id(0) == 0)
    def _():
        loss_ref[...] = jnp.zeros_like(loss_ref)

    loss_ref[...] += jnp.sum(terms.reshape(variables // 8, 8, CHUNK), axis=0)
    stacked = jnp.concatenate(grads, axis=0)
    for h in range(0, width, TILE):
        node_grad = dot(stacked, output_ref[:, h : h + TILE]).reshape(members, CHUNK, TILE)
        slope = slope_ref[:, :, h : h + TILE].astype(jnp.float32)
        pre_ref[:, :, h : h + TILE] = (node_grad * slope).astype(jnp.bfloat16)


def table_kernel(pre_ref, node_ref, slope_ref, place_ref, rows_ref, grad_ref, term_ref):
    members, points, _ = pre_ref.shape
    table_rows = grad_ref.shape[1]
    cast = []
    for m in range(members):
        summed_grad = dot_nt(pre_ref[m], node_ref[...])
        edge = [
            (summed_grad * slope_ref[m, k].astype(jnp.float32)).astype(jnp.bfloat16)
            for k in range(DEGREE)
        ]
        table = dot(place_ref[...], jnp.concatenate(edge, axis=0))[:table_rows]
        grad_ref[m] = table
        cast.append(table.astype(jnp.bfloat16))
    term_ref[...] = dot(rows_ref[...], jnp.concatenate(cast, axis=0)).astype(jnp.bfloat16)


def params():
    return pltpu.CompilerParams(
        dimension_semantics=("arbitrary",), vmem_limit_bytes=VMEM_LIMIT
    )


def whole(array):
    return pl.BlockSpec(array.shape, lambda c: (0,) * array.ndim)


def shards(
    hidden,
    grid_state,
    project_weight,
    node_weight,
    output_weight,
    prior_state,
    target,
    area_weight,
    variable_weight,
    edge_source,
    edge_target,
    edge_count,
    send_index,
):
    members, own_nodes, width = hidden.shape
    points = grid_state.shape[0]
    send_rows = send_index.shape[1]
    variables = output_weight.shape[1]
    slots = edge_source.shape[0]
    everyone = members * lax.axis_size("member")
    space = lax.axis_size("space")
    total_points = points * space
    table_rows = own_nodes + 2 * send_rows
    chunks = points // CHUNK
    padded = -(-variables // 8) * 8

    nodes = jnp.arange(own_nodes, dtype=jnp.int32)
    chosen = (send_index[:, :, None] == nodes).astype(jnp.bfloat16)
    packed = jnp.einsum(
        "dsn,mnh->dmsh", chosen, hidden, preferred_element_type=jnp.float32
    ).astype(jnp.bfloat16)
    forward = [(i, i + 1) for i in range(space - 1)]
    backward = [(i + 1, i) for i in range(space - 1)]
    from_left = lax.ppermute(packed[1], "space", forward)
    from_right = lax.ppermute(packed[0], "space", backward)

    edges = jnp.arange(slots, dtype=jnp.int32)
    live = edges < edge_count[0]
    owner = jnp.where(live, edge_target, points)
    point = jnp.arange(points, dtype=jnp.int32)
    start = jnp.sum((owner[:, None] < point[None, :]).astype(jnp.int32), axis=0)
    end = jnp.sum((owner[:, None] <= point[None, :]).astype(jnp.int32), axis=0)
    order = start[None, :] + jnp.arange(DEGREE, dtype=jnp.int32)[:, None]
    found = jnp.sum(
        jnp.where(order[:, None, :] == edges[None, :, None], edge_source[None, :, None], 0), axis=1
    )
    slot = jnp.where(order < end[None, :], found, table_rows)
    columns = jnp.arange(TABLE + CHUNK, dtype=jnp.int32)
    within = jnp.arange(CHUNK, dtype=jnp.int32)
    by_chunk = slot.reshape(DEGREE, chunks, CHUNK).transpose(1, 0, 2)
    pick = (
        (by_chunk[..., None] == columns) | ((within[:, None] + TABLE) == columns)
    ).astype(jnp.bfloat16).reshape(chunks, DEGREE * CHUNK, TABLE + CHUNK)
    place = (
        slot.reshape(1, DEGREE * points) == jnp.arange(TABLE, dtype=jnp.int32)[:, None]
    ).astype(jnp.bfloat16)
    output_rows = jnp.pad(output_weight.T, ((0, TABLE - variables), (0, 0)))
    prior = jnp.pad(prior_state, ((0, padded - variables), (0, 0)))
    truth = jnp.pad(target, ((0, padded - variables), (0, 0)))
    scale = jnp.pad(variable_weight, (0, padded - variables))[:, None]

    source_rows = jnp.concatenate([hidden, from_left, from_right], axis=1)

    chunk_rows = pl.BlockSpec((CHUNK, width), lambda c: (c, 0))
    member_rows = pl.BlockSpec((members, CHUNK, width), lambda c: (0, c, 0))
    pick_block = pl.BlockSpec((1, DEGREE * CHUNK, TABLE + CHUNK), lambda c: (c, 0, 0))
    by_variable = pl.BlockSpec((padded, CHUNK), lambda c: (0, c))
    own_block = pl.BlockSpec((members, padded, CHUNK), lambda c: (0, 0, c))
    per_point = jax.ShapeDtypeStruct((members, points, width), jnp.bfloat16)
    pred, summed, node_out, comb = pl.pallas_call(
        forward_kernel_with_table,
        grid=(chunks,),
        in_specs=[
            whole(source_rows), whole(project_weight), pick_block, chunk_rows,
            whole(node_weight), whole(output_rows), by_variable,
        ],
        out_specs=[
            own_block, member_rows, member_rows,
            pl.BlockSpec((members, TABLE, width), lambda c: (0, 0, 0)),
        ],
        out_shape=[
            jax.ShapeDtypeStruct((members, padded, points), jnp.float32), per_point, per_point,
            jax.ShapeDtypeStruct((members, TABLE, width), jnp.bfloat16),
        ],
        scratch_shapes=[pltpu.VMEM((members, TABLE + CHUNK, width), jnp.bfloat16)],
        compiler_params=params(),
        name="forward",
    )(source_rows, project_weight, pick, grid_state, node_weight, output_rows, prior)

    everyones = lax.all_gather(pred, "member", axis=0, tiled=True)

    edge_slope, node_slope = pl.pallas_call(
        slope_kernel,
        grid=(chunks,),
        in_specs=[whole(comb), pick_block, chunk_rows, member_rows, whole(node_weight)],
        out_specs=[
            pl.BlockSpec((members, DEGREE, CHUNK, width), lambda c: (0, 0, c, 0)), member_rows,
        ],
        out_shape=[
            jax.ShapeDtypeStruct((members, DEGREE, points, width), jnp.bfloat16), per_point,
        ],
        scratch_shapes=[pltpu.VMEM((members, TABLE + CHUNK, width), jnp.bfloat16)],
        compiler_params=params(),
        name="slopes",
    )(comb, pick, grid_state, summed, node_weight)

    grad_pred, node_pre_grad, loss_rows = pl.pallas_call(
        loss_kernel,
        grid=(chunks,),
        in_specs=[
            own_block,
            pl.BlockSpec((everyone, padded, CHUNK), lambda c: (0, 0, c)),
            by_variable,
            pl.BlockSpec((1, CHUNK), lambda c: (0, c)),
            whole(scale), member_rows, whole(output_rows),
        ],
        out_specs=[own_block, member_rows, pl.BlockSpec((8, CHUNK), lambda c: (0, 0))],
        out_shape=[
            jax.ShapeDtypeStruct((members, padded, points), jnp.bfloat16), per_point,
            jax.ShapeDtypeStruct((8, CHUNK), jnp.float32),
        ],
        compiler_params=params(),
        name="loss",
    )(pred, everyones, truth, area_weight[None, :], scale, node_slope, output_rows)

    node_term = jnp.einsum(
        "mgh,mgk->hk", summed, node_pre_grad, preferred_element_type=jnp.float32
    ).astype(jnp.bfloat16)
    output_term = jnp.einsum(
        "mgh,mvg->hv", node_out, grad_pred, preferred_element_type=jnp.float32
    )[:, :variables]
    loss_part = jnp.broadcast_to(jnp.sum(loss_rows), (width, 1))
    small_term = jnp.concatenate([output_term, loss_part], axis=1)

    source_columns = source_rows.reshape(members * table_rows, width).T
    table_grad, project_term = pl.pallas_call(
        table_kernel,
        grid=(width // TILE,),
        in_specs=[
            whole(node_pre_grad),
            pl.BlockSpec((TILE, width), lambda c: (c, 0)),
            pl.BlockSpec((members, DEGREE, points, TILE), lambda c: (0, 0, 0, c)),
            whole(place),
            whole(source_columns),
        ],
        out_specs=[
            pl.BlockSpec((members, table_rows, TILE), lambda c: (0, 0, c)),
            pl.BlockSpec((width, TILE), lambda c: (0, c)),
        ],
        out_shape=[
            jax.ShapeDtypeStruct((members, table_rows, width), jnp.float32),
            jax.ShapeDtypeStruct((width, width), jnp.bfloat16),
        ],
        compiler_params=params(),
        name="table",
    )(node_pre_grad, node_weight, edge_slope, place, source_columns)

    def reduce_rows(term):
        part = lax.psum_scatter(term, "space", scatter_dimension=0, tiled=True)
        return lax.psum(part.astype(jnp.float32), "member")

    node_sum = reduce_rows(node_term)
    small_sum = reduce_rows(small_term)
    project_sum = reduce_rows(project_term)

    left_back = lax.ppermute(
        table_grad[:, own_nodes : own_nodes + send_rows].astype(jnp.bfloat16), "space", backward
    )
    right_back = lax.ppermute(
        table_grad[:, own_nodes + send_rows :].astype(jnp.bfloat16), "space", forward
    )
    projected_grad = (
        table_grad[:, :own_nodes]
        + jnp.einsum(
            "sn,msh->mnh", chosen[1], left_back, preferred_element_type=jnp.float32
        )
        + jnp.einsum(
            "sn,msh->mnh", chosen[0], right_back, preferred_element_type=jnp.float32
        )
    ).astype(jnp.bfloat16)
    grad_hidden = jnp.einsum(
        "mnk,hk->mnh", projected_grad, project_weight, preferred_element_type=jnp.float32
    ).astype(jnp.bfloat16)
    return (
        grad_hidden,
        project_sum / total_points,
        node_sum / total_points,
        small_sum[:, :variables] / total_points,
        small_sum[0, variables] / (total_points * variables),
    )


def forward_kernel_with_table(*refs):
    inputs, (pred_ref, summed_ref, out_ref, table_ref, comb_ref) = refs[:7], refs[7:]
    forward_kernel(*inputs, pred_ref, summed_ref, out_ref, comb_ref)

    @pl.when(pl.program_id(0) == 0)
    def _():
        table_ref[...] = comb_ref[:, :TABLE]


def solution(mesh):
    placed = (
        P("member", "space", None),
        P("space", None),
        P(),
        P(),
        P(),
        P(None, "space"),
        P(None, "space"),
        P("space"),
        P(),
        P("space"),
        P("space"),
        P("space"),
        P("space", None),
    )
    return jax.shard_map(
        shards,
        mesh=mesh,
        in_specs=placed,
        out_specs=(
            P("member", "space", None),
            P("space", None),
            P("space", None),
            P("space", None),
            P(),
        ),
        check_vma=False,
    )
```

time: 872 us -> 615 us (0.71); the launches traced: 859 us -> 614 us
  other arithmetic: 364 us -> 11.3 us
  waiting for transfers between devices: 139 us -> 424 us
  local copies, waits for them, and re-layouts: 159 us -> 10.1 us
  matrix products: 101 us -> 17.2 us
  Pallas kernels: 0 us -> 83.7 us
  blocking collectives: 67.9 us -> 41.2 us
    reduce_scatter x0 -> x2, waiting for transfers between devices: none -> 324 us  [reduce_rows(): part = lax.psum_scatter(term, 'space', scatter_dimension=0, tiled=True)]
    scatter-add x3 -> x0, other arithmetic: 299 us -> none  [the longest x1 296 us: point_sums(): jax.ops.segment_sum(edge_values, edge_target, num_segments=points, indice...]
    psum x1 -> x0, waiting for transfers between devices: 95 us -> none  [shards(): lax.psum((project_term, node_term, output_term, partial_sum), ('member',...]
    dot_general x7 -> x2, matrix products: 89.7 us -> 1.72 us  [the longest x1 1.38 us: shards(): jnp.einsum('dsn,mnh->dmsh', chosen, hidden, preferred_element_type=jnp.fl...]
    gather x5 -> x0, local copies, waits for them, and re-layouts: 87 us -> none  [the longest x1 43.6 us: shards(): summed_grad[:, edge_target] * gelu_slope(pre_act) * live_mask[None]]
    unnamed x2 -> x5, waiting for transfers between devices: 0.03 us -> 86.7 us
    pallas_call x0 -> x4, Pallas kernels: none -> 83.7 us  [the longest x1 29.5 us: shards(): pl.pallas_call(slope_kernel, grid=(chunks,), in_specs=[whole(comb), pick_...]
    mul x1 -> x0, local copies, waits for them, and re-layouts: 37.9 us -> none  [shards(): gelu_tanh(pre_act) * live_mask[None]]
  transfers between devices with their start and end apart: 6 -> 8, of which waited for: 3 -> 6; matrix products, arithmetic and copies ran while one was open for 3% -> 5% of each run, Pallas kernels for 0% -> 8%
where the time goes in v1:
time: 615 us; the launch traced here: 614 us
  waiting for transfers between devices  424 us (69%)
  Pallas kernels  83.7 us (14%)
  blocking collectives  41.2 us (7%)
  matrix products  17.2 us (3%)
  between operations  16.4 us (3%)
  other arithmetic  11.3 us (2%)
  local copies, waits for them, and re-layouts  10.1 us (2%)
  starting transfers between devices  9.81 us (2%)
    reduce_scatter x2, waiting for transfers between devices, reduce_rows(): part = lax.psum_scatter(term, 'space', scatter_dimension=0, tiled=True)  324 us
    unnamed x5, waiting for transfers between devices  86.7 us
    psum x1, blocking collectives, reduce_rows(): return lax.psum(part.astype(jnp.float32), 'member')  41.2 us
    pallas_call x1, Pallas kernels, shards(): pl.pallas_call(slope_kernel, grid=(chunks,), in_specs=[whole(comb), pick_...  29.5 us
    pallas_call x1, Pallas kernels, shards(): pl.pallas_call(forward_kernel_with_table, grid=(chunks,), in_specs=[whole...  23.7 us
    pallas_call x1, Pallas kernels, shards(): pl.pallas_call(table_kernel, grid=(width // TILE,), in_specs=[whole(node_...  20.9 us
  transfers between devices with their start and end apart: 8, of which 6 were waited for; matrix products, arithmetic and copies ran while one was open for 5% of the time, Pallas kernels for 8%

profile of v1, /device:TPU:1, one launch (start us, length us, event | category | flops | bytes accessed | tf_op | source)
XLA Modules:
  0.0 614.2 jit_solution(11457081320599564879)
XLA Ops:
  7.2 0.0 copy-start.3
  7.2 0.0 all-gather.2.cloned.1.call-start
  7.2 1.4 fusion.10
  8.6 4.4 collective-permute-start
  13.0 1.3 collective-permute-start.1
  15.0 0.7 fusion.15
  15.7 1.0 convert_reduce_fusion
  16.7 2.7 select_reduce_fusion
  19.4 0.1 iota_compare_fusion.5
  19.6 1.3 fusion.3.refs_2_.pick_ref
  20.9 1.1 constant_dynamic-update-slice_fusion.2
  21.9 1.7 pad.16.refs_5_.output_ref
  23.6 0.0 copy-done.3
  23.6 0.7 pad.17.refs_6_
  24.3 0.0 collective-permute-done
  24.3 0.0 collective-permute-done.1
  24.4 0.0 copy-start.1
  24.4 0.9 copy-done.1
  25.2 0.0 copy-start.4
  25.2 0.0 copy-start.7
  25.2 23.7 %forward.1 = (f32[4,104,512]{2,1,0:T(8,128)}, bf16[4,512,1024]{2,1,0:T(8,128)(2,1)}, bf16[4,512,1024]{2,1,0:T(8,128)(2,1)}, bf16[4,128,1024]{2,1,0:T(8,128)(2,1)}) custom-call(bf16[4,96,1024]{2,1,0:T(8,128)(2,1)} %copy-done.1, bf16[1024,1024]{1,0:T(8,128)(2,1)} %refs_1_.1, bf16[4,512,256]{2,1,0:T(8,128)(2,1)} %fusion.3.refs_2_.pick_ref, ...), custom_call_target="tpu_custom_call" | custom-call | tf_op jit(solution)/shard_map/forward/pallas_call | solution.py:244
  49.0 0.0 all-gather.2.cloned.1.call-update
  49.0 0.2 reduce-scatter.10.cloned.1.call-start
  49.2 0.0 copy-done.4
  49.3 0.7 pad.18.truth_ref
  50.0 0.0 copy-done.7
  50.0 0.7 copy.30.variable_ref
  50.7 29.5 %slopes.1 = (bf16[4,4,512,1024]{3,2,1,0:T(8,128)(2,1)}, bf16[4,512,1024]{2,1,0:T(8,128)(2,1)}) custom-call(bf16[4,128,1024]{2,1,0:T(8,128)(2,1)} %get-tuple-element.17.comb_ref, bf16[4,512,256]{2,1,0:T(8,128)(2,1)} %fusion.3.refs_2_.pick_ref, bf16[512,1024]{1,0:T(8,128)(2,1)} %grid_ref.1, bf16[4,512,1024]{2,1,0:T(8,128)(2,1)} %get-tuple-element.18.summed_ref, ...), custom_call_target="tpu_custom_call" | custom-call | tf_op jit(solution)/shard_map/slopes/pallas_call | solution.py:266
  80.2 7.7 %all-gather.2.cloned.1.call-done.all_ref = f32[16,104,512]{2,1,0:T(8,128)} async-done(((f32[4,104,512]{2,1,0:T(8,128)}), f32[16,104,512]{2,1,0:T(8,128)}) %all-gather.2.cloned.1.call-update) | async-done | bytes 3407888 | tf_op jit(solution)/shard_map/all_gather | solution.py:264
  87.9 9.6 %loss.1 = (bf16[4,104,512]{2,1,0:T(8,128)(2,1)}, bf16[4,512,1024]{2,1,0:T(8,128)(2,1)}, f32[8,128]{1,0:T(8,128)}) custom-call(f32[4,104,512]{2,1,0:T(8,128)} %get-tuple-element.16.own_ref, f32[16,104,512]{2,1,0:T(8,128)} %all-gather.2.cloned.1.call-done.all_ref, f32[104,512]{1,0:T(8,128)} %pad.18.truth_ref, f32[1,512]{1,0:T(1,128)} %bitcast.77, ...), custom_call_target="tpu_custom_call" | custom-call | tf_op jit(solution)/shard_map/loss/pallas_call | solution.py:281
  97.4 0.0 copy-start.2
  97.5 1.4 reduce_sum.42
  98.8 3.0 convolution_bitcast_fusion.2
  101.8 0.0 copy-done.6
  101.8 0.7 slice_select_fusion
  102.6 1.1 copy.36
  103.6 0.0 reduce-scatter.10.cloned.1.call-update
  103.6 0.0 reduce-scatter.6.cloned.1.call-start
  103.7 0.9 fusion.12.place_ref
  104.6 0.0 copy-done.2
  104.6 1.2 copy.31
  105.8 20.9 %table.1 = (f32[4,96,1024]{2,1,0:T(8,128)}, bf16[1024,1024]{1,0:T(8,128)(2,1)}) custom-call(bf16[4,512,1024]{2,1,0:T(8,128)(2,1)} %get-tuple-element.20.pre_ref, bf16[1024,1024]{1,0:T(8,128)(2,1)} %node_ref.3, bf16[4,4,512,1024]{3,2,1,0:T(8,128)(2,1)} %get-tuple-element.21.slope_ref, bf16[128,2048]{1,0:T(8,128)(2,1)} %fusion.12.place_ref, ...), custom_call_target="tpu_custom_call" | custom-call | tf_op jit(solution)/shard_map/table/pallas_call | solution.py:310
  126.7 0.0 reduce-scatter.6.cloned.1.call-update
  126.7 0.3 reduce-scatter.8.cloned.1.call-start
  127.0 9.4 %bitcast_convert_fusion = bf16[1024,1024]{1,0:T(8,128)(2,1)} fusion(bf16[4,512,1024]{2,1,0:T(8,128)(2,1)} %get-tuple-element.18.summed_ref, bf16[4,512,1024]{2,1,0:T(8,128)(2,1)} %get-tuple-element.20.pre_ref), kind=kOutput, calls=%fused_computation.2 | convolution fusion | flops 4296015872 | bytes 10485760 | tf_op jit(solution)/shard_map/mgh,mgk->hk/dot_general | solution.py:300
  136.4 0.0 reduce-scatter.8.cloned.1.call-update
  136.4 1.7 convert.4
  138.1 2.3 collective-permute-start.3
  140.4 0.0 copy-done.5
  140.4 0.1 iota_compare_fusion.6
  140.5 1.3 collective-permute-start.2
  141.8 1.5 collective-permute-done.3
  143.3 0.3 convolution_bitcast_fusion
  143.6 4.4 collective-permute-done.2
  148.0 0.0 copy-done
  148.1 3.1 fusion.7
  151.2 86.6 %reduce-scatter.10.cloned.1.call-done = f32[32,101]{1,0:T(8,128)} async-done(((f32[1024,101]{1,0:T(8,128)}), f32[32,101]{1,0:T(8,128)}) %reduce-scatter.10.cloned.1.call-update) | async-done | bytes 12944
  237.8 0.8 copy.37
  238.6 162.6 %reduce-scatter.6.cloned.1.call-done = bf16[32,1024]{1,0:T(8,128)(2,1)} async-done(((bf16[1024,1024]{1,0:T(8,128)(2,1)}), bf16[32,1024]{1,0:T(8,128)(2,1)}) %reduce-scatter.6.cloned.1.call-update) | async-done | bytes 65552 | tf_op jit(solution)/shard_map/reduce_scatter | solution.py:333
  401.2 161.6 %reduce-scatter.8.cloned.1.call-done = bf16[32,1024]{1,0:T(8,128)(2,1)} async-done(((bf16[1024,1024]{1,0:T(8,128)(2,1)}), bf16[32,1024]{1,0:T(8,128)(2,1)}) %reduce-scatter.8.cloned.1.call-update) | async-done | bytes 65552 | tf_op jit(solution)/shard_map/reduce_scatter | solution.py:333
  562.8 41.2 %all-reduce.6 = (f32[32,1024]{1,0:T(8,128)S(1)}, f32[32,1024]{1,0:T(8,128)S(1)}, f32[32,101]{0,1:T(8,128)S(1)}) all-reduce(bf16[32,1024]{1,0:T(8,128)(2,1)} %reduce-scatter.6.cloned.1.call-done, bf16[32,1024]{1,0:T(8,128)(2,1)} %reduce-scatter.8.cloned.1.call-done, ...), channel_id=1, replica_groups=mesh['member'=4,'space'=32] {'member'}, use_global_device_ids=true, to_apply=%region_4.5 | all-reduce | flops 68768 | bytes 419072 | tf_op jit(solution)/shard_map/psum | solution.py:334
  604.0 0.5 slice.51
  604.5 0.7 copy.33
  605.2 0.7 broadcast_multiply_fusion
  (16 shorter events, 0.2 us)
Async XLA Ops:
  7.2 16.4 %copy-start.3 = (f32[100,512]{1,0:T(8,128)S(1)}, f32[100,512]{1,0:T(8,128)}, u32[]{:S(2)}) copy-start(f32[100,512]{1,0:T(8,128)} %param.18) | copy-start | bytes 614404
  7.2 80.7 %all-gather.2.cloned.1.call-start = ((), (), s32[]{:S(2)}) async-start(), calls=%async_computation.3 | async-start | bytes 4259840 | tf_op jit(solution)/shard_map/all_gather | solution.py:264
  8.6 15.7 %collective-permute-start = (bf16[4,16,1024]{2,1,0:T(8,128)(2,1)S(1)}, bf16[4,16,1024]{2,1,0:T(8,128)(2,1)S(1)}, u32[]{:S(2)}, u32[]{:S(2)}) collective-permute-start(bf16[4,16,1024]{2,1,0:T(8,128)(2,1)S(1)} %get-tuple-element.55), channel_id=1, source_target_pairs={{0,1},{1,2},{2,3},{3,4},{4,5},{5,6},{6,7},{7,8},{8,9},{9,10},{10,1... | collective-permute-start | bytes 393224 | tf_op jit(solution)/shard_map/ppermute | solution.py:208
  13.0 11.3 %collective-permute-start.1 = (bf16[4,16,1024]{2,1,0:T(8,128)(2,1)S(1)}, bf16[4,16,1024]{2,1,0:T(8,128)(2,1)S(1)}, u32[]{:S(2)}, u32[]{:S(2)}) collective-permute-start(bf16[4,16,1024]{2,1,0:T(8,128)(2,1)S(1)} %get-tuple-element.54), channel_id=1, source_target_pairs={{1,0},{2,1},{3,2},{4,3},{5,4},{6,5},{7,6},{8,7},{9,8},{10,9},{11,1... | collective-permute-start | bytes 393224 | tf_op jit(solution)/shard_map/ppermute | solution.py:209
  24.4 0.9 copy-start.1
  25.2 24.0 %copy-start.4 = (f32[100,512]{1,0:T(8,128)S(1)}, f32[100,512]{1,0:T(8,128)}, u32[]{:S(2)}) copy-start(f32[100,512]{1,0:T(8,128)} %param.19) | copy-start | bytes 614404
  25.2 24.7 %copy-start.7 = (f32[100]{0:T(128)S(1)}, f32[100]{0:T(128)}, u32[]{:S(2)}) copy-start(f32[100]{0:T(128)} %param.21) | copy-start | bytes 1204
  49.0 188.8 %reduce-scatter.10.cloned.1.call-start = ((), (), s32[]{:S(2)}) async-start(), calls=%async_computation.6 | async-start | bytes 540672
  97.4 4.3 copy-start.6
  97.4 7.2 %copy-start.2 = (bf16[4,96,1024]{2,1,0:T(8,128)(2,1)S(1)}, bf16[4,96,1024]{2,1,0:T(8,128)(2,1)}, u32[]{:S(2)}) copy-start(bf16[4,96,1024]{2,1,0:T(8,128)(2,1)} %copy-done.1) | copy-start | bytes 2359300
  103.6 297.5 %reduce-scatter.6.cloned.1.call-start = ((), (), s32[]{:S(2)}) async-start(), calls=%async_computation.4 | async-start | bytes 2162688 | tf_op jit(solution)/shard_map/reduce_scatter | solution.py:333
  126.7 436.1 %reduce-scatter.8.cloned.1.call-start = ((), (), s32[]{:S(2)}) async-start(), calls=%async_computation.5 | async-start | bytes 2162688 | tf_op jit(solution)/shard_map/reduce_scatter | solution.py:333
  136.4 4.0 copy-start.5
  136.4 11.7 %copy-start = (bf16[1024,1024]{1,0:T(8,128)(2,1)S(1)}, bf16[1024,1024]{1,0:T(8,128)(2,1)}, u32[]{:S(2)}) copy-start(bf16[1024,1024]{1,0:T(8,128)(2,1)} %refs_1_.1) | copy-start | bytes 6291460
  138.1 5.1 collective-permute-start.3
  140.5 7.5 %collective-permute-start.2 = (bf16[4,16,1024]{2,1,0:T(8,128)(2,1)S(1)}, bf16[4,16,1024]{2,1,0:T(8,128)(2,1)S(1)}, u32[]{:S(2)}, u32[]{:S(2)}) collective-permute-start(bf16[4,16,1024]{2,1,0:T(8,128)(2,1)S(1)} %get-tuple-element.52), channel_id=1, source_target_pairs={{1,0},{2,1},{3,2},{4,3},{5,4},{6,5},{7,6},{8,7},{9,8},{10,9},{11,1... | collective-permute-start | bytes 393224 | tf_op jit(solution)/shard_map/ppermute | solution.py:340
Sparse Core Ops, SparseCore 0:
  49.1 38.7 all-gather.1
  103.8 133.9 reduce-scatter.9
  240.3 160.8 reduce-scatter.5
  403.4 159.3 reduce-scatter.7

commit v2 on v1

v2 whole, which is shorter than its diff:
```python
import functools

import jax
import jax.numpy as jnp
from jax import lax
from jax.experimental import pallas as pl
from jax.experimental.pallas import tpu as pltpu
from jax.sharding import PartitionSpec as P

SQRT_TWO_PI = 0.7978845608028654
CUBIC = 0.044715
ALPHA = 0.95
SOFT_EDGE = 0.05
DEGREE = 4
TABLE = 128
EMPTY = -64.0
CHUNK = 128
TILE = 256
PART = 32
LANES = 128
VMEM_LIMIT = 56 * 1024 * 1024


def tanh_of(u):
    s = u * u
    return s, jnp.tanh(u * (SQRT_TWO_PI + (SQRT_TWO_PI * CUBIC) * s))


def gelu_twice(u):
    _, t = tanh_of(u)
    return u + u * t


def slope_twice(u):
    s, t = tanh_of(u)
    q = u * (SQRT_TWO_PI + (3.0 * SQRT_TWO_PI * CUBIC) * s)
    return (1.0 + t) * (1.0 + (1.0 - t) * q)


def dot(left, right):
    return lax.dot_general(
        left, right, (((1,), (0,)), ((), ())), preferred_element_type=jnp.float32
    )


def dot_nt(left, right):
    return lax.dot_general(
        left, right, (((1,), (1,)), ((), ())), preferred_element_type=jnp.float32
    )


def parts(rows):
    return [(r, c) for r in range(0, rows, PART) for c in range(0, TILE, LANES)]


def staged(tiles, work_ref, matmul, finish):
    for i, tile in enumerate(tiles):
        result = matmul(*tile)
        work_ref[i % 2, : result.shape[0]] = result
        if i:
            finish(work_ref.at[(i - 1) % 2], *tiles[i - 1])
    finish(work_ref.at[(len(tiles) - 1) % 2], *tiles[-1])


def edge_stage(pick_ref, comb_ref, work_ref, finish):
    members, _, width = comb_ref.shape
    tiles = [(m, h) for m in range(members) for h in range(0, width, TILE)]
    staged(
        tiles, work_ref, lambda m, h: dot(pick_ref[0], comb_ref[m, :, h : h + TILE]), finish
    )


def node_stage(summed_ref, node_ref, work_ref, finish):
    members, rows, width = summed_ref.shape

    def matmul(h):
        return dot(summed_ref[...].reshape(members * rows, width), node_ref[:, h : h + TILE])

    def finish_all(buffer, h):
        for m in range(members):
            finish(buffer.at[m * rows : (m + 1) * rows], m, h)

    staged([(h,) for h in range(0, width, TILE)], work_ref, matmul, finish_all)


def forward_kernel(
    rows_ref, project_ref, pick_ref, grid_ref, node_ref, output_ref, prior_ref,
    pred_ref, summed_ref, out_ref, comb_ref, work_ref,
):
    members, table_rows, width = rows_ref.shape

    @pl.when(pl.program_id(0) == 0)
    def _():
        for m in range(members):
            comb_ref[m, :table_rows] = dot(rows_ref[m], project_ref[...]).astype(jnp.bfloat16)
            comb_ref[m, table_rows:TABLE] = jnp.full(
                (TABLE - table_rows, width), EMPTY, jnp.bfloat16
            )

    for m in range(members):
        comb_ref[m, TABLE:] = grid_ref[...]

    def sum_edges(buffer, m, h):
        for r, c in parts(CHUNK):
            twice = sum(
                gelu_twice(buffer[k * CHUNK + r : k * CHUNK + r + PART, c : c + LANES])
                for k in range(DEGREE)
            )
            summed_ref[m, r : r + PART, h + c : h + c + LANES] = (0.5 * twice).astype(jnp.bfloat16)

    def node_values(buffer, m, h):
        for r, c in parts(CHUNK):
            value = 0.5 * gelu_twice(buffer[r : r + PART, c : c + LANES])
            out_ref[m, r : r + PART, h + c : h + c + LANES] = value.astype(jnp.bfloat16)

    edge_stage(pick_ref, comb_ref, work_ref, sum_edges)
    node_stage(summed_ref, node_ref, work_ref, node_values)
    for m in range(members):
        pred_ref[m] = jnp.zeros(pred_ref.shape[1:], jnp.float32)
        pred_ref[m, : prior_ref.shape[0]] = prior_ref[...] + dot_nt(output_ref[...], out_ref[m])


def slope_kernel(
    comb_ref, pick_ref, grid_ref, summed_ref, node_ref, edge_ref, point_ref, both_ref, work_ref,
):
    members = comb_ref.shape[0]
    for m in range(members):
        both_ref[m, :TABLE] = comb_ref[m]
        both_ref[m, TABLE:] = grid_ref[...]

    def edge_slopes(buffer, m, h):
        for k in range(DEGREE):
            for r, c in parts(CHUNK):
                value = 0.5 * slope_twice(
                    buffer[k * CHUNK + r : k * CHUNK + r + PART, c : c + LANES]
                )
                edge_ref[m, k, r : r + PART, h + c : h + c + LANES] = value.astype(jnp.bfloat16)

    def node_slopes(buffer, m, h):
        for r, c in parts(CHUNK):
            value = 0.5 * slope_twice(buffer[r : r + PART, c : c + LANES])
            point_ref[m, r : r + PART, h + c : h + c + LANES] = value.astype(jnp.bfloat16)

    edge_stage(pick_ref, both_ref, work_ref, edge_slopes)
    node_stage(summed_ref, node_ref, work_ref, node_slopes)


def loss_kernel(
    core_index_ref, own_ref, core_ref, chip_ref, far_ref, truth_ref, area_ref, variable_ref, slope_ref, output_ref,
    grad_ref, pre_ref, loss_ref, tall_ref, sum_ref,
):
    members = own_ref.shape[0]
    variables = truth_ref.shape[0]
    width = output_ref.shape[1]
    everyone = 4 * members
    fairness = 1.0 - (1.0 - ALPHA) / everyone
    weight = variable_ref[...] * area_ref[...]
    truth = truth_ref[...]
    edge = SOFT_EDGE * SOFT_EDGE
    terms = jnp.zeros((variables, CHUNK), jnp.float32)

    @pl.when(pl.program_id(0) == 0)
    def _():
        sum_ref[...] = jnp.zeros_like(sum_ref)
        tall_ref[...] = jnp.zeros_like(tall_ref)

    grads = []
    for j in range(members):
        own = own_ref[j, :variables]
        pair_abs = jnp.full((variables, CHUNK), -everyone * SOFT_EDGE, jnp.float32)
        pair_sign = jnp.zeros((variables, CHUNK), jnp.float32)
        for other in [ref[k, :variables] for ref in (own_ref, core_ref, chip_ref, far_ref) for k in range(members)]:
            d = own - other
            square = d * d + edge
            r = lax.rsqrt(square)
            pair_abs = pair_abs + square * r
            pair_sign = pair_sign + d * r
        d = own - truth
        square = d * d + edge
        r = lax.rsqrt(square)
        terms = terms + weight * (
            (square * r - SOFT_EDGE) / everyone
            - fairness / (2.0 * everyone * (everyone - 1)) * pair_abs
        )
        gradient = weight * (d * r - fairness / (everyone - 1) * pair_sign)
        grad_ref[j] = gradient.astype(jnp.bfloat16)
        tall_ref[:variables] = gradient
        grads.append(tall_ref[...].T.astype(jnp.bfloat16))

    sum_ref[...] += jnp.sum(terms, axis=0, keepdims=True)

    @pl.when(pl.program_id(0) == pl.num_programs(0) - 1)
    def _():
        rest = jnp.sum(sum_ref[...], axis=1, keepdims=True)
        lane = lax.broadcasted_iota(jnp.int32, (1, CHUNK), 1)
        row = jnp.zeros((1, CHUNK), jnp.float32)
        for part in range(3):
            piece = rest.astype(jnp.bfloat16).astype(jnp.float32)
            row = jnp.where(lane == variables + 3 * core_index_ref[0] + part, piece, row)
            rest = rest - piece
        loss_ref[...] = row

    stacked = jnp.concatenate(grads, axis=0)
    for h in range(0, width, TILE):
        node_grad = dot(stacked, output_ref[:, h : h + TILE]).reshape(members, CHUNK, TILE)
        slope = slope_ref[:, :, h : h + TILE].astype(jnp.float32)
        pre_ref[:, :, h : h + TILE] = (node_grad * slope).astype(jnp.bfloat16)


def table_kernel(pre_ref, node_ref, slope_ref, place_ref, rows_ref, grad_ref, term_ref):
    members, points, _ = pre_ref.shape
    table_rows = grad_ref.shape[1]
    cast = []
    for m in range(members):
        summed_grad = dot_nt(pre_ref[m], node_ref[...]).astype(jnp.bfloat16)
        table = sum(
            dot(place_ref[:, k * points : (k + 1) * points], summed_grad * slope_ref[m, k])
            for k in range(DEGREE)
        )[:table_rows]
        grad_ref[m] = table
        cast.append(table.astype(jnp.bfloat16))
    term_ref[...] = dot(rows_ref[...], jnp.concatenate(cast, axis=0)).astype(jnp.bfloat16)


def params():
    return pltpu.CompilerParams(
        dimension_semantics=("arbitrary",), vmem_limit_bytes=VMEM_LIMIT
    )


def whole(array):
    return pl.BlockSpec(array.shape, lambda c: (0,) * array.ndim)


def shards(
    hidden,
    grid_state,
    project_weight,
    node_weight,
    output_weight,
    prior_state,
    target,
    area_weight,
    variable_weight,
    edge_source,
    edge_target,
    edge_count,
    send_index,
):
    members, own_nodes, width = hidden.shape
    points = grid_state.shape[0]
    send_rows = send_index.shape[1]
    variables = output_weight.shape[1]
    slots = edge_source.shape[0]
    core = lax.axis_index("member") % 2
    space = lax.axis_size("space")
    total_points = points * space
    table_rows = own_nodes + 2 * send_rows
    chunks = points // CHUNK

    nodes = jnp.arange(own_nodes, dtype=jnp.int32)
    chosen = (send_index[:, :, None] == nodes).astype(jnp.bfloat16)
    packed = jnp.einsum(
        "dsn,mnh->dmsh", chosen, hidden, preferred_element_type=jnp.float32
    ).astype(jnp.bfloat16)
    forward = [(i, i + 1) for i in range(space - 1)]
    backward = [(i + 1, i) for i in range(space - 1)]
    from_left = lax.ppermute(packed[1], "space", forward)
    from_right = lax.ppermute(packed[0], "space", backward)

    edges = jnp.arange(slots, dtype=jnp.int32)
    live = edges < edge_count[0]
    owner = jnp.where(live, edge_target, points)
    ahead = jnp.pad(owner, (DEGREE - 1, 0), constant_values=-1)
    rank = sum(
        (lax.slice_in_dim(ahead, k, k + slots) == owner).astype(jnp.int32)
        for k in range(DEGREE - 1)
    )
    ranked = jnp.where(
        rank[None, :] == jnp.arange(DEGREE, dtype=jnp.int32)[:, None], edge_source[None, :] + 1, 0
    ).astype(jnp.bfloat16)
    owned = (owner[:, None] == jnp.arange(points, dtype=jnp.int32)).astype(jnp.bfloat16)
    found = jnp.einsum("ke,eg->kg", ranked, owned, preferred_element_type=jnp.float32)
    found = found.astype(jnp.int32)
    slot = jnp.where(found > 0, found - 1, table_rows)
    columns = jnp.arange(TABLE + CHUNK, dtype=jnp.int32)
    within = jnp.arange(CHUNK, dtype=jnp.int32)
    by_chunk = slot.reshape(DEGREE, chunks, CHUNK).transpose(1, 0, 2)
    pick = (
        (by_chunk[..., None] == columns) | ((within[:, None] + TABLE) == columns)
    ).astype(jnp.bfloat16).reshape(chunks, DEGREE * CHUNK, TABLE + CHUNK)
    place = (
        slot.reshape(1, DEGREE * points) == jnp.arange(TABLE, dtype=jnp.int32)[:, None]
    ).astype(jnp.bfloat16)
    output_rows = output_weight.T
    output_padded = jnp.pad(output_rows, ((0, TABLE - variables), (0, 0)))
    scale = variable_weight[:, None]

    source_rows = jnp.concatenate([hidden, from_left, from_right], axis=1)

    chunk_rows = pl.BlockSpec((CHUNK, width), lambda c: (c, 0))
    member_rows = pl.BlockSpec((members, CHUNK, width), lambda c: (0, c, 0))
    pick_block = pl.BlockSpec((1, DEGREE * CHUNK, TABLE + CHUNK), lambda c: (c, 0, 0))
    by_variable = pl.BlockSpec((variables, CHUNK), lambda c: (0, c))
    tiled_rows = -(-variables // 8) * 8
    own_block = pl.BlockSpec((members, tiled_rows, CHUNK), lambda c: (0, 0, c))
    per_point = jax.ShapeDtypeStruct((members, points, width), jnp.bfloat16)
    pred, summed, node_out, comb = pl.pallas_call(
        forward_kernel_with_table,
        grid=(chunks,),
        in_specs=[
            whole(source_rows), whole(project_weight), pick_block, chunk_rows,
            whole(node_weight), whole(output_rows), by_variable,
        ],
        out_specs=[
            own_block, member_rows, member_rows,
            pl.BlockSpec((members, TABLE, width), lambda c: (0, 0, 0)),
        ],
        out_shape=[
            jax.ShapeDtypeStruct((members, tiled_rows, points), jnp.float32), per_point, per_point,
            jax.ShapeDtypeStruct((members, TABLE, width), jnp.bfloat16),
        ],
        scratch_shapes=[
            pltpu.VMEM((members, TABLE + CHUNK, width), jnp.bfloat16),
            pltpu.VMEM((2, DEGREE * CHUNK, TILE), jnp.float32),
        ],
        compiler_params=params(),
        name="forward",
    )(source_rows, project_weight, pick, grid_state, node_weight, output_rows, prior_state)

    def swap(value, flip):
        return lax.ppermute(value, "member", [(i, i ^ flip) for i in range(lax.axis_size("member"))])

    chip_pred = swap(pred, 2)
    core_pred = swap(pred, 1)
    far_pred = swap(chip_pred, 1)

    edge_slope, node_slope = pl.pallas_call(
        slope_kernel,
        grid=(chunks,),
        in_specs=[whole(comb), pick_block, chunk_rows, member_rows, whole(node_weight)],
        out_specs=[
            pl.BlockSpec((members, DEGREE, CHUNK, width), lambda c: (0, 0, c, 0)), member_rows,
        ],
        out_shape=[
            jax.ShapeDtypeStruct((members, DEGREE, points, width), jnp.bfloat16), per_point,
        ],
        scratch_shapes=[
            pltpu.VMEM((members, TABLE + CHUNK, width), jnp.bfloat16),
            pltpu.VMEM((2, DEGREE * CHUNK, TILE), jnp.float32),
        ],
        compiler_params=params(),
        name="slopes",
    )(comb, pick, grid_state, summed, node_weight)

    grad_pred, node_pre_grad, loss_row = pl.pallas_call(
        loss_kernel,
        grid=(chunks,),
        in_specs=[
            pl.BlockSpec(memory_space=pltpu.SMEM),
            own_block, own_block, own_block, own_block, by_variable,
            pl.BlockSpec((1, CHUNK), lambda c: (0, c)),
            whole(scale), member_rows, whole(output_padded),
        ],
        out_specs=[
            pl.BlockSpec((members, variables, CHUNK), lambda c: (0, 0, c)), member_rows,
            pl.BlockSpec((1, CHUNK), lambda c: (0, 0)),
        ],
        out_shape=[
            jax.ShapeDtypeStruct((members, variables, points), jnp.bfloat16), per_point,
            jax.ShapeDtypeStruct((1, CHUNK), jnp.float32),
        ],
        scratch_shapes=[
            pltpu.VMEM((TABLE, CHUNK), jnp.float32), pltpu.VMEM((1, CHUNK), jnp.float32),
        ],
        compiler_params=params(),
        name="loss",
    )(core[None], pred, core_pred, chip_pred, far_pred, target, area_weight[None, :], scale, node_slope, output_padded)

    def own_half(term):
        blocks = term.reshape(space, 2, width // space // 2, term.shape[1])
        mine = lax.dynamic_index_in_dim(blocks, core, 1, keepdims=False)
        other = swap(lax.dynamic_index_in_dim(blocks, 1 - core, 1, keepdims=False), 1)
        return (mine.astype(jnp.float32) + other.astype(jnp.float32)).astype(jnp.bfloat16)

    def reduce_rows(half):
        parts = lax.all_to_all(half, "space", 0, 0, tiled=True)
        part = jnp.sum(parts.astype(jnp.float32), axis=0)
        mine = part + swap(part, 2)
        other = swap(part, 1) + swap(part, 3)
        return jnp.where(
            core == 0,
            jnp.concatenate([mine, other], axis=0),
            jnp.concatenate([other, mine], axis=0),
        )

    node_term = jnp.einsum(
        "mgh,mgk->hk", summed, node_pre_grad, preferred_element_type=jnp.float32
    ).astype(jnp.bfloat16)
    output_term = jnp.einsum(
        "mgh,mvg->hv", node_out, grad_pred, preferred_element_type=jnp.float32
    )
    output_term = (
        jnp.pad(output_term, ((0, 0), (0, TABLE - variables))) + loss_row
    ).astype(jnp.bfloat16)
    node_half = own_half(jnp.concatenate([node_term, output_term], axis=1))

    source_columns = source_rows.reshape(members * table_rows, width).T
    table_grad, project_term = pl.pallas_call(
        table_kernel,
        grid=(width // TILE,),
        in_specs=[
            whole(node_pre_grad),
            pl.BlockSpec((TILE, width), lambda c: (c, 0)),
            pl.BlockSpec((members, DEGREE, points, TILE), lambda c: (0, 0, 0, c)),
            whole(place),
            whole(source_columns),
        ],
        out_specs=[
            pl.BlockSpec((members, table_rows, TILE), lambda c: (0, 0, c)),
            pl.BlockSpec((width, TILE), lambda c: (0, c)),
        ],
        out_shape=[
            jax.ShapeDtypeStruct((members, table_rows, width), jnp.float32),
            jax.ShapeDtypeStruct((width, width), jnp.bfloat16),
        ],
        compiler_params=params(),
        name="table",
    )(node_pre_grad, node_weight, edge_slope, place, source_columns)

    sums = reduce_rows(jnp.concatenate([own_half(project_term), node_half], axis=2))

    left_back = lax.ppermute(
        table_grad[:, own_nodes : own_nodes + send_rows].astype(jnp.bfloat16), "space", backward
    )
    right_back = lax.ppermute(
        table_grad[:, own_nodes + send_rows :].astype(jnp.bfloat16), "space", forward
    )
    projected_grad = (
        table_grad[:, :own_nodes]
        + jnp.einsum(
            "sn,msh->mnh", chosen[1], left_back, preferred_element_type=jnp.float32
        )
        + jnp.einsum(
            "sn,msh->mnh", chosen[0], right_back, preferred_element_type=jnp.float32
        )
    ).astype(jnp.bfloat16)
    grad_hidden = jnp.einsum(
        "mnk,hk->mnh", projected_grad, project_weight, preferred_element_type=jnp.float32
    ).astype(jnp.bfloat16)
    output_at = 2 * width
    loss_at = output_at + variables
    return (
        grad_hidden,
        sums[:, :width] / total_points,
        sums[:, width:output_at] / total_points,
        sums[:, output_at:loss_at] / total_points,
        jnp.sum(sums[0, loss_at:]) / (total_points * variables),
    )


def forward_kernel_with_table(*refs):
    inputs, (pred_ref, summed_ref, out_ref, table_ref, comb_ref, work_ref) = refs[:7], refs[7:]
    forward_kernel(*inputs, pred_ref, summed_ref, out_ref, comb_ref, work_ref)

    @pl.when(pl.program_id(0) == 0)
    def _():
        table_ref[...] = comb_ref[:, :TABLE]


def solution(mesh):
    placed = (
        P("member", "space", None),
        P("space", None),
        P(),
        P(),
        P(),
        P(None, "space"),
        P(None, "space"),
        P("space"),
        P(),
        P("space"),
        P("space"),
        P("space"),
        P("space", None),
    )
    return jax.shard_map(
        shards,
        mesh=mesh,
        in_specs=placed,
        out_specs=(
            P("member", "space", None),
            P("space", None),
            P("space", None),
            P("space", None),
            P(),
        ),
        check_vma=False,
    )
```

time: 615 us -> 209 us (0.34)
  waiting for transfers between devices: 424 us -> 42.9 us
  blocking collectives: 41.2 us -> 0 us
  starting transfers between devices: 9.81 us -> 35.4 us
  between operations: 16.4 us -> 3.36 us
    reduce_scatter x2 -> x0, waiting for transfers between devices: 324 us -> none  [reduce_rows(): part = lax.psum_scatter(term, 'space', scatter_dimension=0, tiled=True)]
    unnamed x5 -> x0, waiting for transfers between devices: 86.7 us -> none
    psum x1 -> x0, blocking collectives: 41.2 us -> none  [reduce_rows(): return lax.psum(part.astype(jnp.float32), 'member')]
    ppermute x0 -> x8, waiting for transfers between devices: none -> 18.7 us  [swap(): lax.ppermute(value, 'member', [(i, i ^ flip) for i in range(lax.axis_size...]
    ppermute x0 -> x8, starting transfers between devices: none -> 15.7 us  [swap(): lax.ppermute(value, 'member', [(i, i ^ flip) for i in range(lax.axis_size...]
    all_to_all x0 -> x1, waiting for transfers between devices: none -> 14.8 us  [reduce_rows(): parts = lax.all_to_all(half, 'space', 0, 0, tiled=True)]
    all_to_all x0 -> x1, starting transfers between devices: none -> 9.56 us  [reduce_rows(): parts = lax.all_to_all(half, 'space', 0, 0, tiled=True)]
    ppermute x1, waiting for transfers between devices: 1.46 us -> 9.31 us  [shards(): lax.ppermute(table_grad[:, own_nodes + send_rows:].astype(jnp.bfloat16),...]
  transfers between devices with their start and end apart: 8 -> 13, of which waited for: 6 -> 5; matrix products, arithmetic and copies ran while one was open for 5% -> 11% of each run, Pallas kernels for 8% -> 15%
where the time goes in v2:
time: 209 us; the launch traced here: 208 us
  Pallas kernels  85.4 us (41%)
  waiting for transfers between devices  42.9 us (21%)
  starting transfers between devices  35.4 us (17%)
  other arithmetic  14.6 us (7%)
  matrix products  14.1 us (7%)
  local copies, waits for them, and re-layouts  12.2 us (6%)
  between operations  3.36 us (2%)
    pallas_call x1, Pallas kernels, shards(): pl.pallas_call(slope_kernel, grid=(chunks,), in_specs=[whole(comb), pick_...  30.3 us
    pallas_call x1, Pallas kernels, shards(): pl.pallas_call(forward_kernel_with_table, grid=(chunks,), in_specs=[whole...  24.1 us
    pallas_call x1, Pallas kernels, shards(): pl.pallas_call(table_kernel, grid=(width // TILE,), in_specs=[whole(node_...  20.9 us
    ppermute x8, waiting for transfers between devices, swap(): lax.ppermute(value, 'member', [(i, i ^ flip) for i in range(lax.axis_size...  18.7 us
    ppermute x8, starting transfers between devices, swap(): lax.ppermute(value, 'member', [(i, i ^ flip) for i in range(lax.axis_size...  15.7 us
    all_to_all x1, waiting for transfers between devices, reduce_rows(): parts = lax.all_to_all(half, 'space', 0, 0, tiled=True)  14.8 us
    pallas_call x1, Pallas kernels, shards(): pl.pallas_call(loss_kernel, grid=(chunks,), in_specs=[pl.BlockSpec(memory...  10.2 us
    all_to_all x1, starting transfers between devices, reduce_rows(): parts = lax.all_to_all(half, 'space', 0, 0, tiled=True)  9.56 us
  transfers between devices with their start and end apart: 13, of which 5 were waited for; matrix products, arithmetic and copies ran while one was open for 11% of the time, Pallas kernels for 15%

profile of v2, /device:TPU:1, one launch (start us, length us, event | category | flops | bytes accessed | tf_op | source)
XLA Modules:
  0.0 207.8 jit_solution(8921917589654345042)
XLA Ops:
  0.6 1.4 fusion.11
  2.1 4.4 %collective-permute-start = (bf16[4,16,1024]{2,1,0:T(8,128)(2,1)S(1)}, bf16[4,16,1024]{2,1,0:T(8,128)(2,1)S(1)}, u32[]{:S(2)}, u32[]{:S(2)}) collective-permute-start(bf16[4,16,1024]{2,1,0:T(8,128)(2,1)S(1)} %get-tuple-element.32), channel_id=1, source_target_pairs={{0,1},{1,2},{2,3},{3,4},{4,5},{5,6},{6,7},{7,8},{8,9},{9,10},{10,1... | collective-permute-start | bytes 393224 | tf_op jit(solution)/shard_map/ppermute | solution.py:268
  6.4 1.3 collective-permute-start.1
  8.4 0.7 fusion.22
  9.1 0.8 convert_add_fusion.2
  9.9 0.8 add_select_fusion
  10.7 0.1 iota_compare_fusion.6
  10.8 1.3 fusion.7.refs_2_.pick_ref
  12.2 0.0 collective-permute-done
  12.2 0.0 collective-permute-done.1
  12.3 0.9 copy-done
  13.1 24.1 %forward.1 = (f32[4,104,512]{2,1,0:T(8,128)}, bf16[4,512,1024]{2,1,0:T(8,128)(2,1)}, bf16[4,512,1024]{2,1,0:T(8,128)(2,1)}, bf16[4,128,1024]{2,1,0:T(8,128)(2,1)}) custom-call(bf16[4,96,1024]{2,1,0:T(8,128)(2,1)} %copy-done, bf16[1024,1024]{1,0:T(8,128)(2,1)} %refs_1_.1, bf16[4,512,256]{2,1,0:T(8,128)(2,1)} %fusion.7.refs_2_.pick_ref, ...), custom_call_target="tpu_custom_call" | custom-call | tf_op jit(solution)/shard_map/forward/pallas_call | solution.py:308
  37.2 3.4 %collective-permute-start.3 = (f32[4,104,512]{2,1,0:T(8,128)}, f32[4,104,512]{2,1,0:T(8,128)S(1)}, u32[]{:S(2)}, u32[]{:S(2)}) collective-permute-start(f32[4,104,512]{2,1,0:T(8,128)} %get-tuple-element.16.own_ref), channel_id=1, source_target_pairs={{0,64},{32,96},{64,0},{96,32},{1,65},{33,97},{65,1},{97,33},{2,66}... | collective-permute-start | bytes 2555912 | tf_op jit(solution)/shard_map/ppermute | solution.py:332
  40.6 2.3 %collective-permute-start.2 = (f32[4,104,512]{2,1,0:T(8,128)}, f32[4,104,512]{2,1,0:T(8,128)S(1)}, u32[]{:S(2)}, u32[]{:S(2)}) collective-permute-start(f32[4,104,512]{2,1,0:T(8,128)} %get-tuple-element.16.own_ref), channel_id=1, source_target_pairs={{0,32},{32,0},{64,96},{96,64},{1,33},{33,1},{65,97},{97,65},{2,34}... | collective-permute-start | bytes 2555912 | tf_op jit(solution)/shard_map/ppermute | solution.py:332
  42.9 15.1 %collective-permute-done.3.chip_ref = f32[4,104,512]{2,1,0:T(8,128)S(1)} collective-permute-done((f32[4,104,512]{2,1,0:T(8,128)}, f32[4,104,512]{2,1,0:T(8,128)S(1)}, u32[]{:S(2)}, u32[]{:S(2)}) %collective-permute-start.3) | collective-permute-done | bytes 852000 | tf_op jit(solution)/shard_map/ppermute | solution.py:332
  58.1 2.7 %collective-permute-start.4 = (f32[4,104,512]{2,1,0:T(8,128)S(1)}, f32[4,104,512]{2,1,0:T(8,128)S(1)}, u32[]{:S(2)}, u32[]{:S(2)}) collective-permute-start(f32[4,104,512]{2,1,0:T(8,128)S(1)} %collective-permute-done.3.chip_ref), channel_id=1, source_target_pairs={{0,32},{32,0},{64,96},{96,64},{1,33},{33,1},{65,97},{97,65},{2,34}... | collective-permute-start | bytes 2555912 | tf_op jit(solution)/shard_map/ppermute | solution.py:332
  60.7 0.7 pad.13.output_ref
  61.5 0.7 copy.22.variable_ref
  62.2 0.9 fusion.13.place_ref
  63.1 2.3 %copy.23 = bf16[384,1024]{0,1:T(8,128)(2,1)} copy(bf16[384,1024]{1,0:T(8,128)(2,1)} %bitcast.77) | data formatting | bytes 1572864 | tf_op jit(solution)/shard_map/reshape | solution.py:408
  65.4 30.3 %slopes.1 = (bf16[4,4,512,1024]{3,2,1,0:T(8,128)(2,1)}, bf16[4,512,1024]{2,1,0:T(8,128)(2,1)}) custom-call(bf16[4,128,1024]{2,1,0:T(8,128)(2,1)} %get-tuple-element.17.comb_ref, bf16[4,512,256]{2,1,0:T(8,128)(2,1)} %fusion.7.refs_2_.pick_ref, bf16[512,1024]{1,0:T(8,128)(2,1)} %grid_ref.1, bf16[4,512,1024]{2,1,0:T(8,128)(2,1)} %get-tuple-element.18.summed_ref, ...), custom_call_target="tpu_custom_call" | custom-call | tf_op jit(solution)/shard_map/slopes/pallas_call | solution.py:338
  95.7 0.0 collective-permute-done.2.core_ref
  95.7 0.0 collective-permute-done.4.far_ref
  95.7 0.0 copy-start.6
  95.7 0.9 copy-done.5
  96.6 0.3 copy-done.6
  96.9 10.2 %loss.1 = (bf16[4,100,512]{2,1,0:T(8,128)(2,1)}, bf16[4,512,1024]{2,1,0:T(8,128)(2,1)}, f32[1,128]{1,0:T(1,128)}) custom-call(s32[1]{0:T(128)} %bitcast.core_index_ref, f32[4,104,512]{2,1,0:T(8,128)} %get-tuple-element.16.own_ref, f32[4,104,512]{2,1,0:T(8,128)} %copy-done.5, f32[4,104,512]{2,1,0:T(8,128)} %copy-done.4, f32[4,104,512]{2,1,0:T(8,128)} %copy-done.6, ...), custom_call_target="tpu_custom_call" | custom-call | tf_op jit(solution)/shard_map/loss/pallas_call | solution.py:356
  107.1 7.0 %bitcast_convert_fusion = bf16[1024,1024]{0,1:T(8,128)(2,1)S(1)} fusion(bf16[4,512,1024]{2,1,0:T(8,128)(2,1)S(1)} %copy-done.2, bf16[4,512,1024]{2,1,0:T(8,128)(2,1)} %get-tuple-element.20.pre_ref), kind=kOutput, calls=%fused_computation.1 | convolution fusion | flops 4296015872 | bytes 10485760 | tf_op jit(solution)/shard_map/mgh,mgk->hk/dot_general | solution.py:397
  114.1 20.9 %table.1 = (f32[4,96,1024]{2,1,0:T(8,128)}, bf16[1024,1024]{1,0:T(8,128)(2,1)}) custom-call(bf16[4,512,1024]{2,1,0:T(8,128)(2,1)} %get-tuple-element.20.pre_ref, bf16[1024,1024]{1,0:T(8,128)(2,1)} %node_ref.3, bf16[4,4,512,1024]{3,2,1,0:T(8,128)(2,1)} %get-tuple-element.21.slope_ref, bf16[128,2048]{1,0:T(8,128)(2,1)} %fusion.13.place_ref, ...), custom_call_target="tpu_custom_call" | custom-call | tf_op jit(solution)/shard_map/table/pallas_call | solution.py:409
  135.0 2.4 %dynamic-slice_bitcast_fusion.1 = bf16[32,16,1024]{2,1,0:T(8,128)(2,1)} fusion(bf16[32,2,16,1024]{3,2,1,0:T(8,128)(2,1)} %bitcast.79, s32[]{:T(128)S(6)} %select_n.43), kind=kLoop, calls=%fused_computation.24 | loop fusion | bytes 2097156 | tf_op jit(solution)/shard_map/jit(dynamic_index_in_dim)/squeeze | solution.py:383
  137.4 0.1 collective-permute-start.7
  137.5 0.7 convolution_bitcast_fusion.2
  138.2 0.1 add_convert_fusion.2
  138.3 1.6 pad_maximum_fusion
  140.0 3.0 %copy.26 = bf16[1024,1152]{1,0:T(8,128)(2,1)S(1)} copy(bf16[1024,1152]{0,1:T(8,128)(2,1)} %pad_maximum_fusion) | data formatting | bytes 4718592 | tf_op jit(solution)/shard_map/concatenate | solution.py:406
  143.0 0.1 dynamic-slice_bitcast_fusion
  143.1 0.5 collective-permute-start.8
  143.6 0.0 collective-permute-done.7
  143.6 2.0 fusion.2
  145.6 0.6 collective-permute-done.8
  146.2 1.6 fusion.1
  147.8 1.6 pad_maximum_fusion.1
  149.3 9.6 %all-to-all-start = ((bf16[32,16,2176]{2,1,0:T(8,128)(2,1)}), bf16[32,16,2176]{2,1,0:T(8,128)(2,1)S(1)}, u32[]{:S(2)}, u32[]{:S(2)}) async-start(bf16[32,16,2176]{2,1,0:T(8,128)(2,1)} %pad_maximum_fusion.1), calls=%async_computation | async-start | bytes 4456448 | tf_op jit(solution)/shard_map/all_to_all | solution.py:387
  158.9 0.0 copy-start.9
  158.9 1.5 convert.6
  160.4 0.7 fusion.24
  161.1 3.1 %collective-permute-start.6 = (bf16[4,16,1024]{2,1,0:T(8,128)(2,1)S(1)}, bf16[4,16,1024]{2,1,0:T(8,128)(2,1)S(1)}, u32[]{:S(2)}, u32[]{:S(2)}) collective-permute-start(bf16[4,16,1024]{2,1,0:T(8,128)(2,1)S(1)} %get-tuple-element.28), channel_id=1, source_target_pairs={{0,1},{1,2},{2,3},{3,4},{4,5},{5,6},{6,7},{7,8},{8,9},{9,10},{10,1... | collective-permute-start | bytes 393224 | tf_op jit(solution)/shard_map/ppermute | solution.py:436
  164.3 0.1 iota_compare_fusion.8
  164.3 1.3 collective-permute-start.5
  165.6 9.3 %collective-permute-done.6 = bf16[4,16,1024]{2,1,0:T(8,128)(2,1)S(1)} collective-permute-done((bf16[4,16,1024]{2,1,0:T(8,128)(2,1)S(1)}, bf16[4,16,1024]{2,1,0:T(8,128)(2,1)S(1)}, u32[]{:S(2)}, u32[]{:S(2)}) %collective-permute-start.6) | collective-permute-done | bytes 131104 | tf_op jit(solution)/shard_map/ppermute | solution.py:436
  174.9 0.3 convolution_bitcast_fusion
  175.3 14.8 %all-to-all-done = bf16[32,16,2176]{2,1,0:T(8,128)(2,1)S(1)} async-done(((bf16[32,16,2176]{2,1,0:T(8,128)(2,1)}), bf16[32,16,2176]{2,1,0:T(8,128)(2,1)S(1)}, u32[]{:S(2)}, u32[]{:S(2)}) %all-to-all-start) | async-done | bytes 2228256 | tf_op jit(solution)/shard_map/all_to_all | solution.py:387
  190.1 0.3 convert_reduce_fusion
  190.4 3.7 %collective-permute-start.9 = (f32[16,2176]{1,0:T(8,128)S(1)}, f32[16,2176]{1,0:T(8,128)S(1)}, u32[]{:S(2)}, u32[]{:S(2)}) collective-permute-start(f32[16,2176]{1,0:T(8,128)S(1)} %convert_reduce_fusion), channel_id=1, source_target_pairs={{0,64},{32,96},{64,0},{96,32},{1,65},{33,97},{65,1},{97,33},{2,66}... | collective-permute-start | bytes 417800 | tf_op jit(solution)/shard_map/ppermute | solution.py:332
  194.1 3.1 %collective-permute-start.10 = (f32[16,2176]{1,0:T(8,128)S(1)}, f32[16,2176]{1,0:T(8,128)S(1)}, u32[]{:S(2)}, u32[]{:S(2)}) collective-permute-start(f32[16,2176]{1,0:T(8,128)S(1)} %convert_reduce_fusion), channel_id=1, source_target_pairs={{0,32},{32,0},{64,96},{96,64},{1,33},{33,1},{65,97},{97,65},{2,34}... | collective-permute-start | bytes 417800 | tf_op jit(solution)/shard_map/ppermute | solution.py:332
  197.2 0.0 collective-permute-start.11
  197.2 0.0 collective-permute-done.5
  197.2 3.8 %fusion.8 = bf16[4,64,1024]{2,1,0:T(8,128)(2,1)} fusion(bf16[1024,1024]{1,0:T(8,128)(2,1)} %refs_1_.1, f32[4,64,1024]{2,1,0:T(8,128)S(1)} %convolution_bitcast_fusion, f32[4,96,1024]{2,1,0:T(8,128)} %get-tuple-element.22, bf16[4,16,1024]{2,1,0:T(8,128)(2,1)S(1)} %collective-permute-done.5, pred[2,16,64]{2,1,0:T(8,128)(4,1)S(1)} %iota_compare_fusion.8), kind=kOutput, calls=%fused_computation.18 | convolution fusion | flops 546308096 | bytes 4851712 | tf_op jit(solution)/shard_map/mnk,hk->mnh/dot_general | solution.py:448
  201.0 0.0 collective-permute-done.9
  201.0 0.0 collective-permute-done.10
  201.0 2.9 %collective-permute-done.11 = f32[16,2176]{1,0:T(8,128)S(1)} collective-permute-done((f32[16,2176]{1,0:T(8,128)S(1)}, f32[16,2176]{1,0:T(8,128)S(1)}, u32[]{:S(2)}, u32[]{:S(2)}) %collective-permute-start.11) | collective-permute-done | bytes 139296 | tf_op jit(solution)/shard_map/ppermute | solution.py:332
  204.0 0.7 slice_multiply_fusion
  204.7 0.6 slice_multiply_fusion.2
  205.3 0.7 slice_reduce_fusion
  (30 shorter events, 0.2 us)
Async XLA Ops:
  0.6 11.5 %copy-start.3 = (bf16[4,64,1024]{2,1,0:T(8,128)(2,1)S(1)}, bf16[4,64,1024]{2,1,0:T(8,128)(2,1)}, u32[]{:S(2)}) copy-start(bf16[4,64,1024]{2,1,0:T(8,128)(2,1)} %param.13) | copy-start | bytes 1572868
  2.1 10.1 %collective-permute-start = (bf16[4,16,1024]{2,1,0:T(8,128)(2,1)S(1)}, bf16[4,16,1024]{2,1,0:T(8,128)(2,1)S(1)}, u32[]{:S(2)}, u32[]{:S(2)}) collective-permute-start(bf16[4,16,1024]{2,1,0:T(8,128)(2,1)S(1)} %get-tuple-element.32), channel_id=1, source_target_pairs={{0,1},{1,2},{2,3},{3,4},{4,5},{5,6},{6,7},{7,8},{8,9},{9,10},{10,1... | collective-permute-start | bytes 393224 | tf_op jit(solution)/shard_map/ppermute | solution.py:268
  6.4 5.8 %collective-permute-start.1 = (bf16[4,16,1024]{2,1,0:T(8,128)(2,1)S(1)}, bf16[4,16,1024]{2,1,0:T(8,128)(2,1)S(1)}, u32[]{:S(2)}, u32[]{:S(2)}) collective-permute-start(bf16[4,16,1024]{2,1,0:T(8,128)(2,1)S(1)} %get-tuple-element.31), channel_id=1, source_target_pairs={{1,0},{2,1},{3,2},{4,3},{5,4},{6,5},{7,6},{8,7},{9,8},{10,9},{11,1... | collective-permute-start | bytes 393224 | tf_op jit(solution)/shard_map/ppermute | solution.py:269
  12.3 0.9 copy-start
  13.1 47.6 %copy-start.7 = (bf16[1024,100]{0,1:T(8,128)(2,1)S(1)}, bf16[1024,100]{0,1:T(8,128)(2,1)}, u32[]{:S(2)}) copy-start(bf16[1024,100]{0,1:T(8,128)(2,1)} %param.17) | copy-start | bytes 614404
  13.1 48.3 %copy-start.10 = (f32[100]{0:T(128)S(1)}, f32[100]{0:T(128)}, u32[]{:S(2)}) copy-start(f32[100]{0:T(128)} %param.21) | copy-start | bytes 1204
  37.2 20.8 %collective-permute-start.3 = (f32[4,104,512]{2,1,0:T(8,128)}, f32[4,104,512]{2,1,0:T(8,128)S(1)}, u32[]{:S(2)}, u32[]{:S(2)}) collective-permute-start(f32[4,104,512]{2,1,0:T(8,128)} %get-tuple-element.16.own_ref), channel_id=1, source_target_pairs={{0,64},{32,96},{64,0},{96,32},{1,65},{33,97},{65,1},{97,33},{2,66}... | collective-permute-start | bytes 2555912 | tf_op jit(solution)/shard_map/ppermute | solution.py:332
  40.6 55.0 %collective-permute-start.2 = (f32[4,104,512]{2,1,0:T(8,128)}, f32[4,104,512]{2,1,0:T(8,128)S(1)}, u32[]{:S(2)}, u32[]{:S(2)}) collective-permute-start(f32[4,104,512]{2,1,0:T(8,128)} %get-tuple-element.16.own_ref), channel_id=1, source_target_pairs={{0,32},{32,0},{64,96},{96,64},{1,33},{33,1},{65,97},{97,65},{2,34}... | collective-permute-start | bytes 2555912 | tf_op jit(solution)/shard_map/ppermute | solution.py:332
  58.1 37.6 %copy-start.4 = (f32[4,104,512]{2,1,0:T(8,128)}, f32[4,104,512]{2,1,0:T(8,128)S(1)}, u32[]{:S(2)}) copy-start(f32[4,104,512]{2,1,0:T(8,128)S(1)} %collective-permute-done.3.chip_ref) | copy-start | bytes 2555908
  58.1 37.6 %collective-permute-start.4 = (f32[4,104,512]{2,1,0:T(8,128)S(1)}, f32[4,104,512]{2,1,0:T(8,128)S(1)}, u32[]{:S(2)}, u32[]{:S(2)}) collective-permute-start(f32[4,104,512]{2,1,0:T(8,128)S(1)} %collective-permute-done.3.chip_ref), channel_id=1, source_target_pairs={{0,32},{32,0},{64,96},{96,64},{1,33},{33,1},{65,97},{97,65},{2,34}... | collective-permute-start | bytes 2555912 | tf_op jit(solution)/shard_map/ppermute | solution.py:332
  95.7 0.9 copy-start.5
  95.7 1.2 copy-start.6
  96.9 10.2 %copy-start.2 = (bf16[4,512,1024]{2,1,0:T(8,128)(2,1)S(1)}, bf16[4,512,1024]{2,1,0:T(8,128)(2,1)}, u32[]{:S(2)}) copy-start(bf16[4,512,1024]{2,1,0:T(8,128)(2,1)} %get-tuple-element.18.summed_ref) | copy-start | bytes 12582916
  114.1 23.4 %copy-start.1 = (bf16[4,512,1024]{2,1,0:T(8,128)(2,1)S(1)}, bf16[4,512,1024]{2,1,0:T(8,128)(2,1)}, u32[]{:S(2)}) copy-start(bf16[4,512,1024]{2,1,0:T(8,128)(2,1)} %get-tuple-element.24) | copy-start | bytes 12582916
  135.0 2.4 %copy-start.8 = (bf16[4,100,512]{2,1,0:T(8,128)(2,1)S(1)}, bf16[4,100,512]{2,1,0:T(8,128)(2,1)}, u32[]{:S(2)}) copy-start(bf16[4,100,512]{2,1,0:T(8,128)(2,1)} %get-tuple-element.25) | copy-start | bytes 1228804
  137.4 6.2 %collective-permute-start.7 = (bf16[32,16,1024]{2,1,0:T(8,128)(2,1)}, bf16[32,16,1024]{2,1,0:T(8,128)(2,1)}, u32[]{:S(2)}, u32[]{:S(2)}) collective-permute-start(bf16[32,16,1024]{2,1,0:T(8,128)(2,1)} %dynamic-slice_bitcast_fusion.1), channel_id=1, source_target_pairs={{0,32},{32,0},{64,96},{96,64},{1,33},{33,1},{65,97},{97,65},{2,34}... | collective-permute-start | bytes 3145736 | tf_op jit(solution)/shard_map/ppermute | solution.py:332
  137.5 0.8 copy-start.11
  143.1 3.1 %collective-permute-start.8 = (bf16[32,16,1152]{2,1,0:T(8,128)(2,1)S(1)}, bf16[32,16,1152]{2,1,0:T(8,128)(2,1)}, u32[]{:S(2)}, u32[]{:S(2)}) collective-permute-start(bf16[32,16,1152]{2,1,0:T(8,128)(2,1)S(1)} %dynamic-slice_bitcast_fusion), channel_id=1, source_target_pairs={{0,32},{32,0},{64,96},{96,64},{1,33},{33,1},{65,97},{97,65},{2,34}... | collective-permute-start | bytes 3538952 | tf_op jit(solution)/shard_map/ppermute | solution.py:332
  149.3 40.8 %all-to-all-start = ((bf16[32,16,2176]{2,1,0:T(8,128)(2,1)}), bf16[32,16,2176]{2,1,0:T(8,128)(2,1)S(1)}, u32[]{:S(2)}, u32[]{:S(2)}) async-start(bf16[32,16,2176]{2,1,0:T(8,128)(2,1)} %pad_maximum_fusion.1), calls=%async_computation | async-start | bytes 4456448 | tf_op jit(solution)/shard_map/all_to_all | solution.py:387
  158.9 5.4 %copy-start.9 = (s32[2,16]{1,0:T(2,128)S(1)}, s32[2,16]{1,0:T(2,128)}, u32[]{:S(2)}) copy-start(s32[2,16]{1,0:T(2,128)} %param.25) | copy-start | bytes 388
  161.1 13.8 %collective-permute-start.6 = (bf16[4,16,1024]{2,1,0:T(8,128)(2,1)S(1)}, bf16[4,16,1024]{2,1,0:T(8,128)(2,1)S(1)}, u32[]{:S(2)}, u32[]{:S(2)}) collective-permute-start(bf16[4,16,1024]{2,1,0:T(8,128)(2,1)S(1)} %get-tuple-element.28), channel_id=1, source_target_pairs={{0,1},{1,2},{2,3},{3,4},{4,5},{5,6},{6,7},{7,8},{8,9},{9,10},{10,1... | collective-permute-start | bytes 393224 | tf_op jit(solution)/shard_map/ppermute | solution.py:436
  164.3 32.8 %collective-permute-start.5 = (bf16[4,16,1024]{2,1,0:T(8,128)(2,1)}, bf16[4,16,1024]{2,1,0:T(8,128)(2,1)S(1)}, u32[]{:S(2)}, u32[]{:S(2)}) collective-permute-start(bf16[4,16,1024]{2,1,0:T(8,128)(2,1)} %get-tuple-element.27), channel_id=1, source_target_pairs={{1,0},{2,1},{3,2},{4,3},{5,4},{6,5},{7,6},{8,7},{9,8},{10,9},{11,1... | collective-permute-start | bytes 393224 | tf_op jit(solution)/shard_map/ppermute | solution.py:433
  190.4 10.6 %collective-permute-start.9 = (f32[16,2176]{1,0:T(8,128)S(1)}, f32[16,2176]{1,0:T(8,128)S(1)}, u32[]{:S(2)}, u32[]{:S(2)}) collective-permute-start(f32[16,2176]{1,0:T(8,128)S(1)} %convert_reduce_fusion), channel_id=1, source_target_pairs={{0,64},{32,96},{64,0},{96,32},{1,65},{33,97},{65,1},{97,33},{2,66}... | collective-permute-start | bytes 417800 | tf_op jit(solution)/shard_map/ppermute | solution.py:332
  194.1 7.0 %collective-permute-start.10 = (f32[16,2176]{1,0:T(8,128)S(1)}, f32[16,2176]{1,0:T(8,128)S(1)}, u32[]{:S(2)}, u32[]{:S(2)}) collective-permute-start(f32[16,2176]{1,0:T(8,128)S(1)} %convert_reduce_fusion), channel_id=1, source_target_pairs={{0,32},{32,0},{64,96},{96,64},{1,33},{33,1},{65,97},{97,65},{2,34}... | collective-permute-start | bytes 417800 | tf_op jit(solution)/shard_map/ppermute | solution.py:332
  197.2 6.8 %collective-permute-start.11 = (f32[16,2176]{1,0:T(8,128)S(1)}, f32[16,2176]{1,0:T(8,128)S(1)}, u32[]{:S(2)}, u32[]{:S(2)}) collective-permute-start(f32[16,2176]{1,0:T(8,128)S(1)} %convert_reduce_fusion), channel_id=1, source_target_pairs={{0,96},{32,64},{64,32},{96,0},{1,97},{33,65},{65,33},{97,1},{2,98}... | collective-permute-start | bytes 417800 | tf_op jit(solution)/shard_map/ppermute | solution.py:332

commit v3 on v2

--- a/solution.py
+++ b/solution.py
@@ -56,7 +56,7 @@
 def staged(tiles, work_ref, matmul, finish):
     for i, tile in enumerate(tiles):
         result = matmul(*tile)
-        work_ref[i % 2, : result.shape[0]] = result
+        work_ref[i % 2, : result.shape[0]] = result.astype(work_ref.dtype)
         if i:
             finish(work_ref.at[(i - 1) % 2], *tiles[i - 1])
     finish(work_ref.at[(len(tiles) - 1) % 2], *tiles[-1])
@@ -120,28 +120,26 @@
         pred_ref[m, : prior_ref.shape[0]] = prior_ref[...] + dot_nt(output_ref[...], out_ref[m])
 
 
-def slope_kernel(
-    comb_ref, pick_ref, grid_ref, summed_ref, node_ref, edge_ref, point_ref, both_ref, work_ref,
-):
-    members = comb_ref.shape[0]
-    for m in range(members):
+def edge_slope_kernel(comb_ref, pick_ref, grid_ref, edge_ref, both_ref, work_ref):
+    for m in range(comb_ref.shape[0]):
         both_ref[m, :TABLE] = comb_ref[m]
         both_ref[m, TABLE:] = grid_ref[...]
 
     def edge_slopes(buffer, m, h):
         for k in range(DEGREE):
             for r, c in parts(CHUNK):
-                value = 0.5 * slope_twice(
-                    buffer[k * CHUNK + r : k * CHUNK + r + PART, c : c + LANES]
-                )
-                edge_ref[m, k, r : r + PART, h + c : h + c + LANES] = value.astype(jnp.bfloat16)
-
+                value = slope_twice(buffer[k * CHUNK + r : k * CHUNK + r + PART, c : c + LANES])
+                edge_ref[m, k, r : r + PART, h + c : h + c + LANES] = value * 0.5
+
+    edge_stage(pick_ref, both_ref, work_ref, edge_slopes)
+
+
+def node_slope_kernel(summed_ref, node_ref, point_ref, work_ref):
     def node_slopes(buffer, m, h):
         for r, c in parts(CHUNK):
             value = 0.5 * slope_twice(buffer[r : r + PART, c : c + LANES])
             point_ref[m, r : r + PART, h + c : h + c + LANES] = value.astype(jnp.bfloat16)
 
-    edge_stage(pick_ref, both_ref, work_ref, edge_slopes)
     node_stage(summed_ref, node_ref, work_ref, node_slopes)
 
 
@@ -183,9 +181,10 @@
             - fairness / (2.0 * everyone * (everyone - 1)) * pair_abs
         )
         gradient = weight * (d * r - fairness / (everyone - 1) * pair_sign)
-        grad_ref[j] = gradient.astype(jnp.bfloat16)
         tall_ref[:variables] = gradient
-        grads.append(tall_ref[...].T.astype(jnp.bfloat16))
+        tall = tall_ref[...].T.astype(jnp.bfloat16)
+        grad_ref[j] = tall
+        grads.append(tall)
 
     sum_ref[...] += jnp.sum(terms, axis=0, keepdims=True)
 
@@ -207,7 +206,34 @@
         pre_ref[:, :, h : h + TILE] = (node_grad * slope).astype(jnp.bfloat16)
 
 
-def table_kernel(pre_ref, node_ref, slope_ref, place_ref, rows_ref, grad_ref, term_ref):
+def dot_tn(left, right):
+    return lax.dot_general(
+        left, right, (((0,), (0,)), ((), ())), preferred_element_type=jnp.float32
+    )
+
+
+def split_rows(value, core, mine_ref, other_ref, columns):
+    rows = mine_ref.shape[1]
+    pairs = value.reshape(value.shape[0] // (2 * rows), 2, rows, value.shape[1])
+    first, second = pairs[:, 0], pairs[:, 1]
+    mine_ref[:, :, columns] = jnp.where(core == 0, first, second).astype(jnp.bfloat16)
+    other_ref[:, :, columns] = jnp.where(core == 0, second, first).astype(jnp.bfloat16)
+
+
+def node_term_kernel(
+    core_ref, summed_ref, out_ref, pre_ref, grad_ref, loss_ref, mine_ref, other_ref,
+):
+    members, _, width = pre_ref.shape
+    core = core_ref[0]
+    node = sum(dot_tn(summed_ref[m], pre_ref[m]) for m in range(members))
+    split_rows(node, core, mine_ref, other_ref, slice(0, width))
+    output = sum(dot_tn(out_ref[m], grad_ref[m]) for m in range(members)) + loss_ref[...]
+    split_rows(output, core, mine_ref, other_ref, slice(width, width + TABLE))
+
+
+def table_kernel(
+    core_ref, pre_ref, node_ref, slope_ref, place_ref, rows_ref, grad_ref, mine_ref, other_ref,
+):
     members, points, _ = pre_ref.shape
     table_rows = grad_ref.shape[1]
     cast = []
@@ -219,12 +245,19 @@
         )[:table_rows]
         grad_ref[m] = table
         cast.append(table.astype(jnp.bfloat16))
-    term_ref[...] = dot(rows_ref[...], jnp.concatenate(cast, axis=0)).astype(jnp.bfloat16)
+    term = dot(rows_ref[...], jnp.concatenate(cast, axis=0))
+    split_rows(term, core_ref[0], mine_ref, other_ref, slice(0, term.shape[1]))
 
 
 def params():
     return pltpu.CompilerParams(
         dimension_semantics=("arbitrary",), vmem_limit_bytes=VMEM_LIMIT
+    )
+
+
+def cost(elements, depth, work):
+    return pl.CostEstimate(
+        flops=elements * (2 * depth + work), bytes_accessed=2 * elements, transcendentals=elements
     )
 
 
@@ -333,27 +366,36 @@
 
     chip_pred = swap(pred, 2)
     core_pred = swap(pred, 1)
-    far_pred = swap(chip_pred, 1)
-
-    edge_slope, node_slope = pl.pallas_call(
-        slope_kernel,
+
+    edge_slope = pl.pallas_call(
+        edge_slope_kernel,
         grid=(chunks,),
-        in_specs=[whole(comb), pick_block, chunk_rows, member_rows, whole(node_weight)],
-        out_specs=[
-            pl.BlockSpec((members, DEGREE, CHUNK, width), lambda c: (0, 0, c, 0)), member_rows,
-        ],
-        out_shape=[
-            jax.ShapeDtypeStruct((members, DEGREE, points, width), jnp.bfloat16), per_point,
-        ],
+        in_specs=[whole(comb), pick_block, chunk_rows],
+        out_specs=pl.BlockSpec((members, DEGREE, CHUNK, width), lambda c: (0, 0, c, 0)),
+        out_shape=jax.ShapeDtypeStruct((members, DEGREE, points, width), jnp.bfloat16),
         scratch_shapes=[
             pltpu.VMEM((members, TABLE + CHUNK, width), jnp.bfloat16),
-            pltpu.VMEM((2, DEGREE * CHUNK, TILE), jnp.float32),
+            pltpu.VMEM((2, DEGREE * CHUNK, TILE), jnp.bfloat16),
         ],
         compiler_params=params(),
-        name="slopes",
-    )(comb, pick, grid_state, summed, node_weight)
-
-    grad_pred, node_pre_grad, loss_row = pl.pallas_call(
+        cost_estimate=cost(members * DEGREE * points * width, 2 * TABLE, 20),
+        name="edge_slopes",
+    )(comb, pick, grid_state)
+    chip_pred, edge_slope = lax.optimization_barrier((chip_pred, edge_slope))
+    far_pred = swap(chip_pred, 1)
+    node_slope = pl.pallas_call(
+        node_slope_kernel,
+        grid=(chunks,),
+        in_specs=[member_rows, whole(node_weight)],
+        out_specs=member_rows,
+        out_shape=per_point,
+        scratch_shapes=[pltpu.VMEM((2, DEGREE * CHUNK, TILE), jnp.float32)],
+        compiler_params=params(),
+        cost_estimate=cost(members * points * width, width, 20),
+        name="node_slopes",
+    )(summed, node_weight)
+
+    grad_rows, node_pre_grad, loss_row = pl.pallas_call(
         loss_kernel,
         grid=(chunks,),
         in_specs=[
@@ -363,11 +405,11 @@
             whole(scale), member_rows, whole(output_padded),
         ],
         out_specs=[
-            pl.BlockSpec((members, variables, CHUNK), lambda c: (0, 0, c)), member_rows,
+            pl.BlockSpec((members, CHUNK, TABLE), lambda c: (0, c, 0)), member_rows,
             pl.BlockSpec((1, CHUNK), lambda c: (0, 0)),
         ],
         out_shape=[
-            jax.ShapeDtypeStruct((members, variables, points), jnp.bfloat16), per_point,
+            jax.ShapeDtypeStruct((members, points, TABLE), jnp.bfloat16), per_point,
             jax.ShapeDtypeStruct((1, CHUNK), jnp.float32),
         ],
         scratch_shapes=[
@@ -377,15 +419,15 @@
         name="loss",
     )(core[None], pred, core_pred, chip_pred, far_pred, target, area_weight[None, :], scale, node_slope, output_padded)
 
-    def own_half(term):
-        blocks = term.reshape(space, 2, width // space // 2, term.shape[1])
-        mine = lax.dynamic_index_in_dim(blocks, core, 1, keepdims=False)
-        other = swap(lax.dynamic_index_in_dim(blocks, 1 - core, 1, keepdims=False), 1)
-        return (mine.astype(jnp.float32) + other.astype(jnp.float32)).astype(jnp.bfloat16)
+    own_rows = width // space // 2
+    smem = pl.BlockSpec(memory_space=pltpu.SMEM)
+
+    def add_partner(mine, other):
+        return (mine.astype(jnp.float32) + swap(other, 1).astype(jnp.float32)).astype(jnp.bfloat16)
 
     def reduce_rows(half):
-        parts = lax.all_to_all(half, "space", 0, 0, tiled=True)
-        part = jnp.sum(parts.astype(jnp.float32), axis=0)
+        moved = lax.all_to_all(half, "space", 0, 0, tiled=True)
+        part = jnp.sum(moved.astype(jnp.float32), axis=0)
         mine = part + swap(part, 2)
         other = swap(part, 1) + swap(part, 3)
         return jnp.where(
@@ -394,48 +436,77 @@
             jnp.concatenate([other, mine], axis=0),
         )
 
-    node_term = jnp.einsum(
-        "mgh,mgk->hk", summed, node_pre_grad, preferred_element_type=jnp.float32
-    ).astype(jnp.bfloat16)
-    output_term = jnp.einsum(
-        "mgh,mvg->hv", node_out, grad_pred, preferred_element_type=jnp.float32
-    )
-    output_term = (
-        jnp.pad(output_term, ((0, 0), (0, TABLE - variables))) + loss_row
-    ).astype(jnp.bfloat16)
-    node_half = own_half(jnp.concatenate([node_term, output_term], axis=1))
-
-    source_columns = source_rows.reshape(members * table_rows, width).T
-    table_grad, project_term = pl.pallas_call(
-        table_kernel,
+    terms_block = pl.BlockSpec(
+        (TILE // (2 * own_rows), own_rows, width + TABLE), lambda c: (c, 0, 0)
+    )
+    terms_shape = jax.ShapeDtypeStruct((space, own_rows, width + TABLE), jnp.bfloat16)
+    some_columns = pl.BlockSpec((members, points, TILE), lambda c: (0, 0, c))
+    node_mine, node_other = pl.pallas_call(
+        node_term_kernel,
         grid=(width // TILE,),
         in_specs=[
-            whole(node_pre_grad),
-            pl.BlockSpec((TILE, width), lambda c: (c, 0)),
-            pl.BlockSpec((members, DEGREE, points, TILE), lambda c: (0, 0, 0, c)),
-            whole(place),
-            whole(source_columns),
-        ],
-        out_specs=[
-            pl.BlockSpec((members, table_rows, TILE), lambda c: (0, 0, c)),
-            pl.BlockSpec((width, TILE), lambda c: (0, c)),
-        ],
-        out_shape=[
-            jax.ShapeDtypeStruct((members, table_rows, width), jnp.float32),
-            jax.ShapeDtypeStruct((width, width), jnp.bfloat16),
-        ],
+            smem, some_columns, some_columns, whole(node_pre_grad), whole(grad_rows),
+            whole(loss_row),
+        ],
+        out_specs=[terms_block, terms_block],
+        out_shape=[terms_shape, terms_shape],
         compiler_params=params(),
-        name="table",
-    )(node_pre_grad, node_weight, edge_slope, place, source_columns)
-
-    sums = reduce_rows(jnp.concatenate([own_half(project_term), node_half], axis=2))
-
+        cost_estimate=cost(width * width, members * points, 1),
+        name="node_terms",
+    )(core[None], summed, node_out, node_pre_grad, grad_rows, loss_row)
+
+    source_columns = source_rows.reshape(members * table_rows, width).T
+    halves = 2
+    tiles = width // TILE // halves
+
+    def table_half(first, pre_grad):
+        columns = pl.BlockSpec((space, own_rows, TILE), lambda c: (0, 0, c))
+        shape = jax.ShapeDtypeStruct((space, own_rows, tiles * TILE), jnp.bfloat16)
+        return pl.pallas_call(
+            table_kernel,
+            grid=(tiles,),
+            in_specs=[
+                smem,
+                whole(pre_grad),
+                pl.BlockSpec((TILE, width), lambda c: (first + c, 0)),
+                pl.BlockSpec((members, DEGREE, points, TILE), lambda c: (0, 0, 0, first + c)),
+                whole(place),
+                whole(source_columns),
+            ],
+            out_specs=[
+                pl.BlockSpec((members, table_rows, TILE), lambda c: (0, 0, c)), columns, columns,
+            ],
+            out_shape=[
+                jax.ShapeDtypeStruct((members, table_rows, tiles * TILE), jnp.float32),
+                shape, shape,
+            ],
+            compiler_params=params(),
+            cost_estimate=cost(members * points * width // halves, 4 * width, 8),
+            name="table",
+        )(core[None], pre_grad, node_weight, edge_slope, place, source_columns)
+
+    first_grad, first_mine, first_other = table_half(0, node_pre_grad)
+    node_half = add_partner(node_mine, node_other)
+    second_input, node_half, first_mine = lax.optimization_barrier(
+        (node_pre_grad, node_half, first_mine)
+    )
+    node_sums = reduce_rows(node_half)
+    first_half = add_partner(first_mine, first_other)
+    second_grad, second_mine, second_other = table_half(tiles, second_input)
+    second_half = add_partner(second_mine, second_other)
+
+    table_grad = jnp.concatenate([first_grad, second_grad], axis=2)
     left_back = lax.ppermute(
         table_grad[:, own_nodes : own_nodes + send_rows].astype(jnp.bfloat16), "space", backward
     )
     right_back = lax.ppermute(
         table_grad[:, own_nodes + send_rows :].astype(jnp.bfloat16), "space", forward
     )
+    project_half = jnp.concatenate([first_half, second_half], axis=2)
+    project_half, left_back, right_back = lax.optimization_barrier(
+        (project_half, left_back, right_back)
+    )
+    project_sum = reduce_rows(project_half)
     projected_grad = (
         table_grad[:, :own_nodes]
         + jnp.einsum(
@@ -448,14 +519,13 @@
     grad_hidden = jnp.einsum(
         "mnk,hk->mnh", projected_grad, project_weight, preferred_element_type=jnp.float32
     ).astype(jnp.bfloat16)
-    output_at = 2 * width
-    loss_at = output_at + variables
+    loss_at = width + variables
     return (
         grad_hidden,
-        sums[:, :width] / total_points,
-        sums[:, width:output_at] / total_points,
-        sums[:, output_at:loss_at] / total_points,
-        jnp.sum(sums[0, loss_at:]) / (total_points * variables),
+        project_sum / total_points,
+        node_sums[:, :width] / total_points,
+        node_sums[:, width:loss_at] / total_points,
+        jnp.sum(node_sums[0, loss_at:]) / (total_points * variables),
     )
 
 

time: 209 us -> 191 us (0.914)
  waiting for transfers between devices: 42.9 us -> 14.4 us
  Pallas kernels: 85.4 us -> 103 us
  starting transfers between devices: 35.4 us -> 45 us
  matrix products: 14.1 us -> 7.2 us
  other arithmetic: 14.6 us -> 9.83 us
  local copies, waits for them, and re-layouts: 12.2 us -> 7.63 us
    pallas_call x2 -> x5, Pallas kernels: 51.2 us -> 68.9 us  [the longest x2 25.5 us: table_half(): pl.pallas_call(table_kernel, grid=(tiles,), in_specs=[smem, whole(pre_gra...]
    all_to_all x1 -> x2, waiting for transfers between devices: 14.8 us -> 0.01 us  [reduce_rows(): moved = lax.all_to_all(half, 'space', 0, 0, tiled=True)]
    all_to_all x1 -> x2, starting transfers between devices: 9.56 us -> 18.9 us  [reduce_rows(): moved = lax.all_to_all(half, 'space', 0, 0, tiled=True)]
    ppermute x8 -> x12, waiting for transfers between devices: 18.7 us -> 10.9 us  [swap(): lax.ppermute(value, 'member', [(i, i ^ flip) for i in range(lax.axis_size...]
    dot_general x3 -> x1, matrix products: 8.09 us -> 1.33 us  [shards(): jnp.einsum('sn,msh->mnh', chosen[1], left_back, preferred_element_type=jn...]
    ppermute x1, waiting for transfers between devices: 9.31 us -> 2.6 us  [shards(): lax.ppermute(table_grad[:, own_nodes + send_rows:].astype(jnp.bfloat16),...]
    squeeze x2 -> x0, local copies, waits for them, and re-layouts: 2.47 us -> none  [own_half(): lax.dynamic_index_in_dim(blocks, 1 - core, 1, keepdims=False)]
    ppermute x8 -> x12, starting transfers between devices: 15.7 us -> 15.1 us  [swap(): lax.ppermute(value, 'member', [(i, i ^ flip) for i in range(lax.axis_size...]
  transfers between devices with their start and end apart: 13 -> 18, of which waited for: 5 -> 6; matrix products, arithmetic and copies ran while one was open for 11% -> 11% of each run, Pallas kernels for 15% -> 31%
where the time goes in v3:
time: 191 us; the launch traced here: 190 us
  Pallas kernels  103 us (54%)
  starting transfers between devices  45 us (24%)
  waiting for transfers between devices  14.4 us (8%)
  other arithmetic  9.83 us (5%)
  local copies, waits for them, and re-layouts  7.63 us (4%)
  matrix products  7.2 us (4%)
  between operations  3.42 us (2%)
    pallas_call x2, Pallas kernels, table_half(): pl.pallas_call(table_kernel, grid=(tiles,), in_specs=[smem, whole(pre_gra...  25.5 us
    pallas_call x1, Pallas kernels, shards(): pl.pallas_call(forward_kernel_with_table, grid=(chunks,), in_specs=[whole...  24 us
    pallas_call x1, Pallas kernels, shards(): pl.pallas_call(edge_slope_kernel, grid=(chunks,), in_specs=[whole(comb),...  21.8 us
    all_to_all x2, starting transfers between devices, reduce_rows(): moved = lax.all_to_all(half, 'space', 0, 0, tiled=True)  18.9 us
    ppermute x12, starting transfers between devices, swap(): lax.ppermute(value, 'member', [(i, i ^ flip) for i in range(lax.axis_size...  15.1 us
    pallas_call x1, Pallas kernels, shards(): pl.pallas_call(node_slope_kernel, grid=(chunks,), in_specs=[member_rows,...  11.1 us
    ppermute x12, waiting for transfers between devices, swap(): lax.ppermute(value, 'member', [(i, i ^ flip) for i in range(lax.axis_size...  10.9 us
    pallas_call x1, Pallas kernels, shards(): pl.pallas_call(node_term_kernel, grid=(width // TILE,), in_specs=[smem, s...  10.5 us
  transfers between devices with their start and end apart: 18, of which 6 were waited for; matrix products, arithmetic and copies ran while one was open for 11% of the time, Pallas kernels for 31%

profile of v3, /device:TPU:1, one launch (start us, length us, event | category | flops | bytes accessed | tf_op | source)
XLA Modules:
  0.0 190.4 jit_solution(14987220693762812185)
XLA Ops:
  0.6 1.4 fusion.12
  2.1 4.4 %collective-permute-start = (bf16[4,16,1024]{2,1,0:T(8,128)(2,1)S(1)}, bf16[4,16,1024]{2,1,0:T(8,128)(2,1)S(1)}, u32[]{:S(2)}, u32[]{:S(2)}) collective-permute-start(bf16[4,16,1024]{2,1,0:T(8,128)(2,1)S(1)} %get-tuple-element.54), channel_id=1, source_target_pairs={{0,1},{1,2},{2,3},{3,4},{4,5},{5,6},{6,7},{7,8},{8,9},{9,10},{10,1... | collective-permute-start | bytes 393224 | tf_op jit(solution)/shard_map/ppermute | solution.py:301
  6.4 1.3 collective-permute-start.1
  8.4 0.7 fusion.24
  9.1 0.8 convert_add_fusion
  9.9 0.8 add_select_fusion
  10.7 0.1 iota_compare_fusion.6
  10.8 1.3 fusion.5.refs_2_.pick_ref
  12.2 0.0 collective-permute-done
  12.2 0.9 copy-done
  13.1 24.0 %forward.1 = (f32[4,104,512]{2,1,0:T(8,128)}, bf16[4,512,1024]{2,1,0:T(8,128)(2,1)}, bf16[4,512,1024]{2,1,0:T(8,128)(2,1)}, bf16[4,128,1024]{2,1,0:T(8,128)(2,1)}) custom-call(bf16[4,96,1024]{2,1,0:T(8,128)(2,1)} %copy-done, bf16[1024,1024]{1,0:T(8,128)(2,1)} %refs_1_.1, bf16[4,512,256]{2,1,0:T(8,128)(2,1)} %fusion.5.refs_2_.pick_ref, ...), custom_call_target="tpu_custom_call" | custom-call | tf_op jit(solution)/shard_map/forward/pallas_call | solution.py:341
  37.1 3.4 %collective-permute-start.3 = (f32[4,104,512]{2,1,0:T(8,128)}, f32[4,104,512]{2,1,0:T(8,128)S(1)}, u32[]{:S(2)}, u32[]{:S(2)}) collective-permute-start(f32[4,104,512]{2,1,0:T(8,128)} %get-tuple-element.28.own_ref), channel_id=1, source_target_pairs={{0,64},{32,96},{64,0},{96,32},{1,65},{33,97},{65,1},{97,33},{2,66}... | collective-permute-start | bytes 2555912 | tf_op jit(solution)/shard_map/ppermute | solution.py:365
  40.5 2.3 %collective-permute-start.2 = (f32[4,104,512]{2,1,0:T(8,128)}, f32[4,104,512]{2,1,0:T(8,128)S(1)}, u32[]{:S(2)}, u32[]{:S(2)}) collective-permute-start(f32[4,104,512]{2,1,0:T(8,128)} %get-tuple-element.28.own_ref), channel_id=1, source_target_pairs={{0,32},{32,0},{64,96},{96,64},{1,33},{33,1},{65,97},{97,65},{2,34}... | collective-permute-start | bytes 2555912 | tf_op jit(solution)/shard_map/ppermute | solution.py:365
  42.8 21.8 %edge_slopes.1.slope_ref = bf16[4,4,512,1024]{3,2,1,0:T(8,128)(2,1)} custom-call(bf16[4,128,1024]{2,1,0:T(8,128)(2,1)} %get-tuple-element.29.comb_ref, bf16[4,512,256]{2,1,0:T(8,128)(2,1)} %fusion.5.refs_2_.pick_ref, bf16[512,1024]{1,0:T(8,128)(2,1)} %grid_ref.1), custom_call_target="tpu_custom_call" | custom-call | flops 4462739456 | bytes 16777216 | tf_op jit(solution)/shard_map/edge_slopes/pallas_call | solution.py:370
  64.6 0.3 collective-permute-start.4
  64.9 0.7 pad.9.output_ref
  65.6 0.7 copy.20.variable_ref
  66.3 11.1 %node_slopes.1.slope_ref = bf16[4,512,1024]{2,1,0:T(8,128)(2,1)} custom-call(bf16[4,512,1024]{2,1,0:T(8,128)(2,1)} %get-tuple-element.31.summed_ref, bf16[1024,1024]{1,0:T(8,128)(2,1)} %node_ref.5), custom_call_target="tpu_custom_call" | custom-call | flops 4336910336 | bytes 4194304 | tf_op jit(solution)/shard_map/node_slopes/pallas_call | solution.py:386
  77.5 0.9 copy-done.5
  78.4 0.3 copy-done.6
  78.7 10.1 %loss.1 = (bf16[4,512,128]{2,1,0:T(8,128)(2,1)}, bf16[4,512,1024]{2,1,0:T(8,128)(2,1)}, f32[1,128]{1,0:T(1,128)}) custom-call(s32[1]{0:T(128)} %bitcast.core_index_ref.core_ref, f32[4,104,512]{2,1,0:T(8,128)} %get-tuple-element.28.own_ref, f32[4,104,512]{2,1,0:T(8,128)} %copy-done.5, f32[4,104,512]{2,1,0:T(8,128)} %copy-done.4, f32[4,104,512]{2,1,0:T(8,128)} %copy-done.6, ...), custom_call_target="tpu_custom_call" | custom-call | tf_op jit(solution)/shard_map/loss/pallas_call | solution.py:398
  88.9 10.5 %node_terms.1 = (bf16[32,16,1152]{2,1,0:T(8,128)(2,1)}, bf16[32,16,1152]{2,1,0:T(8,128)(2,1)}) custom-call(s32[1]{0:T(128)} %bitcast.core_index_ref.core_ref, bf16[4,512,1024]{2,1,0:T(8,128)(2,1)} %get-tuple-element.31.summed_ref, bf16[4,512,1024]{2,1,0:T(8,128)(2,1)} %get-tuple-element.35.out_ref, bf16[4,512,1024]{2,1,0:T(8,128)(2,1)} %get-tuple-element.41.pre_ref, ...), custom_call_target="tpu_custom_call" | custom-call | flops 4296015872 | bytes 2097152 | tf_op jit(solution)/shard_map/node_terms/pallas_call | solution.py:444
  99.3 0.5 collective-permute-start.5
  99.8 0.9 fusion.14.place_ref
  100.7 0.1 iota_compare_fusion.8
  100.8 1.2 copy.21
  102.0 12.7 %table.2 = (f32[4,96,512]{2,1,0:T(8,128)}, bf16[32,16,512]{2,1,0:T(8,128)(2,1)}, bf16[32,16,512]{2,1,0:T(8,128)(2,1)}) custom-call(s32[1]{0:T(128)} %bitcast.core_index_ref.core_ref, bf16[4,512,1024]{2,1,0:T(8,128)(2,1)} %get-tuple-element.41.pre_ref, bf16[1024,1024]{1,0:T(8,128)(2,1)} %node_ref.5, bf16[4,4,512,1024]{3,2,1,0:T(8,128)(2,1)} %edge_slopes.1.slope_ref, ...), custom_call_target="tpu_custom_call" | custom-call | flops 8598323200 | bytes 2097152 | tf_op jit(solution)/shard_map/table/pallas_call | solution.py:465
  114.7 0.0 collective-permute-start.6
  114.7 1.3 constant_dynamic-update-slice_fusion.4
  116.0 0.2 copy-done.3
  116.2 1.4 add_convert_fusion
  117.6 9.7 %all-to-all-start.1 = ((bf16[32,16,1152]{2,1,0:T(8,128)(2,1)}), bf16[32,16,1152]{2,1,0:T(8,128)(2,1)S(1)}, u32[]{:S(2)}, u32[]{:S(2)}) async-start(bf16[32,16,1152]{2,1,0:T(8,128)(2,1)} %add_convert_fusion), calls=%async_computation.1 | async-start | bytes 2359296 | tf_op jit(solution)/shard_map/all_to_all | solution.py:429
  127.3 12.8 %table.3 = (f32[4,96,512]{2,1,0:T(8,128)}, bf16[32,16,512]{2,1,0:T(8,128)(2,1)}, bf16[32,16,512]{2,1,0:T(8,128)(2,1)}) custom-call(s32[1]{0:T(128)} %bitcast.core_index_ref.core_ref, bf16[4,512,1024]{2,1,0:T(8,128)(2,1)} %get-tuple-element.41.pre_ref, bf16[1024,1024]{1,0:T(8,128)(2,1)} %node_ref.5, bf16[4,4,512,1024]{3,2,1,0:T(8,128)(2,1)} %edge_slopes.1.slope_ref, ...), custom_call_target="tpu_custom_call" | custom-call | flops 8598323200 | bytes 2097152 | tf_op jit(solution)/shard_map/table/pallas_call | solution.py:465
  140.1 0.5 collective-permute-start.7
  140.6 1.3 constant_dynamic-update-slice_fusion.3
  141.8 0.1 convert.4
  142.0 1.3 collective-permute-start.8
  143.3 4.1 %collective-permute-start.9 = (bf16[4,16,1024]{2,1,0:T(8,128)(2,1)S(1)}, bf16[4,16,1024]{2,1,0:T(8,128)(2,1)S(1)}, u32[]{:S(2)}, u32[]{:S(2)}) collective-permute-start(bf16[4,16,1024]{2,1,0:T(8,128)(2,1)S(1)} %get-tuple-element.51), channel_id=1, source_target_pairs={{0,1},{1,2},{2,3},{3,4},{4,5},{5,6},{6,7},{7,8},{8,9},{9,10},{10,1... | collective-permute-start | bytes 393224 | tf_op jit(solution)/shard_map/ppermute | solution.py:502
  147.4 0.0 collective-permute-done.6
  147.4 0.2 add_convert_fusion.2
  147.6 0.2 add_convert_fusion.1
  147.8 1.1 pad_maximum_fusion
  148.9 0.8 collective-permute-done.8
  149.8 2.6 %collective-permute-done.9 = bf16[4,16,1024]{2,1,0:T(8,128)(2,1)S(1)} collective-permute-done((bf16[4,16,1024]{2,1,0:T(8,128)(2,1)S(1)}, bf16[4,16,1024]{2,1,0:T(8,128)(2,1)S(1)}, u32[]{:S(2)}, u32[]{:S(2)}) %collective-permute-start.9) | collective-permute-done | bytes 131104 | tf_op jit(solution)/shard_map/ppermute | solution.py:502
  152.4 1.3 fusion.7
  153.7 0.0 all-to-all-done.1
  153.7 9.3 %all-to-all-start = ((bf16[32,16,1024]{2,1,0:T(8,128)(2,1)}), bf16[32,16,1024]{2,1,0:T(8,128)(2,1)S(1)}, u32[]{:S(2)}, u32[]{:S(2)}) async-start(bf16[32,16,1024]{2,1,0:T(8,128)(2,1)} %pad_maximum_fusion), calls=%async_computation | async-start | bytes 2097152 | tf_op jit(solution)/shard_map/all_to_all | solution.py:429
  163.0 0.2 convert_reduce_fusion
  163.1 0.7 collective-permute-start.13
  163.8 1.7 collective-permute-start.14
  165.5 2.3 %collective-permute-start.15 = (f32[16,1152]{1,0:T(8,128)S(1)}, f32[16,1152]{1,0:T(8,128)S(1)}, u32[]{:S(2)}, u32[]{:S(2)}) collective-permute-start(f32[16,1152]{1,0:T(8,128)S(1)} %convert_reduce_fusion), channel_id=1, source_target_pairs={{0,96},{32,64},{64,32},{96,0},{1,97},{33,65},{65,33},{97,1},{2,98}... | collective-permute-start | bytes 221192 | tf_op jit(solution)/shard_map/ppermute | solution.py:365
  167.8 3.7 %fusion.8 = bf16[4,64,1024]{2,1,0:T(8,128)(2,1)} fusion(bf16[1024,1024]{1,0:T(8,128)(2,1)} %refs_1_.1, f32[4,64,1024]{2,1,0:T(8,128)} %fusion.7, bf16[4,16,1024]{2,1,0:T(8,128)(2,1)S(1)} %collective-permute-done.9, pred[2,16,64]{2,1,0:T(8,128)(4,1)S(1)} %iota_compare_fusion.8), kind=kOutput, calls=%fused_computation.15 | convolution fusion | flops 546045952 | bytes 3803136 | tf_op jit(solution)/shard_map/mnk,hk->mnh/dot_general | solution.py:519
  171.4 0.4 collective-permute-done.13
  171.9 8.4 %collective-permute-done.15 = f32[16,1152]{1,0:T(8,128)S(1)} collective-permute-done((f32[16,1152]{1,0:T(8,128)S(1)}, f32[16,1152]{1,0:T(8,128)S(1)}, u32[]{:S(2)}, u32[]{:S(2)}) %collective-permute-start.15) | collective-permute-done | bytes 73760 | tf_op jit(solution)/shard_map/ppermute | solution.py:365
  180.4 0.6 slice_multiply_fusion.1
  181.0 0.7 slice_multiply_fusion
  181.7 0.2 convert_reduce_fusion.1
  181.8 0.4 collective-permute-start.10
  182.2 0.8 collective-permute-start.11
  183.0 2.3 %collective-permute-start.12 = (f32[16,1024]{1,0:T(8,128)S(1)}, f32[16,1024]{1,0:T(8,128)S(1)}, u32[]{:S(2)}, u32[]{:S(2)}) collective-permute-start(f32[16,1024]{1,0:T(8,128)S(1)} %convert_reduce_fusion.1), channel_id=1, source_target_pairs={{0,96},{32,64},{64,32},{96,0},{1,97},{33,65},{65,33},{97,1},{2,98}... | collective-permute-start | bytes 196616 | tf_op jit(solution)/shard_map/ppermute | solution.py:365
  185.3 0.7 slice_reduce_fusion
  186.6 0.3 collective-permute-done.10
  186.9 1.7 collective-permute-done.12
  188.6 0.7 fusion.16
  (43 shorter events, 0.3 us)
Async XLA Ops:
  0.6 11.5 %copy-start.2 = (bf16[4,64,1024]{2,1,0:T(8,128)(2,1)S(1)}, bf16[4,64,1024]{2,1,0:T(8,128)(2,1)}, u32[]{:S(2)}) copy-start(bf16[4,64,1024]{2,1,0:T(8,128)(2,1)} %param.13) | copy-start | bytes 1572868
  2.1 10.1 %collective-permute-start = (bf16[4,16,1024]{2,1,0:T(8,128)(2,1)S(1)}, bf16[4,16,1024]{2,1,0:T(8,128)(2,1)S(1)}, u32[]{:S(2)}, u32[]{:S(2)}) collective-permute-start(bf16[4,16,1024]{2,1,0:T(8,128)(2,1)S(1)} %get-tuple-element.54), channel_id=1, source_target_pairs={{0,1},{1,2},{2,3},{3,4},{4,5},{5,6},{6,7},{7,8},{8,9},{9,10},{10,1... | collective-permute-start | bytes 393224 | tf_op jit(solution)/shard_map/ppermute | solution.py:301
  6.4 5.8 %collective-permute-start.1 = (bf16[4,16,1024]{2,1,0:T(8,128)(2,1)S(1)}, bf16[4,16,1024]{2,1,0:T(8,128)(2,1)S(1)}, u32[]{:S(2)}, u32[]{:S(2)}) collective-permute-start(bf16[4,16,1024]{2,1,0:T(8,128)(2,1)S(1)} %get-tuple-element.53), channel_id=1, source_target_pairs={{1,0},{2,1},{3,2},{4,3},{5,4},{6,5},{7,6},{8,7},{9,8},{10,9},{11,1... | collective-permute-start | bytes 393224 | tf_op jit(solution)/shard_map/ppermute | solution.py:302
  12.2 0.9 copy-start
  37.1 27.5 %collective-permute-start.3 = (f32[4,104,512]{2,1,0:T(8,128)}, f32[4,104,512]{2,1,0:T(8,128)S(1)}, u32[]{:S(2)}, u32[]{:S(2)}) collective-permute-start(f32[4,104,512]{2,1,0:T(8,128)} %get-tuple-element.28.own_ref), channel_id=1, source_target_pairs={{0,64},{32,96},{64,0},{96,32},{1,65},{33,97},{65,1},{97,33},{2,66}... | collective-permute-start | bytes 2555912 | tf_op jit(solution)/shard_map/ppermute | solution.py:365
  40.5 37.0 %collective-permute-start.2 = (f32[4,104,512]{2,1,0:T(8,128)}, f32[4,104,512]{2,1,0:T(8,128)S(1)}, u32[]{:S(2)}, u32[]{:S(2)}) collective-permute-start(f32[4,104,512]{2,1,0:T(8,128)} %get-tuple-element.28.own_ref), channel_id=1, source_target_pairs={{0,32},{32,0},{64,96},{96,64},{1,33},{33,1},{65,97},{97,65},{2,34}... | collective-permute-start | bytes 2555912 | tf_op jit(solution)/shard_map/ppermute | solution.py:365
  42.8 22.1 %copy-start.7 = (bf16[1024,100]{0,1:T(8,128)(2,1)S(1)}, bf16[1024,100]{0,1:T(8,128)(2,1)}, u32[]{:S(2)}) copy-start(bf16[1024,100]{0,1:T(8,128)(2,1)} %param.17) | copy-start | bytes 614404
  42.8 22.8 %copy-start.11 = (f32[100]{0:T(128)S(1)}, f32[100]{0:T(128)}, u32[]{:S(2)}) copy-start(f32[100]{0:T(128)} %param.21) | copy-start | bytes 1204
  64.6 12.9 %copy-start.4 = (f32[4,104,512]{2,1,0:T(8,128)}, f32[4,104,512]{2,1,0:T(8,128)S(1)}, u32[]{:S(2)}) copy-start(f32[4,104,512]{2,1,0:T(8,128)S(1)} %collective-permute-done.3.chip_ref) | copy-start | bytes 2555908
  64.6 12.9 %collective-permute-start.4 = (f32[4,104,512]{2,1,0:T(8,128)S(1)}, f32[4,104,512]{2,1,0:T(8,128)S(1)}, u32[]{:S(2)}, u32[]{:S(2)}) collective-permute-start(f32[4,104,512]{2,1,0:T(8,128)S(1)} %collective-permute-done.3.chip_ref), channel_id=1, source_target_pairs={{0,32},{32,0},{64,96},{96,64},{1,33},{33,1},{65,97},{97,65},{2,34}... | collective-permute-start | bytes 2555912 | tf_op jit(solution)/shard_map/ppermute | solution.py:365
  77.5 0.9 copy-start.5
  77.5 1.2 copy-start.6
  88.9 11.9 %copy-start.10 = (s32[2,16]{1,0:T(2,128)S(1)}, s32[2,16]{1,0:T(2,128)}, u32[]{:S(2)}) copy-start(s32[2,16]{1,0:T(2,128)} %param.25) | copy-start | bytes 388
  88.9 11.9 %copy-start.1 = (bf16[4,96,1024]{2,1,0:T(8,128)(2,1)S(1)}, bf16[4,96,1024]{2,1,0:T(8,128)(2,1)}, u32[]{:S(2)}) copy-start(bf16[4,96,1024]{2,1,0:T(8,128)(2,1)} %copy-done) | copy-start | bytes 2359300
  99.3 16.7 %collective-permute-start.5 = (bf16[32,16,1152]{2,1,0:T(8,128)(2,1)}, bf16[32,16,1152]{2,1,0:T(8,128)(2,1)S(1)}, u32[]{:S(2)}, u32[]{:S(2)}) collective-permute-start(bf16[32,16,1152]{2,1,0:T(8,128)(2,1)} %get-tuple-element.39), channel_id=1, source_target_pairs={{0,32},{32,0},{64,96},{96,64},{1,33},{33,1},{65,97},{97,65},{2,34}... | collective-permute-start | bytes 3538952 | tf_op jit(solution)/shard_map/ppermute | solution.py:365
  114.7 1.5 copy-start.3
  114.7 32.7 %collective-permute-start.6 = (bf16[32,16,512]{2,1,0:T(8,128)(2,1)}, bf16[32,16,512]{2,1,0:T(8,128)(2,1)S(1)}, u32[]{:S(2)}, u32[]{:S(2)}) collective-permute-start(bf16[32,16,512]{2,1,0:T(8,128)(2,1)} %get-tuple-element.44), channel_id=1, source_target_pairs={{0,32},{32,0},{64,96},{96,64},{1,33},{33,1},{65,97},{97,65},{2,34}... | collective-permute-start | bytes 1572872 | tf_op jit(solution)/shard_map/ppermute | solution.py:365
  117.6 36.1 %all-to-all-start.1 = ((bf16[32,16,1152]{2,1,0:T(8,128)(2,1)}), bf16[32,16,1152]{2,1,0:T(8,128)(2,1)S(1)}, u32[]{:S(2)}, u32[]{:S(2)}) async-start(bf16[32,16,1152]{2,1,0:T(8,128)(2,1)} %add_convert_fusion), calls=%async_computation.1 | async-start | bytes 2359296 | tf_op jit(solution)/shard_map/all_to_all | solution.py:429
  140.1 7.5 %collective-permute-start.7 = (bf16[32,16,512]{2,1,0:T(8,128)(2,1)}, bf16[32,16,512]{2,1,0:T(8,128)(2,1)S(1)}, u32[]{:S(2)}, u32[]{:S(2)}) collective-permute-start(bf16[32,16,512]{2,1,0:T(8,128)(2,1)} %get-tuple-element.46), channel_id=1, source_target_pairs={{0,32},{32,0},{64,96},{96,64},{1,33},{33,1},{65,97},{97,65},{2,34}... | collective-permute-start | bytes 1572872 | tf_op jit(solution)/shard_map/ppermute | solution.py:365
  140.6 6.8 %copy-start.8 = (bf16[32,16,512]{2,1,0:T(8,128)(2,1)S(1)}, bf16[32,16,512]{2,1,0:T(8,128)(2,1)}, u32[]{:S(2)}) copy-start(bf16[32,16,512]{2,1,0:T(8,128)(2,1)} %get-tuple-element.43) | copy-start | bytes 1572868
  141.8 5.7 %copy-start.9 = (bf16[32,16,512]{2,1,0:T(8,128)(2,1)S(1)}, bf16[32,16,512]{2,1,0:T(8,128)(2,1)}, u32[]{:S(2)}) copy-start(bf16[32,16,512]{2,1,0:T(8,128)(2,1)} %get-tuple-element.45) | copy-start | bytes 1572868
  142.0 7.8 %collective-permute-start.8 = (bf16[4,16,1024]{2,1,0:T(8,128)(2,1)S(1)}, bf16[4,16,1024]{2,1,0:T(8,128)(2,1)S(1)}, u32[]{:S(2)}, u32[]{:S(2)}) collective-permute-start(bf16[4,16,1024]{2,1,0:T(8,128)(2,1)S(1)} %get-tuple-element.52), channel_id=1, source_target_pairs={{1,0},{2,1},{3,2},{4,3},{5,4},{6,5},{7,6},{8,7},{9,8},{10,9},{11,1... | collective-permute-start | bytes 393224 | tf_op jit(solution)/shard_map/ppermute | solution.py:499
  143.3 9.1 %collective-permute-start.9 = (bf16[4,16,1024]{2,1,0:T(8,128)(2,1)S(1)}, bf16[4,16,1024]{2,1,0:T(8,128)(2,1)S(1)}, u32[]{:S(2)}, u32[]{:S(2)}) collective-permute-start(bf16[4,16,1024]{2,1,0:T(8,128)(2,1)S(1)} %get-tuple-element.51), channel_id=1, source_target_pairs={{0,1},{1,2},{2,3},{3,4},{4,5},{5,6},{6,7},{7,8},{8,9},{9,10},{10,1... | collective-permute-start | bytes 393224 | tf_op jit(solution)/shard_map/ppermute | solution.py:502
  153.7 28.0 %all-to-all-start = ((bf16[32,16,1024]{2,1,0:T(8,128)(2,1)}), bf16[32,16,1024]{2,1,0:T(8,128)(2,1)S(1)}, u32[]{:S(2)}, u32[]{:S(2)}) async-start(bf16[32,16,1024]{2,1,0:T(8,128)(2,1)} %pad_maximum_fusion), calls=%async_computation | async-start | bytes 2097152 | tf_op jit(solution)/shard_map/all_to_all | solution.py:429
  163.1 8.8 %collective-permute-start.13 = (f32[16,1152]{1,0:T(8,128)S(1)}, f32[16,1152]{1,0:T(8,128)S(1)}, u32[]{:S(2)}, u32[]{:S(2)}) collective-permute-start(f32[16,1152]{1,0:T(8,128)S(1)} %convert_reduce_fusion), channel_id=1, source_target_pairs={{0,64},{32,96},{64,0},{96,32},{1,65},{33,97},{65,1},{97,33},{2,66}... | collective-permute-start | bytes 221192 | tf_op jit(solution)/shard_map/ppermute | solution.py:365
  163.8 8.1 %collective-permute-start.14 = (f32[16,1152]{1,0:T(8,128)S(1)}, f32[16,1152]{1,0:T(8,128)S(1)}, u32[]{:S(2)}, u32[]{:S(2)}) collective-permute-start(f32[16,1152]{1,0:T(8,128)S(1)} %convert_reduce_fusion), channel_id=1, source_target_pairs={{0,32},{32,0},{64,96},{96,64},{1,33},{33,1},{65,97},{97,65},{2,34}... | collective-permute-start | bytes 221192 | tf_op jit(solution)/shard_map/ppermute | solution.py:365
  165.5 14.9 %collective-permute-start.15 = (f32[16,1152]{1,0:T(8,128)S(1)}, f32[16,1152]{1,0:T(8,128)S(1)}, u32[]{:S(2)}, u32[]{:S(2)}) collective-permute-start(f32[16,1152]{1,0:T(8,128)S(1)} %convert_reduce_fusion), channel_id=1, source_target_pairs={{0,96},{32,64},{64,32},{96,0},{1,97},{33,65},{65,33},{97,1},{2,98}... | collective-permute-start | bytes 221192 | tf_op jit(solution)/shard_map/ppermute | solution.py:365
  181.8 5.0 %collective-permute-start.10 = (f32[16,1024]{1,0:T(8,128)S(1)}, f32[16,1024]{1,0:T(8,128)S(1)}, u32[]{:S(2)}, u32[]{:S(2)}) collective-permute-start(f32[16,1024]{1,0:T(8,128)S(1)} %convert_reduce_fusion.1), channel_id=1, source_target_pairs={{0,64},{32,96},{64,0},{96,32},{1,65},{33,97},{65,1},{97,33},{2,66}... | collective-permute-start | bytes 196616 | tf_op jit(solution)/shard_map/ppermute | solution.py:365
  182.2 4.7 %collective-permute-start.11 = (f32[16,1024]{1,0:T(8,128)S(1)}, f32[16,1024]{1,0:T(8,128)S(1)}, u32[]{:S(2)}, u32[]{:S(2)}) collective-permute-start(f32[16,1024]{1,0:T(8,128)S(1)} %convert_reduce_fusion.1), channel_id=1, source_target_pairs={{0,32},{32,0},{64,96},{96,64},{1,33},{33,1},{65,97},{97,65},{2,34}... | collective-permute-start | bytes 196616 | tf_op jit(solution)/shard_map/ppermute | solution.py:365
  183.0 5.6 %collective-permute-start.12 = (f32[16,1024]{1,0:T(8,128)S(1)}, f32[16,1024]{1,0:T(8,128)S(1)}, u32[]{:S(2)}, u32[]{:S(2)}) collective-permute-start(f32[16,1024]{1,0:T(8,128)S(1)} %convert_reduce_fusion.1), channel_id=1, source_target_pairs={{0,96},{32,64},{64,32},{96,0},{1,97},{33,65},{65,33},{97,1},{2,98}... | collective-permute-start | bytes 196616 | tf_op jit(solution)/shard_map/ppermute | solution.py:365

commit v4 on v3

--- a/solution.py
+++ b/solution.py
@@ -18,7 +18,6 @@
 TILE = 256
 PART = 32
 LANES = 128
-VMEM_LIMIT = 56 * 1024 * 1024
 
 
 def tanh_of(u):
@@ -31,8 +30,9 @@
     return u + u * t
 
 
-def slope_twice(u):
-    s, t = tanh_of(u)
+def slope_twice(u, s=None, t=None):
+    if t is None:
+        s, t = tanh_of(u)
     q = u * (SQRT_TWO_PI + (3.0 * SQRT_TWO_PI * CUBIC) * s)
     return (1.0 + t) * (1.0 + (1.0 - t) * q)
 
@@ -56,10 +56,10 @@
 def staged(tiles, work_ref, matmul, finish):
     for i, tile in enumerate(tiles):
         result = matmul(*tile)
-        work_ref[i % 2, : result.shape[0]] = result.astype(work_ref.dtype)
+        work_ref[i % 2][: result.shape[0]] = result.astype(work_ref[0].dtype)
         if i:
-            finish(work_ref.at[(i - 1) % 2], *tiles[i - 1])
-    finish(work_ref.at[(len(tiles) - 1) % 2], *tiles[-1])
+            finish(work_ref[(i - 1) % 2], *tiles[i - 1])
+    finish(work_ref[(len(tiles) - 1) % 2], *tiles[-1])
 
 
 def edge_stage(pick_ref, comb_ref, work_ref, finish):
@@ -85,7 +85,7 @@
 
 def forward_kernel(
     rows_ref, project_ref, pick_ref, grid_ref, node_ref, output_ref, prior_ref,
-    pred_ref, summed_ref, out_ref, comb_ref, work_ref,
+    pred_ref, summed_ref, out_ref, slope_ref, comb_ref, *work_ref,
 ):
     members, table_rows, width = rows_ref.shape
 
@@ -110,8 +110,11 @@
 
     def node_values(buffer, m, h):
         for r, c in parts(CHUNK):
-            value = 0.5 * gelu_twice(buffer[r : r + PART, c : c + LANES])
-            out_ref[m, r : r + PART, h + c : h + c + LANES] = value.astype(jnp.bfloat16)
+            u = buffer[r : r + PART, c : c + LANES]
+            s, t = tanh_of(u)
+            place = (m, slice(r, r + PART), slice(h + c, h + c + LANES))
+            out_ref[place] = (0.5 * (u + u * t)).astype(jnp.bfloat16)
+            slope_ref[place] = (0.5 * slope_twice(u, s, t)).astype(jnp.bfloat16)
 
     edge_stage(pick_ref, comb_ref, work_ref, sum_edges)
     node_stage(summed_ref, node_ref, work_ref, node_values)
@@ -120,7 +123,7 @@
         pred_ref[m, : prior_ref.shape[0]] = prior_ref[...] + dot_nt(output_ref[...], out_ref[m])
 
 
-def edge_slope_kernel(comb_ref, pick_ref, grid_ref, edge_ref, both_ref, work_ref):
+def edge_slope_kernel(comb_ref, pick_ref, grid_ref, edge_ref, both_ref, *work_ref):
     for m in range(comb_ref.shape[0]):
         both_ref[m, :TABLE] = comb_ref[m]
         both_ref[m, TABLE:] = grid_ref[...]
@@ -132,15 +135,6 @@
                 edge_ref[m, k, r : r + PART, h + c : h + c + LANES] = value * 0.5
 
     edge_stage(pick_ref, both_ref, work_ref, edge_slopes)
-
-
-def node_slope_kernel(summed_ref, node_ref, point_ref, work_ref):
-    def node_slopes(buffer, m, h):
-        for r, c in parts(CHUNK):
-            value = 0.5 * slope_twice(buffer[r : r + PART, c : c + LANES])
-            point_ref[m, r : r + PART, h + c : h + c + LANES] = value.astype(jnp.bfloat16)
-
-    node_stage(summed_ref, node_ref, work_ref, node_slopes)
 
 
 def loss_kernel(
@@ -152,41 +146,45 @@
     width = output_ref.shape[1]
     everyone = 4 * members
     fairness = 1.0 - (1.0 - ALPHA) / everyone
-    weight = variable_ref[...] * area_ref[...]
-    truth = truth_ref[...]
     edge = SOFT_EDGE * SOFT_EDGE
-    terms = jnp.zeros((variables, CHUNK), jnp.float32)
 
     @pl.when(pl.program_id(0) == 0)
     def _():
         sum_ref[...] = jnp.zeros_like(sum_ref)
         tall_ref[...] = jnp.zeros_like(tall_ref)
 
+    everyones = [ref.at[k] for ref in (own_ref, core_ref, chip_ref, far_ref) for k in range(members)]
+    total = jnp.zeros((1, CHUNK), jnp.float32)
+    for first in range(0, variables, PART):
+        rows = slice(first, min(first + PART, variables))
+        weight = variable_ref[rows] * area_ref[...]
+        truth = truth_ref[rows]
+        terms = jnp.zeros_like(truth)
+        for j in range(members):
+            own = own_ref[j, rows]
+            pair_abs = jnp.full_like(truth, -everyone * SOFT_EDGE)
+            pair_sign = jnp.zeros_like(truth)
+            for other in everyones:
+                d = own - other[rows]
+                square = d * d + edge
+                r = lax.rsqrt(square)
+                pair_abs = pair_abs + square * r
+                pair_sign = pair_sign + d * r
+            d = own - truth
+            square = d * d + edge
+            r = lax.rsqrt(square)
+            terms = terms + (
+                (square * r - SOFT_EDGE) / everyone
+                - fairness / (2.0 * everyone * (everyone - 1)) * pair_abs
+            )
+            tall_ref[j, rows] = weight * (d * r - fairness / (everyone - 1) * pair_sign)
+        total = total + jnp.sum(weight * terms, axis=0, keepdims=True)
+    sum_ref[...] += total
     grads = []
     for j in range(members):
-        own = own_ref[j, :variables]
-        pair_abs = jnp.full((variables, CHUNK), -everyone * SOFT_EDGE, jnp.float32)
-        pair_sign = jnp.zeros((variables, CHUNK), jnp.float32)
-        for other in [ref[k, :variables] for ref in (own_ref, core_ref, chip_ref, far_ref) for k in range(members)]:
-            d = own - other
-            square = d * d + edge
-            r = lax.rsqrt(square)
-            pair_abs = pair_abs + square * r
-            pair_sign = pair_sign + d * r
-        d = own - truth
-        square = d * d + edge
-        r = lax.rsqrt(square)
-        terms = terms + weight * (
-            (square * r - SOFT_EDGE) / everyone
-            - fairness / (2.0 * everyone * (everyone - 1)) * pair_abs
-        )
-        gradient = weight * (d * r - fairness / (everyone - 1) * pair_sign)
-        tall_ref[:variables] = gradient
-        tall = tall_ref[...].T.astype(jnp.bfloat16)
+        tall = tall_ref[j].T.astype(jnp.bfloat16)
         grad_ref[j] = tall
         grads.append(tall)
-
-    sum_ref[...] += jnp.sum(terms, axis=0, keepdims=True)
 
     @pl.when(pl.program_id(0) == pl.num_programs(0) - 1)
     def _():
@@ -249,9 +247,9 @@
     split_rows(term, core_ref[0], mine_ref, other_ref, slice(0, term.shape[1]))
 
 
-def params():
+def params(mebibytes):
     return pltpu.CompilerParams(
-        dimension_semantics=("arbitrary",), vmem_limit_bytes=VMEM_LIMIT
+        dimension_semantics=("arbitrary",), vmem_limit_bytes=mebibytes * 1024 * 1024
     )
 
 
@@ -338,7 +336,7 @@
     tiled_rows = -(-variables // 8) * 8
     own_block = pl.BlockSpec((members, tiled_rows, CHUNK), lambda c: (0, 0, c))
     per_point = jax.ShapeDtypeStruct((members, points, width), jnp.bfloat16)
-    pred, summed, node_out, comb = pl.pallas_call(
+    pred, summed, node_out, node_slope, comb = pl.pallas_call(
         forward_kernel_with_table,
         grid=(chunks,),
         in_specs=[
@@ -346,18 +344,19 @@
             whole(node_weight), whole(output_rows), by_variable,
         ],
         out_specs=[
-            own_block, member_rows, member_rows,
+            own_block, member_rows, member_rows, member_rows,
             pl.BlockSpec((members, TABLE, width), lambda c: (0, 0, 0)),
         ],
         out_shape=[
             jax.ShapeDtypeStruct((members, tiled_rows, points), jnp.float32), per_point, per_point,
-            jax.ShapeDtypeStruct((members, TABLE, width), jnp.bfloat16),
+            per_point, jax.ShapeDtypeStruct((members, TABLE, width), jnp.bfloat16),
         ],
         scratch_shapes=[
             pltpu.VMEM((members, TABLE + CHUNK, width), jnp.bfloat16),
-            pltpu.VMEM((2, DEGREE * CHUNK, TILE), jnp.float32),
-        ],
-        compiler_params=params(),
+            pltpu.VMEM((DEGREE * CHUNK, TILE), jnp.float32),
+            pltpu.VMEM((DEGREE * CHUNK, TILE), jnp.float32),
+        ],
+        compiler_params=params(30),
         name="forward",
     )(source_rows, project_weight, pick, grid_state, node_weight, output_rows, prior_state)
 
@@ -375,26 +374,15 @@
         out_shape=jax.ShapeDtypeStruct((members, DEGREE, points, width), jnp.bfloat16),
         scratch_shapes=[
             pltpu.VMEM((members, TABLE + CHUNK, width), jnp.bfloat16),
-            pltpu.VMEM((2, DEGREE * CHUNK, TILE), jnp.bfloat16),
-        ],
-        compiler_params=params(),
+            pltpu.VMEM((DEGREE * CHUNK, TILE), jnp.bfloat16),
+            pltpu.VMEM((DEGREE * CHUNK, TILE), jnp.bfloat16),
+        ],
+        compiler_params=params(24),
         cost_estimate=cost(members * DEGREE * points * width, 2 * TABLE, 20),
         name="edge_slopes",
     )(comb, pick, grid_state)
     chip_pred, edge_slope = lax.optimization_barrier((chip_pred, edge_slope))
     far_pred = swap(chip_pred, 1)
-    node_slope = pl.pallas_call(
-        node_slope_kernel,
-        grid=(chunks,),
-        in_specs=[member_rows, whole(node_weight)],
-        out_specs=member_rows,
-        out_shape=per_point,
-        scratch_shapes=[pltpu.VMEM((2, DEGREE * CHUNK, TILE), jnp.float32)],
-        compiler_params=params(),
-        cost_estimate=cost(members * points * width, width, 20),
-        name="node_slopes",
-    )(summed, node_weight)
-
     grad_rows, node_pre_grad, loss_row = pl.pallas_call(
         loss_kernel,
         grid=(chunks,),
@@ -413,9 +401,9 @@
             jax.ShapeDtypeStruct((1, CHUNK), jnp.float32),
         ],
         scratch_shapes=[
-            pltpu.VMEM((TABLE, CHUNK), jnp.float32), pltpu.VMEM((1, CHUNK), jnp.float32),
-        ],
-        compiler_params=params(),
+            pltpu.VMEM((members, TABLE, CHUNK), jnp.float32), pltpu.VMEM((1, CHUNK), jnp.float32),
+        ],
+        compiler_params=params(16),
         name="loss",
     )(core[None], pred, core_pred, chip_pred, far_pred, target, area_weight[None, :], scale, node_slope, output_padded)
 
@@ -425,9 +413,11 @@
     def add_partner(mine, other):
         return (mine.astype(jnp.float32) + swap(other, 1).astype(jnp.float32)).astype(jnp.bfloat16)
 
-    def reduce_rows(half):
+    def sum_space(half):
         moved = lax.all_to_all(half, "space", 0, 0, tiled=True)
-        part = jnp.sum(moved.astype(jnp.float32), axis=0)
+        return jnp.sum(moved.astype(jnp.float32), axis=0)
+
+    def sum_members(part):
         mine = part + swap(part, 2)
         other = swap(part, 1) + swap(part, 3)
         return jnp.where(
@@ -450,7 +440,7 @@
         ],
         out_specs=[terms_block, terms_block],
         out_shape=[terms_shape, terms_shape],
-        compiler_params=params(),
+        compiler_params=params(32),
         cost_estimate=cost(width * width, members * points, 1),
         name="node_terms",
     )(core[None], summed, node_out, node_pre_grad, grad_rows, loss_row)
@@ -480,7 +470,7 @@
                 jax.ShapeDtypeStruct((members, table_rows, tiles * TILE), jnp.float32),
                 shape, shape,
             ],
-            compiler_params=params(),
+            compiler_params=params(40),
             cost_estimate=cost(members * points * width // halves, 4 * width, 8),
             name="table",
         )(core[None], pre_grad, node_weight, edge_slope, place, source_columns)
@@ -490,7 +480,7 @@
     second_input, node_half, first_mine = lax.optimization_barrier(
         (node_pre_grad, node_half, first_mine)
     )
-    node_sums = reduce_rows(node_half)
+    node_part = sum_space(node_half)
     first_half = add_partner(first_mine, first_other)
     second_grad, second_mine, second_other = table_half(tiles, second_input)
     second_half = add_partner(second_mine, second_other)
@@ -503,10 +493,10 @@
         table_grad[:, own_nodes + send_rows :].astype(jnp.bfloat16), "space", forward
     )
     project_half = jnp.concatenate([first_half, second_half], axis=2)
-    project_half, left_back, right_back = lax.optimization_barrier(
-        (project_half, left_back, right_back)
-    )
-    project_sum = reduce_rows(project_half)
+    project_half, node_part, left_back, right_back = lax.optimization_barrier(
+        (project_half, node_part, left_back, right_back)
+    )
+    sums = sum_members(jnp.concatenate([sum_space(project_half), node_part], axis=1))
     projected_grad = (
         table_grad[:, :own_nodes]
         + jnp.einsum(
@@ -519,19 +509,20 @@
     grad_hidden = jnp.einsum(
         "mnk,hk->mnh", projected_grad, project_weight, preferred_element_type=jnp.float32
     ).astype(jnp.bfloat16)
-    loss_at = width + variables
+    output_at = 2 * width
+    loss_at = output_at + variables
     return (
         grad_hidden,
-        project_sum / total_points,
-        node_sums[:, :width] / total_points,
-        node_sums[:, width:loss_at] / total_points,
-        jnp.sum(node_sums[0, loss_at:]) / (total_points * variables),
+        sums[:, :width] / total_points,
+        sums[:, width:output_at] / total_points,
+        sums[:, output_at:loss_at] / total_points,
+        jnp.sum(sums[0, loss_at:]) / (total_points * variables),
     )
 
 
 def forward_kernel_with_table(*refs):
-    inputs, (pred_ref, summed_ref, out_ref, table_ref, comb_ref, work_ref) = refs[:7], refs[7:]
-    forward_kernel(*inputs, pred_ref, summed_ref, out_ref, comb_ref, work_ref)
+    table_ref, comb_ref = refs[11:13]
+    forward_kernel(*refs[:11], *refs[12:])
 
     @pl.when(pl.program_id(0) == 0)
     def _():

time: 191 us -> 202 us (1.058)
  local copies, waits for them, and re-layouts: 7.63 us -> 32.6 us
  Pallas kernels: 103 us -> 80.1 us
  waiting for transfers between devices: 14.4 us -> 21.5 us
  other arithmetic: 9.83 us -> 12 us
    unnamed x28 -> x66, local copies, waits for them, and re-layouts: 3.63 us -> 30.2 us
    all_to_all x2, waiting for transfers between devices: 0.01 us -> 14 us  [sum_space(): moved = lax.all_to_all(half, 'space', 0, 0, tiled=True)]
    pallas_call x1 -> x0, Pallas kernels: 11.1 us -> none  [shards(): pl.pallas_call(node_slope_kernel, grid=(chunks,), in_specs=[member_rows,...]
    ppermute x12 -> x9, waiting for transfers between devices: 10.9 us -> 5.77 us  [swap(): lax.ppermute(value, 'member', [(i, i ^ flip) for i in range(lax.axis_size...]
    pallas_call x2, Pallas kernels: 25.5 us -> 21 us  [table_half(): pl.pallas_call(table_kernel, grid=(tiles,), in_specs=[smem, whole(pre_gra...]
    ppermute x12 -> x9, starting transfers between devices: 15.1 us -> 12.4 us  [swap(): lax.ppermute(value, 'member', [(i, i ^ flip) for i in range(lax.axis_size...]
    pallas_call x1, Pallas kernels: 10.5 us -> 8.05 us  [shards(): pl.pallas_call(node_term_kernel, grid=(width // TILE,), in_specs=[smem, s...]
    pallas_call x1, Pallas kernels: 21.8 us -> 19.4 us  [shards(): pl.pallas_call(edge_slope_kernel, grid=(chunks,), in_specs=[whole(comb),...]
  transfers between devices with their start and end apart: 18 -> 15, of which waited for: 6 -> 5; matrix products, arithmetic and copies ran while one was open for 11% -> 10% of each run, Pallas kernels for 31% -> 20%
where the time goes in v4:
time: 202 us; the launch traced here: 201 us
  Pallas kernels  80.1 us (40%)
  starting transfers between devices  43 us (21%)
  local copies, waits for them, and re-layouts  32.6 us (16%)
  waiting for transfers between devices  21.5 us (11%)
  other arithmetic  12 us (6%)
  matrix products  7.99 us (4%)
  between operations  3.53 us (2%)
    unnamed x66, local copies, waits for them, and re-layouts  30.2 us
    pallas_call x1, Pallas kernels, shards(): pl.pallas_call(forward_kernel_with_table, grid=(chunks,), in_specs=[whole...  23.4 us
    pallas_call x2, Pallas kernels, table_half(): pl.pallas_call(table_kernel, grid=(tiles,), in_specs=[smem, whole(pre_gra...  21 us
    all_to_all x2, starting transfers between devices, sum_space(): moved = lax.all_to_all(half, 'space', 0, 0, tiled=True)  19.5 us
    pallas_call x1, Pallas kernels, shards(): pl.pallas_call(edge_slope_kernel, grid=(chunks,), in_specs=[whole(comb),...  19.4 us
    all_to_all x2, waiting for transfers between devices, sum_space(): moved = lax.all_to_all(half, 'space', 0, 0, tiled=True)  14 us
    ppermute x9, starting transfers between devices, swap(): lax.ppermute(value, 'member', [(i, i ^ flip) for i in range(lax.axis_size...  12.4 us
    pallas_call x1, Pallas kernels, shards(): pl.pallas_call(loss_kernel, grid=(chunks,), in_specs=[pl.BlockSpec(memory...  8.27 us
  transfers between devices with their start and end apart: 15, of which 5 were waited for; matrix products, arithmetic and copies ran while one was open for 10% of the time, Pallas kernels for 20%

profile of v4, /device:TPU:1, one launch (start us, length us, event | category | flops | bytes accessed | tf_op | source)
XLA Modules:
  0.0 200.8 jit_solution(8635001323170298831)
XLA Ops:
  0.6 1.4 fusion.12
  2.1 4.5 %collective-permute-start = (bf16[4,16,1024]{2,1,0:T(8,128)(2,1)S(1)}, bf16[4,16,1024]{2,1,0:T(8,128)(2,1)S(1)}, u32[]{:S(2)}, u32[]{:S(2)}) collective-permute-start(bf16[4,16,1024]{2,1,0:T(8,128)(2,1)S(1)} %get-tuple-element.60), channel_id=1, source_target_pairs={{0,1},{1,2},{2,3},{3,4},{4,5},{5,6},{6,7},{7,8},{8,9},{9,10},{10,1... | collective-permute-start | bytes 393224 | tf_op jit(solution)/shard_map/ppermute | solution.py:299
  6.6 1.3 collective-permute-start.1
  8.6 0.7 fusion.23
  9.3 0.8 convert_add_fusion
  10.0 0.8 add_select_fusion
  10.9 0.1 iota_compare_fusion.6
  11.0 0.5 fusion.5.refs_2_.pick_ref
  11.6 0.7 collective-permute-done.1
  12.4 1.6 copy-done.4
  14.0 1.6 copy-done.6
  15.6 23.4 %forward.1 = (f32[4,104,512]{2,1,0:T(8,128)S(1)}, bf16[4,512,1024]{2,1,0:T(8,128)(2,1)S(1)}, bf16[4,512,1024]{2,1,0:T(8,128)(2,1)S(1)}, bf16[4,512,1024]{2,1,0:T(8,128)(2,1)S(1)}, bf16[4,128,1024]{2,1,0:T(8,128)(2,1)S(1)}) custom-call(bf16[4,96,1024]{2,1,0:T(8,128)(2,1)S(1)} %constant_dynamic-update-slice_fusion.refs_0_, bf16[1024,1024]{1,0:T(8,128)(2,1)S(1)} %copy-done.6, ...), custom_call_target="tpu_custom_call" | custom-call | tf_op jit(solution)/shard_map/forward/pallas_call | solution.py:339
  39.0 2.0 %copy-done.18 = bf16[4,512,1024]{2,1,0:T(8,128)(2,1)} copy-done((bf16[4,512,1024]{2,1,0:T(8,128)(2,1)}, bf16[4,512,1024]{2,1,0:T(8,128)(2,1)S(1)}, u32[]{:S(2)}) %copy-start.18) | copy-done | bytes 4194328
  41.0 2.1 %copy-done.20 = bf16[4,512,1024]{2,1,0:T(8,128)(2,1)} copy-done((bf16[4,512,1024]{2,1,0:T(8,128)(2,1)}, bf16[4,512,1024]{2,1,0:T(8,128)(2,1)S(1)}, u32[]{:S(2)}) %copy-start.20) | copy-done | bytes 4194328
  43.0 3.3 %collective-permute-start.3 = (f32[4,104,512]{2,1,0:T(8,128)S(1)}, f32[4,104,512]{2,1,0:T(8,128)S(1)}, u32[]{:S(2)}, u32[]{:S(2)}) collective-permute-start(f32[4,104,512]{2,1,0:T(8,128)S(1)} %get-tuple-element.30.own_ref), channel_id=1, source_target_pairs={{0,64},{32,96},{64,0},{96,32},{1,65},{33,97},{65,1},{97,33},{2,66}... | collective-permute-start | bytes 2555912 | tf_op jit(solution)/shard_map/ppermute | solution.py:364
  46.3 2.4 %collective-permute-start.2 = (f32[4,104,512]{2,1,0:T(8,128)S(1)}, f32[4,104,512]{2,1,0:T(8,128)}, u32[]{:S(2)}, u32[]{:S(2)}) collective-permute-start(f32[4,104,512]{2,1,0:T(8,128)S(1)} %get-tuple-element.30.own_ref), channel_id=1, source_target_pairs={{0,32},{32,0},{64,96},{96,64},{1,33},{33,1},{65,97},{97,65},{2,34}... | collective-permute-start | bytes 2555912 | tf_op jit(solution)/shard_map/ppermute | solution.py:364
  48.7 19.4 %edge_slopes.1.slope_ref = bf16[4,4,512,1024]{3,2,1,0:T(8,128)(2,1)S(1)} custom-call(bf16[4,128,1024]{2,1,0:T(8,128)(2,1)S(1)} %get-tuple-element.31.comb_ref, bf16[4,512,256]{2,1,0:T(8,128)(2,1)S(1)} %fusion.5.refs_2_.pick_ref, bf16[512,1024]{1,0:T(8,128)(2,1)S(1)} %copy-done.1), custom_call_target="tpu_custom_call" | custom-call | flops 4462739456 | bytes 16777216 | tf_op jit(solution)/shard_map/edge_slopes/pallas_call | solution.py:369
  68.1 5.7 %copy-done = bf16[4,4,512,1024]{3,2,1,0:T(8,128)(2,1)} copy-done((bf16[4,4,512,1024]{3,2,1,0:T(8,128)(2,1)}, bf16[4,4,512,1024]{3,2,1,0:T(8,128)(2,1)S(1)}, u32[]{:S(2)}) %copy-start) | copy-done | bytes 16777240
  73.9 1.0 pad.9.output_ref
  74.9 0.1 copy.20.variable_ref
  75.0 1.4 collective-permute-done.4.far_ref
  76.4 2.2 %copy-done.3 = bf16[4,512,1024]{2,1,0:T(8,128)(2,1)S(1)} copy-done((bf16[4,512,1024]{2,1,0:T(8,128)(2,1)S(1)}, bf16[4,512,1024]{2,1,0:T(8,128)(2,1)}, u32[]{:S(2)}) %copy-start.3) | copy-done | bytes 4194328
  78.6 0.9 copy-done.16
  79.5 8.3 %loss.1 = (bf16[4,512,128]{2,1,0:T(8,128)(2,1)S(1)}, bf16[4,512,1024]{2,1,0:T(8,128)(2,1)S(1)}, f32[1,128]{1,0:T(1,128)S(1)}) custom-call(s32[1]{0:T(128)} %bitcast.core_index_ref.core_ref, f32[4,104,512]{2,1,0:T(8,128)S(1)} %get-tuple-element.30.own_ref, f32[4,104,512]{2,1,0:T(8,128)} %collective-permute-done.2.core_ref, ...), custom_call_target="tpu_custom_call" | custom-call | tf_op jit(solution)/shard_map/loss/pallas_call | solution.py:386
  87.8 3.7 %copy-done.21 = bf16[4,512,1024]{2,1,0:T(8,128)(2,1)S(1)} copy-done((bf16[4,512,1024]{2,1,0:T(8,128)(2,1)S(1)}, bf16[4,512,1024]{2,1,0:T(8,128)(2,1)}, u32[]{:S(2)}) %copy-start.21) | copy-done | bytes 4194328
  91.5 8.0 %node_terms.1 = (bf16[32,16,1152]{2,1,0:T(8,128)(2,1)S(1)}, bf16[32,16,1152]{2,1,0:T(8,128)(2,1)}) custom-call(s32[1]{0:T(128)} %bitcast.core_index_ref.core_ref, bf16[4,512,1024]{2,1,0:T(8,128)(2,1)S(1)} %copy-done.19, bf16[4,512,1024]{2,1,0:T(8,128)(2,1)S(1)} %copy-done.21, bf16[4,512,1024]{2,1,0:T(8,128)(2,1)S(1)} %get-tuple-element.44.pre_ref, ...), custom_call_target="tpu_custom_call" | custom-call | flops 4296015872 | bytes 2097152 | tf_op jit(solution)/shard_map/node_terms/pallas_call | solution.py:434
  99.6 1.1 copy-done.8
  100.7 0.1 collective-permute-start.5
  100.8 0.9 fusion.14.place_ref
  101.7 1.2 copy.21
  102.9 1.1 copy-done.11
  104.0 1.0 copy-done.13
  105.0 2.2 %copy-done.23 = bf16[4,512,1024]{2,1,0:T(8,128)(2,1)S(1)} copy-done((bf16[4,512,1024]{2,1,0:T(8,128)(2,1)S(1)}, bf16[4,512,1024]{2,1,0:T(8,128)(2,1)}, u32[]{:S(2)}) %copy-start.23) | copy-done | bytes 4194328
  107.2 10.8 %table.2 = (f32[4,96,512]{2,1,0:T(8,128)S(1)}, bf16[32,16,512]{2,1,0:T(8,128)(2,1)S(1)}, bf16[32,16,512]{2,1,0:T(8,128)(2,1)}) custom-call(s32[1]{0:T(128)} %bitcast.core_index_ref.core_ref, bf16[4,512,1024]{2,1,0:T(8,128)(2,1)S(1)} %copy-done.23, bf16[1024,1024]{1,0:T(8,128)(2,1)S(1)} %copy-done.5, bf16[4,4,512,1024]{3,2,1,0:T(8,128)(2,1)} %copy-done, ...), custom_call_target="tpu_custom_call" | custom-call | flops 8598323200 | bytes 2097152 | tf_op jit(solution)/shard_map/table/pallas_call | solution.py:455
  118.0 0.4 collective-permute-start.6
  118.4 1.0 constant_dynamic-update-slice_fusion.4
  119.4 2.7 %add_convert_fusion = bf16[32,16,1152]{2,1,0:T(8,128)(2,1)} fusion(bf16[32,16,1152]{2,1,0:T(8,128)(2,1)} %collective-permute-done.5, bf16[32,16,1152]{2,1,0:T(8,128)(2,1)S(1)} %copy-done.9), kind=kLoop, calls=%fused_computation.3 | loop fusion | flops 2359296 | bytes 3538944 | tf_op jit(solution)/shard_map/convert_element_type | solution.py:414
  122.1 9.8 %all-to-all-start = ((bf16[32,16,1152]{2,1,0:T(8,128)(2,1)}), bf16[32,16,1152]{2,1,0:T(8,128)(2,1)}, u32[]{:S(2)}, u32[]{:S(2)}) async-start(bf16[32,16,1152]{2,1,0:T(8,128)(2,1)} %add_convert_fusion), calls=%async_computation | async-start | bytes 2359296 | tf_op jit(solution)/shard_map/all_to_all | solution.py:417
  131.9 1.0 copy-done.14
  132.9 2.2 %copy-done.24 = bf16[4,512,1024]{2,1,0:T(8,128)(2,1)S(1)} copy-done((bf16[4,512,1024]{2,1,0:T(8,128)(2,1)S(1)}, bf16[4,512,1024]{2,1,0:T(8,128)(2,1)}, u32[]{:S(2)}) %copy-start.24) | copy-done | bytes 4194328
  135.1 10.3 %table.3 = (f32[4,96,512]{2,1,0:T(8,128)S(1)}, bf16[32,16,512]{2,1,0:T(8,128)(2,1)S(1)}, bf16[32,16,512]{2,1,0:T(8,128)(2,1)S(1)}) custom-call(s32[1]{0:T(128)} %bitcast.core_index_ref.core_ref, bf16[4,512,1024]{2,1,0:T(8,128)(2,1)S(1)} %copy-done.24, bf16[1024,1024]{1,0:T(8,128)(2,1)S(1)} %copy-done.5, bf16[4,4,512,1024]{3,2,1,0:T(8,128)(2,1)} %copy-done, ...), custom_call_target="tpu_custom_call" | custom-call | flops 8598323200 | bytes 2097152 | tf_op jit(solution)/shard_map/table/pallas_call | solution.py:455
  145.4 0.9 collective-permute-start.7
  146.4 0.1 convert.4
  146.5 1.3 collective-permute-start.8
  147.8 4.0 %collective-permute-start.9 = (bf16[4,16,1024]{2,1,0:T(8,128)(2,1)S(1)}, bf16[4,16,1024]{2,1,0:T(8,128)(2,1)S(1)}, u32[]{:S(2)}, u32[]{:S(2)}) collective-permute-start(bf16[4,16,1024]{2,1,0:T(8,128)(2,1)S(1)} %get-tuple-element.55), channel_id=1, source_target_pairs={{0,1},{1,2},{2,3},{3,4},{4,5},{5,6},{6,7},{7,8},{8,9},{9,10},{10,1... | collective-permute-start | bytes 393224 | tf_op jit(solution)/shard_map/ppermute | solution.py:492
  151.8 1.2 add_convert_fusion.2
  153.1 0.2 add_convert_fusion.1
  153.3 1.1 pad_maximum_fusion
  154.4 1.4 convert_reduce_fusion
  155.8 1.0 collective-permute-done.9
  156.8 0.7 copy-done.30
  157.5 9.7 %all-to-all-start.1 = ((bf16[32,16,1024]{2,1,0:T(8,128)(2,1)}), bf16[32,16,1024]{2,1,0:T(8,128)(2,1)S(1)}, u32[]{:S(2)}, u32[]{:S(2)}) async-start(bf16[32,16,1024]{2,1,0:T(8,128)(2,1)} %pad_maximum_fusion), calls=%async_computation.1 | async-start | bytes 2097152 | tf_op jit(solution)/shard_map/all_to_all | solution.py:417
  167.2 0.1 iota_compare_fusion.8
  167.3 2.7 %fusion.7 = f32[4,64,1024]{2,1,0:T(8,128)} fusion(bf16[4,16,1024]{2,1,0:T(8,128)(2,1)S(1)} %collective-permute-done.8, f32[4,96,1024]{2,1,0:T(8,128)} %copy-done.26, pred[2,16,64]{2,1,0:T(8,128)(4,1)S(1)} %iota_compare_fusion.8), kind=kOutput, calls=%fused_computation.14 | convolution fusion | flops 8650752 | bytes 2230272 | tf_op jit(solution)/shard_map/sn,msh->mnh/dot_general | solution.py:502
  170.0 14.0 %all-to-all-done.1 = bf16[32,16,1024]{2,1,0:T(8,128)(2,1)S(1)} async-done(((bf16[32,16,1024]{2,1,0:T(8,128)(2,1)}), bf16[32,16,1024]{2,1,0:T(8,128)(2,1)S(1)}, u32[]{:S(2)}, u32[]{:S(2)}) %all-to-all-start.1) | async-done | bytes 1048608 | tf_op jit(solution)/shard_map/all_to_all | solution.py:417
  184.0 0.2 convert_reduce_fusion.1
  184.2 0.7 collective-permute-start.10
  184.9 3.1 %fusion.8 = bf16[4,64,1024]{2,1,0:T(8,128)(2,1)} fusion(bf16[1024,1024]{1,0:T(8,128)(2,1)S(1)} %copy-done.7, f32[4,64,1024]{2,1,0:T(8,128)} %fusion.7, bf16[4,16,1024]{2,1,0:T(8,128)(2,1)} %copy-done.30, pred[2,16,64]{2,1,0:T(8,128)(4,1)S(1)} %iota_compare_fusion.8), kind=kOutput, calls=%fused_computation.15 | convolution fusion | flops 546045952 | bytes 3803136 | tf_op jit(solution)/shard_map/mnk,hk->mnh/dot_general | solution.py:509
  187.9 2.2 %collective-permute-start.11 = (f32[16,2176]{1,0:T(8,128)S(1)}, f32[16,2176]{1,0:T(8,128)S(1)}, u32[]{:S(2)}, u32[]{:S(2)}) collective-permute-start(f32[16,2176]{1,0:T(8,128)S(1)} %pad_maximum_fusion.1), channel_id=1, source_target_pairs={{0,32},{32,0},{64,96},{96,64},{1,33},{33,1},{65,97},{97,65},{2,34}... | collective-permute-start | bytes 417800 | tf_op jit(solution)/shard_map/ppermute | solution.py:364
  190.2 2.4 %collective-permute-start.12 = (f32[16,2176]{1,0:T(8,128)S(1)}, f32[16,2176]{1,0:T(8,128)S(1)}, u32[]{:S(2)}, u32[]{:S(2)}) collective-permute-start(f32[16,2176]{1,0:T(8,128)S(1)} %pad_maximum_fusion.1), channel_id=1, source_target_pairs={{0,96},{32,64},{64,32},{96,0},{1,97},{33,65},{65,33},{97,1},{2,98}... | collective-permute-start | bytes 417800 | tf_op jit(solution)/shard_map/ppermute | solution.py:364
  192.6 4.4 %collective-permute-done.12 = f32[16,2176]{1,0:T(8,128)S(1)} collective-permute-done((f32[16,2176]{1,0:T(8,128)S(1)}, f32[16,2176]{1,0:T(8,128)S(1)}, u32[]{:S(2)}, u32[]{:S(2)}) %collective-permute-start.12) | collective-permute-done | bytes 139296 | tf_op jit(solution)/shard_map/ppermute | solution.py:364
  197.0 0.7 slice_multiply_fusion
  197.7 0.6 slice_multiply_fusion.2
  198.3 0.7 slice_reduce_fusion
  (72 shorter events, 0.4 us)
Async XLA Ops:
  0.6 10.9 %copy-start.27 = (bf16[4,64,1024]{2,1,0:T(8,128)(2,1)S(1)}, bf16[4,64,1024]{2,1,0:T(8,128)(2,1)}, u32[]{:S(2)}) copy-start(bf16[4,64,1024]{2,1,0:T(8,128)(2,1)} %param.13) | copy-start | bytes 1572868
  2.1 10.3 %copy-start.1 = (bf16[512,1024]{1,0:T(8,128)(2,1)S(1)}, bf16[512,1024]{1,0:T(8,128)(2,1)}, u32[]{:S(2)}) copy-start(bf16[512,1024]{1,0:T(8,128)(2,1)} %grid_ref.1) | copy-start | bytes 3145732
  2.1 10.3 %copy-start.10 = (bf16[1024,100]{0,1:T(8,128)(2,1)S(1)}, bf16[1024,100]{0,1:T(8,128)(2,1)}, u32[]{:S(2)}) copy-start(bf16[1024,100]{0,1:T(8,128)(2,1)} %param.17) | copy-start | bytes 614404
  2.1 10.3 %copy-start.15 = (f32[100,512]{1,0:T(8,128)S(1)}, f32[100,512]{1,0:T(8,128)}, u32[]{:S(2)}) copy-start(f32[100,512]{1,0:T(8,128)} %refs_6_.1) | copy-start | bytes 614404
  2.1 9.5 %collective-permute-start = (bf16[4,16,1024]{2,1,0:T(8,128)(2,1)S(1)}, bf16[4,16,1024]{2,1,0:T(8,128)(2,1)S(1)}, u32[]{:S(2)}, u32[]{:S(2)}) collective-permute-start(bf16[4,16,1024]{2,1,0:T(8,128)(2,1)S(1)} %get-tuple-element.60), channel_id=1, source_target_pairs={{0,1},{1,2},{2,3},{3,4},{4,5},{5,6},{6,7},{7,8},{8,9},{9,10},{10,1... | collective-permute-start | bytes 393224 | tf_op jit(solution)/shard_map/ppermute | solution.py:299
  6.6 5.7 %collective-permute-start.1 = (bf16[4,16,1024]{2,1,0:T(8,128)(2,1)S(1)}, bf16[4,16,1024]{2,1,0:T(8,128)(2,1)S(1)}, u32[]{:S(2)}, u32[]{:S(2)}) collective-permute-start(bf16[4,16,1024]{2,1,0:T(8,128)(2,1)S(1)} %get-tuple-element.59), channel_id=1, source_target_pairs={{1,0},{2,1},{3,2},{4,3},{5,4},{6,5},{7,6},{8,7},{9,8},{10,9},{11,1... | collective-permute-start | bytes 393224 | tf_op jit(solution)/shard_map/ppermute | solution.py:300
  12.4 1.6 copy-start.4
  14.0 1.6 copy-start.6
  38.9 2.0 %copy-start.18 = (bf16[4,512,1024]{2,1,0:T(8,128)(2,1)}, bf16[4,512,1024]{2,1,0:T(8,128)(2,1)S(1)}, u32[]{:S(2)}) copy-start(bf16[4,512,1024]{2,1,0:T(8,128)(2,1)S(1)} %get-tuple-element.37.summed_ref) | copy-start | bytes 12582916
  41.0 2.1 %copy-start.20 = (bf16[4,512,1024]{2,1,0:T(8,128)(2,1)}, bf16[4,512,1024]{2,1,0:T(8,128)(2,1)S(1)}, u32[]{:S(2)}) copy-start(bf16[4,512,1024]{2,1,0:T(8,128)(2,1)S(1)} %get-tuple-element.38.out_ref) | copy-start | bytes 12582916
  43.0 25.1 %copy-start.2 = (bf16[4,512,1024]{2,1,0:T(8,128)(2,1)}, bf16[4,512,1024]{2,1,0:T(8,128)(2,1)S(1)}, u32[]{:S(2)}) copy-start(bf16[4,512,1024]{2,1,0:T(8,128)(2,1)S(1)} %get-tuple-element.33.slope_ref) | copy-start | bytes 12582916
  43.0 30.9 %collective-permute-start.3 = (f32[4,104,512]{2,1,0:T(8,128)S(1)}, f32[4,104,512]{2,1,0:T(8,128)S(1)}, u32[]{:S(2)}, u32[]{:S(2)}) collective-permute-start(f32[4,104,512]{2,1,0:T(8,128)S(1)} %get-tuple-element.30.own_ref), channel_id=1, source_target_pairs={{0,64},{32,96},{64,0},{96,32},{1,65},{33,97},{65,1},{97,33},{2,66}... | collective-permute-start | bytes 2555912 | tf_op jit(solution)/shard_map/ppermute | solution.py:364
  46.3 28.7 %collective-permute-start.2 = (f32[4,104,512]{2,1,0:T(8,128)S(1)}, f32[4,104,512]{2,1,0:T(8,128)}, u32[]{:S(2)}, u32[]{:S(2)}) collective-permute-start(f32[4,104,512]{2,1,0:T(8,128)S(1)} %get-tuple-element.30.own_ref), channel_id=1, source_target_pairs={{0,32},{32,0},{64,96},{96,64},{1,33},{33,1},{65,97},{97,65},{2,34}... | collective-permute-start | bytes 2555912 | tf_op jit(solution)/shard_map/ppermute | solution.py:364
  48.7 26.2 %copy-start.29 = (f32[100]{0:T(128)S(1)}, f32[100]{0:T(128)}, u32[]{:S(2)}) copy-start(f32[100]{0:T(128)} %param.21) | copy-start | bytes 1204
  48.7 27.7 %copy-start.17 = (f32[512]{0:T(512)S(1)}, f32[512]{0:T(512)}, u32[]{:S(2)}) copy-start(f32[512]{0:T(512)} %param.20) | copy-start | bytes 6148
  68.1 5.8 %copy-start = (bf16[4,4,512,1024]{3,2,1,0:T(8,128)(2,1)}, bf16[4,4,512,1024]{3,2,1,0:T(8,128)(2,1)S(1)}, u32[]{:S(2)}) copy-start(bf16[4,4,512,1024]{3,2,1,0:T(8,128)(2,1)S(1)} %edge_slopes.1.slope_ref) | copy-start | bytes 50331652
  73.9 2.5 %collective-permute-start.4 = (f32[4,104,512]{2,1,0:T(8,128)S(1)}, f32[4,104,512]{2,1,0:T(8,128)}, u32[]{:S(2)}, u32[]{:S(2)}) collective-permute-start(f32[4,104,512]{2,1,0:T(8,128)S(1)} %collective-permute-done.3.chip_ref), channel_id=1, source_target_pairs={{0,32},{32,0},{64,96},{96,64},{1,33},{33,1},{65,97},{97,65},{2,34}... | collective-permute-start | bytes 2555912 | tf_op jit(solution)/shard_map/ppermute | solution.py:364
  76.4 2.2 %copy-start.3 = (bf16[4,512,1024]{2,1,0:T(8,128)(2,1)S(1)}, bf16[4,512,1024]{2,1,0:T(8,128)(2,1)}, u32[]{:S(2)}) copy-start(bf16[4,512,1024]{2,1,0:T(8,128)(2,1)} %copy-done.2) | copy-start | bytes 12582916
  78.6 0.9 copy-start.16
  79.5 8.3 %copy-start.19 = (bf16[4,512,1024]{2,1,0:T(8,128)(2,1)S(1)}, bf16[4,512,1024]{2,1,0:T(8,128)(2,1)}, u32[]{:S(2)}) copy-start(bf16[4,512,1024]{2,1,0:T(8,128)(2,1)} %copy-done.18) | copy-start | bytes 12582916
  87.8 11.8 %copy-start.22 = (bf16[4,512,1024]{2,1,0:T(8,128)(2,1)}, bf16[4,512,1024]{2,1,0:T(8,128)(2,1)S(1)}, u32[]{:S(2)}) copy-start(bf16[4,512,1024]{2,1,0:T(8,128)(2,1)S(1)} %get-tuple-element.44.pre_ref) | copy-start | bytes 12582916
  87.8 3.7 %copy-start.21 = (bf16[4,512,1024]{2,1,0:T(8,128)(2,1)S(1)}, bf16[4,512,1024]{2,1,0:T(8,128)(2,1)}, u32[]{:S(2)}) copy-start(bf16[4,512,1024]{2,1,0:T(8,128)(2,1)} %copy-done.20) | copy-start | bytes 12582916
  99.6 1.1 copy-start.8
  100.7 2.2 %copy-start.5 = (bf16[1024,1024]{1,0:T(8,128)(2,1)S(1)}, bf16[1024,1024]{1,0:T(8,128)(2,1)}, u32[]{:S(2)}) copy-start(bf16[1024,1024]{1,0:T(8,128)(2,1)} %node_ref.3) | copy-start | bytes 6291460
  100.7 18.7 %collective-permute-start.5 = (bf16[32,16,1152]{2,1,0:T(8,128)(2,1)}, bf16[32,16,1152]{2,1,0:T(8,128)(2,1)}, u32[]{:S(2)}, u32[]{:S(2)}) collective-permute-start(bf16[32,16,1152]{2,1,0:T(8,128)(2,1)} %get-tuple-element.42), channel_id=1, source_target_pairs={{0,32},{32,0},{64,96},{96,64},{1,33},{33,1},{65,97},{97,65},{2,34}... | collective-permute-start | bytes 3538952 | tf_op jit(solution)/shard_map/ppermute | solution.py:364
  102.9 1.1 copy-start.11
  104.0 1.0 copy-start.13
  105.0 2.2 %copy-start.23 = (bf16[4,512,1024]{2,1,0:T(8,128)(2,1)S(1)}, bf16[4,512,1024]{2,1,0:T(8,128)(2,1)}, u32[]{:S(2)}) copy-start(bf16[4,512,1024]{2,1,0:T(8,128)(2,1)} %copy-done.22) | copy-start | bytes 12582916
  118.0 1.4 copy-start.9
  118.0 33.8 %collective-permute-start.6 = (bf16[32,16,512]{2,1,0:T(8,128)(2,1)}, bf16[32,16,512]{2,1,0:T(8,128)(2,1)}, u32[]{:S(2)}, u32[]{:S(2)}) collective-permute-start(bf16[32,16,512]{2,1,0:T(8,128)(2,1)} %get-tuple-element.47), channel_id=1, source_target_pairs={{0,32},{32,0},{64,96},{96,64},{1,33},{33,1},{65,97},{97,65},{2,34}... | collective-permute-start | bytes 1572872 | tf_op jit(solution)/shard_map/ppermute | solution.py:364
  119.4 12.5 %copy-start.12 = (bf16[384,1024]{0,1:T(8,128)(2,1)S(1)}, bf16[384,1024]{0,1:T(8,128)(2,1)}, u32[]{:S(2)}) copy-start(bf16[384,1024]{0,1:T(8,128)(2,1)} %copy.21) | copy-start | bytes 2359300
  122.1 32.3 %all-to-all-start = ((bf16[32,16,1152]{2,1,0:T(8,128)(2,1)}), bf16[32,16,1152]{2,1,0:T(8,128)(2,1)}, u32[]{:S(2)}, u32[]{:S(2)}) async-start(bf16[32,16,1152]{2,1,0:T(8,128)(2,1)} %add_convert_fusion), calls=%async_computation | async-start | bytes 2359296 | tf_op jit(solution)/shard_map/all_to_all | solution.py:417
  131.9 1.0 copy-start.14
  132.9 2.2 %copy-start.24 = (bf16[4,512,1024]{2,1,0:T(8,128)(2,1)S(1)}, bf16[4,512,1024]{2,1,0:T(8,128)(2,1)}, u32[]{:S(2)}) copy-start(bf16[4,512,1024]{2,1,0:T(8,128)(2,1)} %copy-done.22) | copy-start | bytes 12582916
  135.1 11.2 %copy-start.25 = (f32[4,96,1024]{2,1,0:T(8,128)S(1)}, f32[4,96,1024]{2,1,0:T(8,128)}, u32[]{:S(2)}) copy-start(f32[4,96,1024]{2,1,0:T(8,128)} %constant_dynamic-update-slice_fusion.4) | copy-start | bytes 4718596
  145.4 7.7 %collective-permute-start.7 = (bf16[32,16,512]{2,1,0:T(8,128)(2,1)S(1)}, bf16[32,16,512]{2,1,0:T(8,128)(2,1)S(1)}, u32[]{:S(2)}, u32[]{:S(2)}) collective-permute-start(bf16[32,16,512]{2,1,0:T(8,128)(2,1)S(1)} %get-tuple-element.49), channel_id=1, source_target_pairs={{0,32},{32,0},{64,96},{96,64},{1,33},{33,1},{65,97},{97,65},{2,34}... | collective-permute-start | bytes 1572872 | tf_op jit(solution)/shard_map/ppermute | solution.py:364
  146.4 6.9 %copy-start.26 = (f32[4,96,1024]{2,1,0:T(8,128)}, f32[4,96,1024]{2,1,0:T(8,128)S(1)}, u32[]{:S(2)}) copy-start(f32[4,96,1024]{2,1,0:T(8,128)S(1)} %constant_dynamic-update-slice_fusion.3) | copy-start | bytes 4718596
  146.5 9.3 %collective-permute-start.8 = (bf16[4,16,1024]{2,1,0:T(8,128)(2,1)S(1)}, bf16[4,16,1024]{2,1,0:T(8,128)(2,1)S(1)}, u32[]{:S(2)}, u32[]{:S(2)}) collective-permute-start(bf16[4,16,1024]{2,1,0:T(8,128)(2,1)S(1)} %get-tuple-element.56), channel_id=1, source_target_pairs={{1,0},{2,1},{3,2},{4,3},{5,4},{6,5},{7,6},{8,7},{9,8},{10,9},{11,1... | collective-permute-start | bytes 393224 | tf_op jit(solution)/shard_map/ppermute | solution.py:489
  147.8 9.0 %collective-permute-start.9 = (bf16[4,16,1024]{2,1,0:T(8,128)(2,1)S(1)}, bf16[4,16,1024]{2,1,0:T(8,128)(2,1)S(1)}, u32[]{:S(2)}, u32[]{:S(2)}) collective-permute-start(bf16[4,16,1024]{2,1,0:T(8,128)(2,1)S(1)} %get-tuple-element.55), channel_id=1, source_target_pairs={{0,1},{1,2},{2,3},{3,4},{4,5},{5,6},{6,7},{7,8},{8,9},{9,10},{10,1... | collective-permute-start | bytes 393224 | tf_op jit(solution)/shard_map/ppermute | solution.py:492
  154.4 12.8 %copy-start.28 = (s32[2,16]{1,0:T(2,128)S(1)}, s32[2,16]{1,0:T(2,128)}, u32[]{:S(2)}) copy-start(s32[2,16]{1,0:T(2,128)} %param.25) | copy-start | bytes 388
  156.8 0.7 copy-start.30
  157.5 26.6 %all-to-all-start.1 = ((bf16[32,16,1024]{2,1,0:T(8,128)(2,1)}), bf16[32,16,1024]{2,1,0:T(8,128)(2,1)S(1)}, u32[]{:S(2)}, u32[]{:S(2)}) async-start(bf16[32,16,1024]{2,1,0:T(8,128)(2,1)} %pad_maximum_fusion), calls=%async_computation.1 | async-start | bytes 2097152 | tf_op jit(solution)/shard_map/all_to_all | solution.py:417
  167.2 17.7 %copy-start.7 = (bf16[1024,1024]{1,0:T(8,128)(2,1)S(1)}, bf16[1024,1024]{1,0:T(8,128)(2,1)}, u32[]{:S(2)}) copy-start(bf16[1024,1024]{1,0:T(8,128)(2,1)} %refs_1_.1) | copy-start | bytes 6291460
  184.2 8.4 %collective-permute-start.10 = (f32[16,2176]{1,0:T(8,128)S(1)}, f32[16,2176]{1,0:T(8,128)S(1)}, u32[]{:S(2)}, u32[]{:S(2)}) collective-permute-start(f32[16,2176]{1,0:T(8,128)S(1)} %pad_maximum_fusion.1), channel_id=1, source_target_pairs={{0,64},{32,96},{64,0},{96,32},{1,65},{33,97},{65,1},{97,33},{2,66}... | collective-permute-start | bytes 417800 | tf_op jit(solution)/shard_map/ppermute | solution.py:364
  187.9 4.7 %collective-permute-start.11 = (f32[16,2176]{1,0:T(8,128)S(1)}, f32[16,2176]{1,0:T(8,128)S(1)}, u32[]{:S(2)}, u32[]{:S(2)}) collective-permute-start(f32[16,2176]{1,0:T(8,128)S(1)} %pad_maximum_fusion.1), channel_id=1, source_target_pairs={{0,32},{32,0},{64,96},{96,64},{1,33},{33,1},{65,97},{97,65},{2,34}... | collective-permute-start | bytes 417800 | tf_op jit(solution)/shard_map/ppermute | solution.py:364
  190.2 6.8 %collective-permute-start.12 = (f32[16,2176]{1,0:T(8,128)S(1)}, f32[16,2176]{1,0:T(8,128)S(1)}, u32[]{:S(2)}, u32[]{:S(2)}) collective-permute-start(f32[16,2176]{1,0:T(8,128)S(1)} %pad_maximum_fusion.1), channel_id=1, source_target_pairs={{0,96},{32,64},{64,32},{96,0},{1,97},{33,65},{65,33},{97,1},{2,98}... | collective-permute-start | bytes 417800 | tf_op jit(solution)/shard_map/ppermute | solution.py:364

commit v5 on v4

--- a/solution.py
+++ b/solution.py
@@ -17,6 +17,8 @@
 CHUNK = 128
 TILE = 256
 PART = 32
+PIECES = 2
+VMEM_LIMIT = 56 * 1024 * 1024
 LANES = 128
 
 
@@ -49,38 +51,47 @@
     )
 
 
-def parts(rows):
-    return [(r, c) for r in range(0, rows, PART) for c in range(0, TILE, LANES)]
+def blocks(rows, piece):
+    share = rows // PIECES
+    first = piece * share
+    return [(r, c) for r in range(first, first + share, PART) for c in range(0, TILE, LANES)]
 
 
 def staged(tiles, work_ref, matmul, finish):
-    for i, tile in enumerate(tiles):
-        result = matmul(*tile)
-        work_ref[i % 2][: result.shape[0]] = result.astype(work_ref[0].dtype)
-        if i:
-            finish(work_ref[(i - 1) % 2], *tiles[i - 1])
-    finish(work_ref[(len(tiles) - 1) % 2], *tiles[-1])
+    for i in range(len(tiles) + 1):
+        for piece in range(PIECES):
+            if i < len(tiles):
+                result = matmul(*tiles[i], piece)
+                rows = result.shape[0]
+                work_ref[i % 2][piece * rows : (piece + 1) * rows] = result
+            if i:
+                finish(work_ref[(i - 1) % 2], *tiles[i - 1], piece)
 
 
 def edge_stage(pick_ref, comb_ref, work_ref, finish):
     members, _, width = comb_ref.shape
     tiles = [(m, h) for m in range(members) for h in range(0, width, TILE)]
-    staged(
-        tiles, work_ref, lambda m, h: dot(pick_ref[0], comb_ref[m, :, h : h + TILE]), finish
-    )
+    rows = pick_ref.shape[1] // PIECES
+
+    def matmul(m, h, piece):
+        return dot(pick_ref[0, piece * rows : (piece + 1) * rows], comb_ref[m, :, h : h + TILE])
+
+    staged(tiles, work_ref, matmul, finish)
 
 
 def node_stage(summed_ref, node_ref, work_ref, finish):
     members, rows, width = summed_ref.shape
-
-    def matmul(h):
-        return dot(summed_ref[...].reshape(members * rows, width), node_ref[:, h : h + TILE])
-
-    def finish_all(buffer, h):
-        for m in range(members):
-            finish(buffer.at[m * rows : (m + 1) * rows], m, h)
-
-    staged([(h,) for h in range(0, width, TILE)], work_ref, matmul, finish_all)
+    share = members // PIECES
+
+    def matmul(h, piece):
+        some = summed_ref[piece * share : (piece + 1) * share].reshape(share * rows, width)
+        return dot(some, node_ref[:, h : h + TILE])
+
+    def finish_members(buffer, h, piece):
+        for m in range(piece * share, (piece + 1) * share):
+            finish(buffer, m * rows, m, h)
+
+    staged([(h,) for h in range(0, width, TILE)], work_ref, matmul, finish_members)
 
 
 def forward_kernel(
@@ -100,21 +111,22 @@
     for m in range(members):
         comb_ref[m, TABLE:] = grid_ref[...]
 
-    def sum_edges(buffer, m, h):
-        for r, c in parts(CHUNK):
+    def sum_edges(buffer, m, h, piece):
+        for r, c in blocks(CHUNK, piece):
             twice = sum(
                 gelu_twice(buffer[k * CHUNK + r : k * CHUNK + r + PART, c : c + LANES])
                 for k in range(DEGREE)
             )
             summed_ref[m, r : r + PART, h + c : h + c + LANES] = (0.5 * twice).astype(jnp.bfloat16)
 
-    def node_values(buffer, m, h):
-        for r, c in parts(CHUNK):
-            u = buffer[r : r + PART, c : c + LANES]
-            s, t = tanh_of(u)
-            place = (m, slice(r, r + PART), slice(h + c, h + c + LANES))
-            out_ref[place] = (0.5 * (u + u * t)).astype(jnp.bfloat16)
-            slope_ref[place] = (0.5 * slope_twice(u, s, t)).astype(jnp.bfloat16)
+    def node_values(buffer, first, m, h):
+        for r in range(0, CHUNK, PART):
+            for c in range(0, TILE, LANES):
+                u = buffer[first + r : first + r + PART, c : c + LANES]
+                s, t = tanh_of(u)
+                place = (m, slice(r, r + PART), slice(h + c, h + c + LANES))
+                out_ref[place] = (0.5 * (u + u * t)).astype(jnp.bfloat16)
+                slope_ref[place] = (0.5 * slope_twice(u, s, t)).astype(jnp.bfloat16)
 
     edge_stage(pick_ref, comb_ref, work_ref, sum_edges)
     node_stage(summed_ref, node_ref, work_ref, node_values)
@@ -128,11 +140,13 @@
         both_ref[m, :TABLE] = comb_ref[m]
         both_ref[m, TABLE:] = grid_ref[...]
 
-    def edge_slopes(buffer, m, h):
+    def edge_slopes(buffer, m, h, piece):
         for k in range(DEGREE):
-            for r, c in parts(CHUNK):
-                value = slope_twice(buffer[k * CHUNK + r : k * CHUNK + r + PART, c : c + LANES])
-                edge_ref[m, k, r : r + PART, h + c : h + c + LANES] = value * 0.5
+            for r, c in blocks(CHUNK, piece):
+                value = 0.5 * slope_twice(
+                    buffer[k * CHUNK + r : k * CHUNK + r + PART, c : c + LANES]
+                )
+                edge_ref[m, k, r : r + PART, h + c : h + c + LANES] = value.astype(jnp.bfloat16)
 
     edge_stage(pick_ref, both_ref, work_ref, edge_slopes)
 
@@ -247,9 +261,9 @@
     split_rows(term, core_ref[0], mine_ref, other_ref, slice(0, term.shape[1]))
 
 
-def params(mebibytes):
+def params():
     return pltpu.CompilerParams(
-        dimension_semantics=("arbitrary",), vmem_limit_bytes=mebibytes * 1024 * 1024
+        dimension_semantics=("arbitrary",), vmem_limit_bytes=VMEM_LIMIT
     )
 
 
@@ -356,7 +370,7 @@
             pltpu.VMEM((DEGREE * CHUNK, TILE), jnp.float32),
             pltpu.VMEM((DEGREE * CHUNK, TILE), jnp.float32),
         ],
-        compiler_params=params(30),
+        compiler_params=params(),
         name="forward",
     )(source_rows, project_weight, pick, grid_state, node_weight, output_rows, prior_state)
 
@@ -374,15 +388,19 @@
         out_shape=jax.ShapeDtypeStruct((members, DEGREE, points, width), jnp.bfloat16),
         scratch_shapes=[
             pltpu.VMEM((members, TABLE + CHUNK, width), jnp.bfloat16),
-            pltpu.VMEM((DEGREE * CHUNK, TILE), jnp.bfloat16),
-            pltpu.VMEM((DEGREE * CHUNK, TILE), jnp.bfloat16),
-        ],
-        compiler_params=params(24),
+            pltpu.VMEM((DEGREE * CHUNK, TILE), jnp.float32),
+            pltpu.VMEM((DEGREE * CHUNK, TILE), jnp.float32),
+        ],
+        compiler_params=params(),
         cost_estimate=cost(members * DEGREE * points * width, 2 * TABLE, 20),
         name="edge_slopes",
     )(comb, pick, grid_state)
-    chip_pred, edge_slope = lax.optimization_barrier((chip_pred, edge_slope))
+    chip_pred, core_pred, edge_slope = lax.optimization_barrier((chip_pred, core_pred, edge_slope))
     far_pred = swap(chip_pred, 1)
+    source_columns = source_rows.reshape(members * table_rows, width).T
+    far_pred, source_columns, place, output_padded = lax.optimization_barrier(
+        (far_pred, source_columns, place, output_padded)
+    )
     grad_rows, node_pre_grad, loss_row = pl.pallas_call(
         loss_kernel,
         grid=(chunks,),
@@ -403,7 +421,7 @@
         scratch_shapes=[
             pltpu.VMEM((members, TABLE, CHUNK), jnp.float32), pltpu.VMEM((1, CHUNK), jnp.float32),
         ],
-        compiler_params=params(16),
+        compiler_params=params(),
         name="loss",
     )(core[None], pred, core_pred, chip_pred, far_pred, target, area_weight[None, :], scale, node_slope, output_padded)
 
@@ -413,9 +431,8 @@
     def add_partner(mine, other):
         return (mine.astype(jnp.float32) + swap(other, 1).astype(jnp.float32)).astype(jnp.bfloat16)
 
-    def sum_space(half):
-        moved = lax.all_to_all(half, "space", 0, 0, tiled=True)
-        return jnp.sum(moved.astype(jnp.float32), axis=0)
+    def across_space(half):
+        return lax.all_to_all(half, "space", 0, 0, tiled=True)
 
     def sum_members(part):
         mine = part + swap(part, 2)
@@ -440,12 +457,11 @@
         ],
         out_specs=[terms_block, terms_block],
         out_shape=[terms_shape, terms_shape],
-        compiler_params=params(32),
+        compiler_params=params(),
         cost_estimate=cost(width * width, members * points, 1),
         name="node_terms",
     )(core[None], summed, node_out, node_pre_grad, grad_rows, loss_row)
 
-    source_columns = source_rows.reshape(members * table_rows, width).T
     halves = 2
     tiles = width // TILE // halves
 
@@ -470,7 +486,7 @@
                 jax.ShapeDtypeStruct((members, table_rows, tiles * TILE), jnp.float32),
                 shape, shape,
             ],
-            compiler_params=params(40),
+            compiler_params=params(),
             cost_estimate=cost(members * points * width // halves, 4 * width, 8),
             name="table",
         )(core[None], pre_grad, node_weight, edge_slope, place, source_columns)
@@ -480,7 +496,7 @@
     second_input, node_half, first_mine = lax.optimization_barrier(
         (node_pre_grad, node_half, first_mine)
     )
-    node_part = sum_space(node_half)
+    node_moved = across_space(node_half)
     first_half = add_partner(first_mine, first_other)
     second_grad, second_mine, second_other = table_half(tiles, second_input)
     second_half = add_partner(second_mine, second_other)
@@ -493,10 +509,14 @@
         table_grad[:, own_nodes + send_rows :].astype(jnp.bfloat16), "space", forward
     )
     project_half = jnp.concatenate([first_half, second_half], axis=2)
-    project_half, node_part, left_back, right_back = lax.optimization_barrier(
-        (project_half, node_part, left_back, right_back)
-    )
-    sums = sum_members(jnp.concatenate([sum_space(project_half), node_part], axis=1))
+    project_half, node_moved, left_back, right_back = lax.optimization_barrier(
+        (project_half, node_moved, left_back, right_back)
+    )
+    node_part, project_part = (
+        jnp.sum(moved.astype(jnp.float32), axis=0)
+        for moved in (node_moved, across_space(project_half))
+    )
+    sums = sum_members(jnp.concatenate([project_part, node_part], axis=1))
     projected_grad = (
         table_grad[:, :own_nodes]
         + jnp.einsum(

time: 202 us -> 193 us (0.955)
  local copies, waits for them, and re-layouts: 32.6 us -> 9.29 us
  Pallas kernels: 80.1 us -> 95.5 us
  waiting for transfers between devices: 21.5 us -> 23.8 us
  matrix products: 7.99 us -> 5.92 us
    unnamed x66 -> x28, local copies, waits for them, and re-layouts: 30.2 us -> 4.63 us
    pallas_call x1, Pallas kernels: 23.4 us -> 28.4 us  [shards(): pl.pallas_call(forward_kernel_with_table, grid=(chunks,), in_specs=[whole...]
    pallas_call x2, Pallas kernels: 21 us -> 25.4 us  [table_half(): pl.pallas_call(table_kernel, grid=(tiles,), in_specs=[smem, whole(pre_gra...]
    dot_general x1, matrix products: 2.73 us -> 0.36 us  [shards(): jnp.einsum('sn,msh->mnh', chosen[1], left_back, preferred_element_type=jn...]
    convert_element_type x3, other arithmetic: 4.11 us -> 1.76 us  [add_partner(): (mine.astype(jnp.float32) + swap(other, 1).astype(jnp.float32)).astype(jn...]
    pallas_call x1, Pallas kernels: 8.05 us -> 10.4 us  [shards(): pl.pallas_call(node_term_kernel, grid=(width // TILE,), in_specs=[smem, s...]
    pallas_call x1, Pallas kernels: 19.4 us -> 21.5 us  [shards(): pl.pallas_call(edge_slope_kernel, grid=(chunks,), in_specs=[whole(comb),...]
  transfers between devices with their start and end apart: 15 -> 15, of which waited for: 5 -> 4; matrix products, arithmetic and copies ran while one was open for 10% -> 10% of each run, Pallas kernels for 20% -> 24%
where the time goes in v5:
time: 193 us; the launch traced here: 192 us
  Pallas kernels  95.5 us (49%)
  starting transfers between devices  42.6 us (22%)
  waiting for transfers between devices  23.8 us (12%)
  other arithmetic  11.2 us (6%)
  local copies, waits for them, and re-layouts  9.29 us (5%)
  matrix products  5.92 us (3%)
  between operations  3.42 us (2%)
    pallas_call x1, Pallas kernels, shards(): pl.pallas_call(forward_kernel_with_table, grid=(chunks,), in_specs=[whole...  28.4 us
    pallas_call x2, Pallas kernels, table_half(): pl.pallas_call(table_kernel, grid=(tiles,), in_specs=[smem, whole(pre_gra...  25.4 us
    pallas_call x1, Pallas kernels, shards(): pl.pallas_call(edge_slope_kernel, grid=(chunks,), in_specs=[whole(comb),...  21.5 us
    all_to_all x2, starting transfers between devices, across_space(): return lax.all_to_all(half, 'space', 0, 0, tiled=True)  19 us
    all_to_all x2, waiting for transfers between devices, across_space(): return lax.all_to_all(half, 'space', 0, 0, tiled=True)  15.8 us
    ppermute x9, starting transfers between devices, swap(): lax.ppermute(value, 'member', [(i, i ^ flip) for i in range(lax.axis_size...  12.5 us
    pallas_call x1, Pallas kernels, shards(): pl.pallas_call(node_term_kernel, grid=(width // TILE,), in_specs=[smem, s...  10.4 us
    pallas_call x1, Pallas kernels, shards(): pl.pallas_call(loss_kernel, grid=(chunks,), in_specs=[pl.BlockSpec(memory...  9.76 us
  transfers between devices with their start and end apart: 15, of which 4 were waited for; matrix products, arithmetic and copies ran while one was open for 10% of the time, Pallas kernels for 24%

profile of v5, /device:TPU:1, one launch (start us, length us, event | category | flops | bytes accessed | tf_op | source)
XLA Modules:
  0.0 191.7 jit_solution(16523148062834819754)
XLA Ops:
  0.6 1.4 fusion.12
  2.1 4.4 %collective-permute-start = (bf16[4,16,1024]{2,1,0:T(8,128)(2,1)S(1)}, bf16[4,16,1024]{2,1,0:T(8,128)(2,1)S(1)}, u32[]{:S(2)}, u32[]{:S(2)}) collective-permute-start(bf16[4,16,1024]{2,1,0:T(8,128)(2,1)S(1)} %get-tuple-element.70), channel_id=1, source_target_pairs={{0,1},{1,2},{2,3},{3,4},{4,5},{5,6},{6,7},{7,8},{8,9},{9,10},{10,1... | collective-permute-start | bytes 393224 | tf_op jit(solution)/shard_map/ppermute | solution.py:313
  6.4 1.3 collective-permute-start.1
  8.4 0.7 fusion.23
  9.1 0.8 convert_add_fusion
  9.9 0.8 add_select_fusion
  10.7 0.1 iota_compare_fusion.6
  10.8 1.3 fusion.5.refs_2_.pick_ref
  12.2 0.0 collective-permute-done
  12.2 0.0 collective-permute-done.1
  12.2 0.9 copy-done
  13.1 28.4 %forward.1 = (f32[4,104,512]{2,1,0:T(8,128)}, bf16[4,512,1024]{2,1,0:T(8,128)(2,1)}, bf16[4,512,1024]{2,1,0:T(8,128)(2,1)}, bf16[4,512,1024]{2,1,0:T(8,128)(2,1)}, bf16[4,128,1024]{2,1,0:T(8,128)(2,1)}) custom-call(bf16[4,96,1024]{2,1,0:T(8,128)(2,1)} %copy-done, bf16[1024,1024]{1,0:T(8,128)(2,1)} %refs_1_.1, bf16[4,512,256]{2,1,0:T(8,128)(2,1)} %fusion.5.refs_2_.pick_ref, ...), custom_call_target="tpu_custom_call" | custom-call | tf_op jit(solution)/shard_map/forward/pallas_call | solution.py:353
  41.6 3.4 %collective-permute-start.2 = (f32[4,104,512]{2,1,0:T(8,128)}, f32[4,104,512]{2,1,0:T(8,128)S(1)}, u32[]{:S(2)}, u32[]{:S(2)}) collective-permute-start(f32[4,104,512]{2,1,0:T(8,128)} %get-tuple-element.35.own_ref), channel_id=1, source_target_pairs={{0,64},{32,96},{64,0},{96,32},{1,65},{33,97},{65,1},{97,33},{2,66}... | collective-permute-start | bytes 2555912 | tf_op jit(solution)/shard_map/ppermute | solution.py:378
  44.9 2.3 %collective-permute-start.3 = (f32[4,104,512]{2,1,0:T(8,128)}, f32[4,104,512]{2,1,0:T(8,128)S(1)}, u32[]{:S(2)}, u32[]{:S(2)}) collective-permute-start(f32[4,104,512]{2,1,0:T(8,128)} %get-tuple-element.35.own_ref), channel_id=1, source_target_pairs={{0,32},{32,0},{64,96},{96,64},{1,33},{33,1},{65,97},{97,65},{2,34}... | collective-permute-start | bytes 2555912 | tf_op jit(solution)/shard_map/ppermute | solution.py:378
  47.3 21.5 %edge_slopes.1.slope_ref = bf16[4,4,512,1024]{3,2,1,0:T(8,128)(2,1)} custom-call(bf16[4,128,1024]{2,1,0:T(8,128)(2,1)} %get-tuple-element.36.comb_ref, bf16[4,512,256]{2,1,0:T(8,128)(2,1)} %fusion.5.refs_2_.pick_ref, bf16[512,1024]{1,0:T(8,128)(2,1)} %grid_ref.1), custom_call_target="tpu_custom_call" | custom-call | flops 4462739456 | bytes 16777216 | tf_op jit(solution)/shard_map/edge_slopes/pallas_call | solution.py:383
  68.8 0.0 collective-permute-done.2.chip_ref
  68.8 0.0 collective-permute-done.3.core_ref
  68.8 0.1 collective-permute-start.4
  68.9 1.3 copy.23
  70.2 0.7 pad.9.output_ref
  71.0 1.4 copy.21.variable_ref
  72.4 1.6 fusion.14.place_ref
  74.0 1.2 copy.20
  75.1 0.0 collective-permute-done.4.far_ref
  75.2 0.9 copy-done.6
  76.1 9.8 %loss.1 = (bf16[4,512,128]{2,1,0:T(8,128)(2,1)}, bf16[4,512,1024]{2,1,0:T(8,128)(2,1)}, f32[1,128]{1,0:T(1,128)}) custom-call(s32[1]{0:T(128)} %bitcast.core_index_ref.core_ref, f32[4,104,512]{2,1,0:T(8,128)} %get-tuple-element.35.own_ref, f32[4,104,512]{2,1,0:T(8,128)} %copy-done.5, f32[4,104,512]{2,1,0:T(8,128)} %copy-done.4, f32[4,104,512]{2,1,0:T(8,128)} %copy-done.6, ...), custom_call_target="tpu_custom_call" | custom-call | tf_op jit(solution)/shard_map/loss/pallas_call | solution.py:404
  85.8 10.4 %node_terms.1 = (bf16[32,16,1152]{2,1,0:T(8,128)(2,1)}, bf16[32,16,1152]{2,1,0:T(8,128)(2,1)}) custom-call(s32[1]{0:T(128)} %bitcast.core_index_ref.core_ref, bf16[4,512,1024]{2,1,0:T(8,128)(2,1)} %get-tuple-element.47.summed_ref, bf16[4,512,1024]{2,1,0:T(8,128)(2,1)} %get-tuple-element.48.out_ref, bf16[4,512,1024]{2,1,0:T(8,128)(2,1)} %get-tuple-element.54.pre_ref, ...), custom_call_target="tpu_custom_call" | custom-call | flops 4296015872 | bytes 2097152 | tf_op jit(solution)/shard_map/node_terms/pallas_call | solution.py:451
  96.2 0.5 collective-permute-start.5
  96.7 12.7 %table.2 = (f32[4,96,512]{2,1,0:T(8,128)}, bf16[32,16,512]{2,1,0:T(8,128)(2,1)}, bf16[32,16,512]{2,1,0:T(8,128)(2,1)}) custom-call(s32[1]{0:T(128)} %bitcast.core_index_ref.core_ref, bf16[4,512,1024]{2,1,0:T(8,128)(2,1)} %get-tuple-element.54.pre_ref, bf16[1024,1024]{1,0:T(8,128)(2,1)} %node_ref.3, bf16[4,4,512,1024]{3,2,1,0:T(8,128)(2,1)} %edge_slopes.1.slope_ref, ...), custom_call_target="tpu_custom_call" | custom-call | flops 8598323200 | bytes 2097152 | tf_op jit(solution)/shard_map/table/pallas_call | solution.py:471
  109.4 0.1 collective-permute-start.6
  109.5 1.3 constant_dynamic-update-slice_fusion.4
  110.7 0.0 collective-permute-done.5
  110.7 0.1 copy-done.3
  110.9 1.4 add_convert_fusion
  112.3 9.6 %all-to-all-start = ((bf16[32,16,1152]{2,1,0:T(8,128)(2,1)}), bf16[32,16,1152]{2,1,0:T(8,128)(2,1)S(1)}, u32[]{:S(2)}, u32[]{:S(2)}) async-start(bf16[32,16,1152]{2,1,0:T(8,128)(2,1)} %add_convert_fusion), calls=%async_computation | async-start | bytes 2359296 | tf_op jit(solution)/shard_map/all_to_all | solution.py:435
  121.9 12.7 %table.3 = (f32[4,96,512]{2,1,0:T(8,128)}, bf16[32,16,512]{2,1,0:T(8,128)(2,1)}, bf16[32,16,512]{2,1,0:T(8,128)(2,1)}) custom-call(s32[1]{0:T(128)} %bitcast.core_index_ref.core_ref, bf16[4,512,1024]{2,1,0:T(8,128)(2,1)} %get-tuple-element.54.pre_ref, bf16[1024,1024]{1,0:T(8,128)(2,1)} %node_ref.3, bf16[4,4,512,1024]{3,2,1,0:T(8,128)(2,1)} %edge_slopes.1.slope_ref, ...), custom_call_target="tpu_custom_call" | custom-call | flops 8598323200 | bytes 2097152 | tf_op jit(solution)/shard_map/table/pallas_call | solution.py:471
  134.7 0.5 collective-permute-start.7
  135.2 1.3 constant_dynamic-update-slice_fusion.3
  136.5 0.1 convert.4
  136.6 1.3 collective-permute-start.8
  137.9 4.0 %collective-permute-start.9 = (bf16[4,16,1024]{2,1,0:T(8,128)(2,1)S(1)}, bf16[4,16,1024]{2,1,0:T(8,128)(2,1)S(1)}, u32[]{:S(2)}, u32[]{:S(2)}) collective-permute-start(bf16[4,16,1024]{2,1,0:T(8,128)(2,1)S(1)} %get-tuple-element.65), channel_id=1, source_target_pairs={{0,1},{1,2},{2,3},{3,4},{4,5},{5,6},{6,7},{7,8},{8,9},{9,10},{10,1... | collective-permute-start | bytes 393224 | tf_op jit(solution)/shard_map/ppermute | solution.py:508
  142.0 0.2 add_convert_fusion.2
  142.2 0.2 add_convert_fusion.1
  142.4 0.0 copy-start.11
  142.4 1.1 pad_maximum_fusion
  143.6 0.8 collective-permute-done.8
  144.3 2.7 %collective-permute-done.9 = bf16[4,16,1024]{2,1,0:T(8,128)(2,1)S(1)} collective-permute-done((bf16[4,16,1024]{2,1,0:T(8,128)(2,1)S(1)}, bf16[4,16,1024]{2,1,0:T(8,128)(2,1)S(1)}, u32[]{:S(2)}, u32[]{:S(2)}) %collective-permute-start.9) | collective-permute-done | bytes 131104 | tf_op jit(solution)/shard_map/ppermute | solution.py:508
  147.0 0.0 all-to-all-done
  147.0 9.4 %all-to-all-start.1 = ((bf16[32,16,1024]{2,1,0:T(8,128)(2,1)}), bf16[32,16,1024]{2,1,0:T(8,128)(2,1)}, u32[]{:S(2)}, u32[]{:S(2)}) async-start(bf16[32,16,1024]{2,1,0:T(8,128)(2,1)} %pad_maximum_fusion), calls=%async_computation.1 | async-start | bytes 2097152 | tf_op jit(solution)/shard_map/all_to_all | solution.py:435
  156.4 0.1 iota_compare_fusion.8
  156.5 0.2 convert_reduce_fusion
  156.7 0.4 fusion.7
  157.0 15.8 %all-to-all-done.1 = bf16[32,16,1024]{2,1,0:T(8,128)(2,1)} async-done(((bf16[32,16,1024]{2,1,0:T(8,128)(2,1)}), bf16[32,16,1024]{2,1,0:T(8,128)(2,1)}, u32[]{:S(2)}, u32[]{:S(2)}) %all-to-all-start.1) | async-done | bytes 1048608 | tf_op jit(solution)/shard_map/all_to_all | solution.py:435
  172.9 1.4 convert_reduce_fusion.1
  174.3 0.7 collective-permute-start.10
  174.9 3.4 %fusion.8 = bf16[4,64,1024]{2,1,0:T(8,128)(2,1)} fusion(bf16[1024,1024]{1,0:T(8,128)(2,1)} %refs_1_.1, f32[4,64,1024]{2,1,0:T(8,128)S(1)} %fusion.7, bf16[4,16,1024]{2,1,0:T(8,128)(2,1)S(1)} %collective-permute-done.9, pred[2,16,64]{2,1,0:T(8,128)(4,1)S(1)} %iota_compare_fusion.8), kind=kOutput, calls=%fused_computation.15 | convolution fusion | flops 546045952 | bytes 3803136 | tf_op jit(solution)/shard_map/mnk,hk->mnh/dot_general | solution.py:529
  178.3 2.7 %collective-permute-start.11 = (f32[16,2176]{1,0:T(8,128)S(1)}, f32[16,2176]{1,0:T(8,128)S(1)}, u32[]{:S(2)}, u32[]{:S(2)}) collective-permute-start(f32[16,2176]{1,0:T(8,128)S(1)} %pad_maximum_fusion.1), channel_id=1, source_target_pairs={{0,32},{32,0},{64,96},{96,64},{1,33},{33,1},{65,97},{97,65},{2,34}... | collective-permute-start | bytes 417800 | tf_op jit(solution)/shard_map/ppermute | solution.py:378
  181.0 2.3 %collective-permute-start.12 = (f32[16,2176]{1,0:T(8,128)S(1)}, f32[16,2176]{1,0:T(8,128)S(1)}, u32[]{:S(2)}, u32[]{:S(2)}) collective-permute-start(f32[16,2176]{1,0:T(8,128)S(1)} %pad_maximum_fusion.1), channel_id=1, source_target_pairs={{0,96},{32,64},{64,32},{96,0},{1,97},{33,65},{65,33},{97,1},{2,98}... | collective-permute-start | bytes 417800 | tf_op jit(solution)/shard_map/ppermute | solution.py:378
  183.3 0.0 collective-permute-done.10
  183.3 0.0 collective-permute-done.11
  183.3 4.5 %collective-permute-done.12 = f32[16,2176]{1,0:T(8,128)S(1)} collective-permute-done((f32[16,2176]{1,0:T(8,128)S(1)}, f32[16,2176]{1,0:T(8,128)S(1)}, u32[]{:S(2)}, u32[]{:S(2)}) %collective-permute-start.12) | collective-permute-done | bytes 139296 | tf_op jit(solution)/shard_map/ppermute | solution.py:378
  187.9 0.7 slice_multiply_fusion
  188.6 0.6 slice_multiply_fusion.2
  189.2 0.7 slice_reduce_fusion
  (34 shorter events, 0.3 us)
Async XLA Ops:
  0.6 11.5 %copy-start.2 = (bf16[4,64,1024]{2,1,0:T(8,128)(2,1)S(1)}, bf16[4,64,1024]{2,1,0:T(8,128)(2,1)}, u32[]{:S(2)}) copy-start(bf16[4,64,1024]{2,1,0:T(8,128)(2,1)} %param.13) | copy-start | bytes 1572868
  2.1 10.1 %collective-permute-start = (bf16[4,16,1024]{2,1,0:T(8,128)(2,1)S(1)}, bf16[4,16,1024]{2,1,0:T(8,128)(2,1)S(1)}, u32[]{:S(2)}, u32[]{:S(2)}) collective-permute-start(bf16[4,16,1024]{2,1,0:T(8,128)(2,1)S(1)} %get-tuple-element.70), channel_id=1, source_target_pairs={{0,1},{1,2},{2,3},{3,4},{4,5},{5,6},{6,7},{7,8},{8,9},{9,10},{10,1... | collective-permute-start | bytes 393224 | tf_op jit(solution)/shard_map/ppermute | solution.py:313
  6.4 5.8 %collective-permute-start.1 = (bf16[4,16,1024]{2,1,0:T(8,128)(2,1)S(1)}, bf16[4,16,1024]{2,1,0:T(8,128)(2,1)S(1)}, u32[]{:S(2)}, u32[]{:S(2)}) collective-permute-start(bf16[4,16,1024]{2,1,0:T(8,128)(2,1)S(1)} %get-tuple-element.69), channel_id=1, source_target_pairs={{1,0},{2,1},{3,2},{4,3},{5,4},{6,5},{7,6},{8,7},{9,8},{10,9},{11,1... | collective-permute-start | bytes 393224 | tf_op jit(solution)/shard_map/ppermute | solution.py:314
  10.7 30.9 %copy-start.10 = (s32[4,512]{1,0:T(4,128)}, s32[4,512]{1,0:T(4,128)S(1)}, u32[]{:S(2)}) copy-start(s32[4,512]{1,0:T(4,128)S(1)} %add_select_fusion) | copy-start | bytes 24580
  12.2 0.9 copy-start
  41.6 27.2 %collective-permute-start.2 = (f32[4,104,512]{2,1,0:T(8,128)}, f32[4,104,512]{2,1,0:T(8,128)S(1)}, u32[]{:S(2)}, u32[]{:S(2)}) collective-permute-start(f32[4,104,512]{2,1,0:T(8,128)} %get-tuple-element.35.own_ref), channel_id=1, source_target_pairs={{0,64},{32,96},{64,0},{96,32},{1,65},{33,97},{65,1},{97,33},{2,66}... | collective-permute-start | bytes 2555912 | tf_op jit(solution)/shard_map/ppermute | solution.py:378
  44.9 23.9 %collective-permute-start.3 = (f32[4,104,512]{2,1,0:T(8,128)}, f32[4,104,512]{2,1,0:T(8,128)S(1)}, u32[]{:S(2)}, u32[]{:S(2)}) collective-permute-start(f32[4,104,512]{2,1,0:T(8,128)} %get-tuple-element.35.own_ref), channel_id=1, source_target_pairs={{0,32},{32,0},{64,96},{96,64},{1,33},{33,1},{65,97},{97,65},{2,34}... | collective-permute-start | bytes 2555912 | tf_op jit(solution)/shard_map/ppermute | solution.py:378
  47.3 23.0 %copy-start.7 = (bf16[1024,100]{0,1:T(8,128)(2,1)S(1)}, bf16[1024,100]{0,1:T(8,128)(2,1)}, u32[]{:S(2)}) copy-start(bf16[1024,100]{0,1:T(8,128)(2,1)} %param.17) | copy-start | bytes 614404
  47.3 26.7 %copy-start.1 = (bf16[4,96,1024]{2,1,0:T(8,128)(2,1)S(1)}, bf16[4,96,1024]{2,1,0:T(8,128)(2,1)}, u32[]{:S(2)}) copy-start(bf16[4,96,1024]{2,1,0:T(8,128)(2,1)} %copy-done) | copy-start | bytes 2359300
  68.8 6.4 %copy-start.4 = (f32[4,104,512]{2,1,0:T(8,128)}, f32[4,104,512]{2,1,0:T(8,128)S(1)}, u32[]{:S(2)}) copy-start(f32[4,104,512]{2,1,0:T(8,128)S(1)} %collective-permute-done.2.chip_ref) | copy-start | bytes 2555908
  68.8 6.4 %copy-start.5 = (f32[4,104,512]{2,1,0:T(8,128)}, f32[4,104,512]{2,1,0:T(8,128)S(1)}, u32[]{:S(2)}) copy-start(f32[4,104,512]{2,1,0:T(8,128)S(1)} %collective-permute-done.3.core_ref) | copy-start | bytes 2555908
  68.8 6.3 %collective-permute-start.4 = (f32[4,104,512]{2,1,0:T(8,128)S(1)}, f32[4,104,512]{2,1,0:T(8,128)S(1)}, u32[]{:S(2)}, u32[]{:S(2)}) collective-permute-start(f32[4,104,512]{2,1,0:T(8,128)S(1)} %collective-permute-done.2.chip_ref), channel_id=1, source_target_pairs={{0,32},{32,0},{64,96},{96,64},{1,33},{33,1},{65,97},{97,65},{2,34}... | collective-permute-start | bytes 2555912 | tf_op jit(solution)/shard_map/ppermute | solution.py:378
  75.1 0.9 copy-start.6
  96.2 14.5 %collective-permute-start.5 = (bf16[32,16,1152]{2,1,0:T(8,128)(2,1)}, bf16[32,16,1152]{2,1,0:T(8,128)(2,1)S(1)}, u32[]{:S(2)}, u32[]{:S(2)}) collective-permute-start(bf16[32,16,1152]{2,1,0:T(8,128)(2,1)} %get-tuple-element.52), channel_id=1, source_target_pairs={{0,32},{32,0},{64,96},{96,64},{1,33},{33,1},{65,97},{97,65},{2,34}... | collective-permute-start | bytes 3538952 | tf_op jit(solution)/shard_map/ppermute | solution.py:378
  109.4 1.5 copy-start.3
  109.4 32.6 %collective-permute-start.6 = (bf16[32,16,512]{2,1,0:T(8,128)(2,1)}, bf16[32,16,512]{2,1,0:T(8,128)(2,1)S(1)}, u32[]{:S(2)}, u32[]{:S(2)}) collective-permute-start(bf16[32,16,512]{2,1,0:T(8,128)(2,1)} %get-tuple-element.57), channel_id=1, source_target_pairs={{0,32},{32,0},{64,96},{96,64},{1,33},{33,1},{65,97},{97,65},{2,34}... | collective-permute-start | bytes 1572872 | tf_op jit(solution)/shard_map/ppermute | solution.py:378
  112.3 34.7 %all-to-all-start = ((bf16[32,16,1152]{2,1,0:T(8,128)(2,1)}), bf16[32,16,1152]{2,1,0:T(8,128)(2,1)S(1)}, u32[]{:S(2)}, u32[]{:S(2)}) async-start(bf16[32,16,1152]{2,1,0:T(8,128)(2,1)} %add_convert_fusion), calls=%async_computation | async-start | bytes 2359296 | tf_op jit(solution)/shard_map/all_to_all | solution.py:435
  134.7 7.5 %collective-permute-start.7 = (bf16[32,16,512]{2,1,0:T(8,128)(2,1)}, bf16[32,16,512]{2,1,0:T(8,128)(2,1)S(1)}, u32[]{:S(2)}, u32[]{:S(2)}) collective-permute-start(bf16[32,16,512]{2,1,0:T(8,128)(2,1)} %get-tuple-element.59), channel_id=1, source_target_pairs={{0,32},{32,0},{64,96},{96,64},{1,33},{33,1},{65,97},{97,65},{2,34}... | collective-permute-start | bytes 1572872 | tf_op jit(solution)/shard_map/ppermute | solution.py:378
  135.2 6.8 %copy-start.8 = (bf16[32,16,512]{2,1,0:T(8,128)(2,1)S(1)}, bf16[32,16,512]{2,1,0:T(8,128)(2,1)}, u32[]{:S(2)}) copy-start(bf16[32,16,512]{2,1,0:T(8,128)(2,1)} %get-tuple-element.56) | copy-start | bytes 1572868
  136.5 5.7 %copy-start.9 = (bf16[32,16,512]{2,1,0:T(8,128)(2,1)S(1)}, bf16[32,16,512]{2,1,0:T(8,128)(2,1)}, u32[]{:S(2)}) copy-start(bf16[32,16,512]{2,1,0:T(8,128)(2,1)} %get-tuple-element.58) | copy-start | bytes 1572868
  136.6 7.7 %collective-permute-start.8 = (bf16[4,16,1024]{2,1,0:T(8,128)(2,1)S(1)}, bf16[4,16,1024]{2,1,0:T(8,128)(2,1)S(1)}, u32[]{:S(2)}, u32[]{:S(2)}) collective-permute-start(bf16[4,16,1024]{2,1,0:T(8,128)(2,1)S(1)} %get-tuple-element.66), channel_id=1, source_target_pairs={{1,0},{2,1},{3,2},{4,3},{5,4},{6,5},{7,6},{8,7},{9,8},{10,9},{11,1... | collective-permute-start | bytes 393224 | tf_op jit(solution)/shard_map/ppermute | solution.py:505
  137.9 9.1 %collective-permute-start.9 = (bf16[4,16,1024]{2,1,0:T(8,128)(2,1)S(1)}, bf16[4,16,1024]{2,1,0:T(8,128)(2,1)S(1)}, u32[]{:S(2)}, u32[]{:S(2)}) collective-permute-start(bf16[4,16,1024]{2,1,0:T(8,128)(2,1)S(1)} %get-tuple-element.65), channel_id=1, source_target_pairs={{0,1},{1,2},{2,3},{3,4},{4,5},{5,6},{6,7},{7,8},{8,9},{9,10},{10,1... | collective-permute-start | bytes 393224 | tf_op jit(solution)/shard_map/ppermute | solution.py:508
  142.4 14.0 %copy-start.11 = (s32[2,16]{1,0:T(2,128)S(1)}, s32[2,16]{1,0:T(2,128)}, u32[]{:S(2)}) copy-start(s32[2,16]{1,0:T(2,128)} %param.25) | copy-start | bytes 388
  147.0 25.9 %all-to-all-start.1 = ((bf16[32,16,1024]{2,1,0:T(8,128)(2,1)}), bf16[32,16,1024]{2,1,0:T(8,128)(2,1)}, u32[]{:S(2)}, u32[]{:S(2)}) async-start(bf16[32,16,1024]{2,1,0:T(8,128)(2,1)} %pad_maximum_fusion), calls=%async_computation.1 | async-start | bytes 2097152 | tf_op jit(solution)/shard_map/all_to_all | solution.py:435
  174.3 9.0 %collective-permute-start.10 = (f32[16,2176]{1,0:T(8,128)S(1)}, f32[16,2176]{1,0:T(8,128)S(1)}, u32[]{:S(2)}, u32[]{:S(2)}) collective-permute-start(f32[16,2176]{1,0:T(8,128)S(1)} %pad_maximum_fusion.1), channel_id=1, source_target_pairs={{0,64},{32,96},{64,0},{96,32},{1,65},{33,97},{65,1},{97,33},{2,66}... | collective-permute-start | bytes 417800 | tf_op jit(solution)/shard_map/ppermute | solution.py:378
  178.3 5.0 %collective-permute-start.11 = (f32[16,2176]{1,0:T(8,128)S(1)}, f32[16,2176]{1,0:T(8,128)S(1)}, u32[]{:S(2)}, u32[]{:S(2)}) collective-permute-start(f32[16,2176]{1,0:T(8,128)S(1)} %pad_maximum_fusion.1), channel_id=1, source_target_pairs={{0,32},{32,0},{64,96},{96,64},{1,33},{33,1},{65,97},{97,65},{2,34}... | collective-permute-start | bytes 417800 | tf_op jit(solution)/shard_map/ppermute | solution.py:378
  181.0 6.8 %collective-permute-start.12 = (f32[16,2176]{1,0:T(8,128)S(1)}, f32[16,2176]{1,0:T(8,128)S(1)}, u32[]{:S(2)}, u32[]{:S(2)}) collective-permute-start(f32[16,2176]{1,0:T(8,128)S(1)} %pad_maximum_fusion.1), channel_id=1, source_target_pairs={{0,96},{32,64},{64,32},{96,0},{1,97},{33,65},{65,33},{97,1},{2,98}... | collective-permute-start | bytes 417800 | tf_op jit(solution)/shard_map/ppermute | solution.py:378

commit v6 on v5

--- a/solution.py
+++ b/solution.py
@@ -17,7 +17,7 @@
 CHUNK = 128
 TILE = 256
 PART = 32
-PIECES = 2
+PIECES = 1
 VMEM_LIMIT = 56 * 1024 * 1024
 LANES = 128
 
@@ -95,18 +95,28 @@
 
 
 def forward_kernel(
-    rows_ref, project_ref, pick_ref, grid_ref, node_ref, output_ref, prior_ref,
-    pred_ref, summed_ref, out_ref, slope_ref, comb_ref, *work_ref,
+    own_ref, left_ref, right_ref, project_ref, pick_ref, grid_ref, node_ref, output_ref, prior_ref,
+    pred_ref, summed_ref, out_ref, slope_ref, table_ref, columns_ref,
+    comb_ref, rows_ref, *work_ref,
 ):
-    members, table_rows, width = rows_ref.shape
+    members, own_nodes, width = own_ref.shape
+    table_rows = own_nodes + left_ref.shape[1] + right_ref.shape[1]
 
     @pl.when(pl.program_id(0) == 0)
     def _():
         for m in range(members):
-            comb_ref[m, :table_rows] = dot(rows_ref[m], project_ref[...]).astype(jnp.bfloat16)
+            first = m * table_rows
+            for ref in (own_ref, left_ref, right_ref):
+                rows_ref[first : first + ref.shape[1]] = ref[m]
+                first += ref.shape[1]
+        projected = dot(rows_ref[...], project_ref[...]).astype(jnp.bfloat16)
+        for m in range(members):
+            comb_ref[m, :table_rows] = projected[m * table_rows : (m + 1) * table_rows]
             comb_ref[m, table_rows:TABLE] = jnp.full(
                 (TABLE - table_rows, width), EMPTY, jnp.bfloat16
             )
+        table_ref[...] = comb_ref[:, :TABLE]
+        columns_ref[...] = rows_ref[...].astype(jnp.float32).T.astype(jnp.bfloat16)
 
     for m in range(members):
         comb_ref[m, TABLE:] = grid_ref[...]
@@ -152,7 +162,7 @@
 
 
 def loss_kernel(
-    core_index_ref, own_ref, core_ref, chip_ref, far_ref, truth_ref, area_ref, variable_ref, slope_ref, output_ref,
+    core_index_ref, own_ref, core_ref, chip_ref, far_ref, truth_ref, weight_ref, slope_ref, output_ref,
     grad_ref, pre_ref, loss_ref, tall_ref, sum_ref,
 ):
     members = own_ref.shape[0]
@@ -171,7 +181,7 @@
     total = jnp.zeros((1, CHUNK), jnp.float32)
     for first in range(0, variables, PART):
         rows = slice(first, min(first + PART, variables))
-        weight = variable_ref[rows] * area_ref[...]
+        weight = weight_ref[rows]
         truth = truth_ref[rows]
         terms = jnp.zeros_like(truth)
         for j in range(members):
@@ -244,10 +254,20 @@
 
 
 def table_kernel(
-    core_ref, pre_ref, node_ref, slope_ref, place_ref, rows_ref, grad_ref, mine_ref, other_ref,
+    core_ref, pre_ref, node_ref, slope_ref, slot_ref, rows_ref, grad_ref, mine_ref, other_ref,
+    place_ref,
 ):
     members, points, _ = pre_ref.shape
     table_rows = grad_ref.shape[1]
+
+    @pl.when(pl.program_id(0) == 0)
+    def _():
+        for k in range(DEGREE):
+            columns = slice(k * points, (k + 1) * points)
+            row = lax.broadcasted_iota(jnp.int32, (TABLE, points), 0)
+            picked = jnp.where(slot_ref[:, columns] == row, 1.0, 0.0)
+            place_ref[:, columns] = picked.astype(jnp.bfloat16)
+
     cast = []
     for m in range(members):
         summed_grad = dot_nt(pre_ref[m], node_ref[...]).astype(jnp.bfloat16)
@@ -334,14 +354,10 @@
     pick = (
         (by_chunk[..., None] == columns) | ((within[:, None] + TABLE) == columns)
     ).astype(jnp.bfloat16).reshape(chunks, DEGREE * CHUNK, TABLE + CHUNK)
-    place = (
-        slot.reshape(1, DEGREE * points) == jnp.arange(TABLE, dtype=jnp.int32)[:, None]
-    ).astype(jnp.bfloat16)
+    slot_row = slot.reshape(1, DEGREE * points)
     output_rows = output_weight.T
     output_padded = jnp.pad(output_rows, ((0, TABLE - variables), (0, 0)))
-    scale = variable_weight[:, None]
-
-    source_rows = jnp.concatenate([hidden, from_left, from_right], axis=1)
+    weight_map = variable_weight[:, None] * area_weight[None, :]
 
     chunk_rows = pl.BlockSpec((CHUNK, width), lambda c: (c, 0))
     member_rows = pl.BlockSpec((members, CHUNK, width), lambda c: (0, c, 0))
@@ -350,29 +366,33 @@
     tiled_rows = -(-variables // 8) * 8
     own_block = pl.BlockSpec((members, tiled_rows, CHUNK), lambda c: (0, 0, c))
     per_point = jax.ShapeDtypeStruct((members, points, width), jnp.bfloat16)
-    pred, summed, node_out, node_slope, comb = pl.pallas_call(
-        forward_kernel_with_table,
+    pred, summed, node_out, node_slope, comb, source_columns = pl.pallas_call(
+        forward_kernel,
         grid=(chunks,),
         in_specs=[
-            whole(source_rows), whole(project_weight), pick_block, chunk_rows,
+            whole(hidden), whole(from_left), whole(from_right), whole(project_weight), pick_block,
+            chunk_rows,
             whole(node_weight), whole(output_rows), by_variable,
         ],
         out_specs=[
             own_block, member_rows, member_rows, member_rows,
             pl.BlockSpec((members, TABLE, width), lambda c: (0, 0, 0)),
+            pl.BlockSpec((width, members * table_rows), lambda c: (0, 0)),
         ],
         out_shape=[
             jax.ShapeDtypeStruct((members, tiled_rows, points), jnp.float32), per_point, per_point,
             per_point, jax.ShapeDtypeStruct((members, TABLE, width), jnp.bfloat16),
+            jax.ShapeDtypeStruct((width, members * table_rows), jnp.bfloat16),
         ],
         scratch_shapes=[
             pltpu.VMEM((members, TABLE + CHUNK, width), jnp.bfloat16),
+            pltpu.VMEM((members * table_rows, width), jnp.bfloat16),
             pltpu.VMEM((DEGREE * CHUNK, TILE), jnp.float32),
             pltpu.VMEM((DEGREE * CHUNK, TILE), jnp.float32),
         ],
         compiler_params=params(),
         name="forward",
-    )(source_rows, project_weight, pick, grid_state, node_weight, output_rows, prior_state)
+    )(hidden, from_left, from_right, project_weight, pick, grid_state, node_weight, output_rows, prior_state)
 
     def swap(value, flip):
         return lax.ppermute(value, "member", [(i, i ^ flip) for i in range(lax.axis_size("member"))])
@@ -397,18 +417,15 @@
     )(comb, pick, grid_state)
     chip_pred, core_pred, edge_slope = lax.optimization_barrier((chip_pred, core_pred, edge_slope))
     far_pred = swap(chip_pred, 1)
-    source_columns = source_rows.reshape(members * table_rows, width).T
-    far_pred, source_columns, place, output_padded = lax.optimization_barrier(
-        (far_pred, source_columns, place, output_padded)
+    far_pred, weight_map, output_padded = lax.optimization_barrier(
+        (far_pred, weight_map, output_padded)
     )
     grad_rows, node_pre_grad, loss_row = pl.pallas_call(
         loss_kernel,
         grid=(chunks,),
         in_specs=[
             pl.BlockSpec(memory_space=pltpu.SMEM),
-            own_block, own_block, own_block, own_block, by_variable,
-            pl.BlockSpec((1, CHUNK), lambda c: (0, c)),
-            whole(scale), member_rows, whole(output_padded),
+            own_block, own_block, own_block, own_block, by_variable, by_variable, member_rows, whole(output_padded),
         ],
         out_specs=[
             pl.BlockSpec((members, CHUNK, TABLE), lambda c: (0, c, 0)), member_rows,
@@ -423,7 +440,7 @@
         ],
         compiler_params=params(),
         name="loss",
-    )(core[None], pred, core_pred, chip_pred, far_pred, target, area_weight[None, :], scale, node_slope, output_padded)
+    )(core[None], pred, core_pred, chip_pred, far_pred, target, weight_map, node_slope, output_padded)
 
     own_rows = width // space // 2
     smem = pl.BlockSpec(memory_space=pltpu.SMEM)
@@ -462,61 +479,46 @@
         name="node_terms",
     )(core[None], summed, node_out, node_pre_grad, grad_rows, loss_row)
 
-    halves = 2
-    tiles = width // TILE // halves
-
-    def table_half(first, pre_grad):
-        columns = pl.BlockSpec((space, own_rows, TILE), lambda c: (0, 0, c))
-        shape = jax.ShapeDtypeStruct((space, own_rows, tiles * TILE), jnp.bfloat16)
-        return pl.pallas_call(
-            table_kernel,
-            grid=(tiles,),
-            in_specs=[
-                smem,
-                whole(pre_grad),
-                pl.BlockSpec((TILE, width), lambda c: (first + c, 0)),
-                pl.BlockSpec((members, DEGREE, points, TILE), lambda c: (0, 0, 0, first + c)),
-                whole(place),
-                whole(source_columns),
-            ],
-            out_specs=[
-                pl.BlockSpec((members, table_rows, TILE), lambda c: (0, 0, c)), columns, columns,
-            ],
-            out_shape=[
-                jax.ShapeDtypeStruct((members, table_rows, tiles * TILE), jnp.float32),
-                shape, shape,
-            ],
-            compiler_params=params(),
-            cost_estimate=cost(members * points * width // halves, 4 * width, 8),
-            name="table",
-        )(core[None], pre_grad, node_weight, edge_slope, place, source_columns)
-
-    first_grad, first_mine, first_other = table_half(0, node_pre_grad)
     node_half = add_partner(node_mine, node_other)
-    second_input, node_half, first_mine = lax.optimization_barrier(
-        (node_pre_grad, node_half, first_mine)
-    )
+    pre_grad, node_half = lax.optimization_barrier((node_pre_grad, node_half))
     node_moved = across_space(node_half)
-    first_half = add_partner(first_mine, first_other)
-    second_grad, second_mine, second_other = table_half(tiles, second_input)
-    second_half = add_partner(second_mine, second_other)
-
-    table_grad = jnp.concatenate([first_grad, second_grad], axis=2)
+    columns = pl.BlockSpec((space, own_rows, TILE), lambda c: (0, 0, c))
+    columns_shape = jax.ShapeDtypeStruct((space, own_rows, width), jnp.bfloat16)
+    table_grad, project_mine, project_other = pl.pallas_call(
+        table_kernel,
+        grid=(width // TILE,),
+        in_specs=[
+            smem,
+            whole(pre_grad),
+            pl.BlockSpec((TILE, width), lambda c: (c, 0)),
+            pl.BlockSpec((members, DEGREE, points, TILE), lambda c: (0, 0, 0, c)),
+            whole(slot_row),
+            whole(source_columns),
+        ],
+        out_specs=[
+            pl.BlockSpec((members, table_rows, TILE), lambda c: (0, 0, c)), columns, columns,
+        ],
+        out_shape=[
+            jax.ShapeDtypeStruct((members, table_rows, width), jnp.float32),
+            columns_shape, columns_shape,
+        ],
+        scratch_shapes=[pltpu.VMEM((TABLE, DEGREE * points), jnp.bfloat16)],
+        compiler_params=params(),
+        cost_estimate=cost(members * points * width, 4 * width, 8),
+        name="table",
+    )(core[None], pre_grad, node_weight, edge_slope, slot_row, source_columns)
+    project_half = add_partner(project_mine, project_other)
+
     left_back = lax.ppermute(
         table_grad[:, own_nodes : own_nodes + send_rows].astype(jnp.bfloat16), "space", backward
     )
     right_back = lax.ppermute(
         table_grad[:, own_nodes + send_rows :].astype(jnp.bfloat16), "space", forward
     )
-    project_half = jnp.concatenate([first_half, second_half], axis=2)
     project_half, node_moved, left_back, right_back = lax.optimization_barrier(
         (project_half, node_moved, left_back, right_back)
     )
-    node_part, project_part = (
-        jnp.sum(moved.astype(jnp.float32), axis=0)
-        for moved in (node_moved, across_space(project_half))
-    )
-    sums = sum_members(jnp.concatenate([project_part, node_part], axis=1))
+    project_moved = across_space(project_half)
     projected_grad = (
         table_grad[:, :own_nodes]
         + jnp.einsum(
@@ -529,6 +531,11 @@
     grad_hidden = jnp.einsum(
         "mnk,hk->mnh", projected_grad, project_weight, preferred_element_type=jnp.float32
     ).astype(jnp.bfloat16)
+    project_moved, grad_hidden = lax.optimization_barrier((project_moved, grad_hidden))
+    project_part, node_part = (
+        jnp.sum(moved.astype(jnp.float32), axis=0) for moved in (project_moved, node_moved)
+    )
+    sums = sum_members(jnp.concatenate([project_part, node_part], axis=1))
     output_at = 2 * width
     loss_at = output_at + variables
     return (
@@ -538,15 +545,6 @@
         sums[:, output_at:loss_at] / total_points,
         jnp.sum(sums[0, loss_at:]) / (total_points * variables),
     )
-
-
-def forward_kernel_with_table(*refs):
-    table_ref, comb_ref = refs[11:13]
-    forward_kernel(*refs[:11], *refs[12:])
-
-    @pl.when(pl.program_id(0) == 0)
-    def _():
-        table_ref[...] = comb_ref[:, :TABLE]
 
 
 def solution(mesh):

time: 193 us -> 188 us (0.974)
  waiting for transfers between devices: 23.8 us -> 30.9 us
  Pallas kernels: 95.5 us -> 88.9 us
  local copies, waits for them, and re-layouts: 9.29 us -> 3.2 us
    ppermute x1, waiting for transfers between devices: 0.78 us -> 8.39 us  [shards(): lax.ppermute(table_grad[:, own_nodes:own_nodes + send_rows].astype(jnp.bf...]
    pallas_call x3 -> x2, Pallas kernels: 53.8 us -> 47.7 us  [the longest x1 27.1 us: shards(): pl.pallas_call(forward_kernel, grid=(chunks,), in_specs=[whole(hidden), w...]
    ppermute x9 -> x8, waiting for transfers between devices: 4.51 us -> 8.73 us  [swap(): lax.ppermute(value, 'member', [(i, i ^ flip) for i in range(lax.axis_size...]
    convert_element_type x3 -> x2, other arithmetic: 1.76 us -> 5.29 us  [add_partner(): (mine.astype(jnp.float32) + swap(other, 1).astype(jnp.float32)).astype(jn...]
    ppermute x1, waiting for transfers between devices: 2.66 us -> 0.01 us  [shards(): lax.ppermute(table_grad[:, own_nodes + send_rows:].astype(jnp.bfloat16),...]
    unnamed x28 -> x25, local copies, waits for them, and re-layouts: 4.63 us -> 2.25 us
    all_to_all x2, waiting for transfers between devices: 15.8 us -> 13.8 us  [across_space(): return lax.all_to_all(half, 'space', 0, 0, tiled=True)]
    ppermute x9 -> x8, starting transfers between devices: 12.5 us -> 11.7 us  [swap(): lax.ppermute(value, 'member', [(i, i ^ flip) for i in range(lax.axis_size...]
  transfers between devices with their start and end apart: 15 -> 14, of which waited for: 4 -> 6; matrix products, arithmetic and copies ran while one was open for 10% -> 7% of each run, Pallas kernels for 24% -> 11%
where the time goes in v6:
time: 188 us
  Pallas kernels  88.9 us (47%)
  starting transfers between devices  42.9 us (23%)
  waiting for transfers between devices  30.9 us (16%)
  other arithmetic  12.8 us (7%)
  matrix products  5.63 us (3%)
  between operations  3.29 us (2%)
  local copies, waits for them, and re-layouts  3.2 us (2%)
    pallas_call x1, Pallas kernels, shards(): pl.pallas_call(forward_kernel, grid=(chunks,), in_specs=[whole(hidden), w...  27.1 us
    pallas_call x1, Pallas kernels, shards(): pl.pallas_call(edge_slope_kernel, grid=(chunks,), in_specs=[whole(comb),...  21.1 us
    pallas_call x1, Pallas kernels, shards(): pl.pallas_call(table_kernel, grid=(width // TILE,), in_specs=[smem, whole...  20.6 us
    all_to_all x2, starting transfers between devices, across_space(): return lax.all_to_all(half, 'space', 0, 0, tiled=True)  19.4 us
    all_to_all x2, waiting for transfers between devices, across_space(): return lax.all_to_all(half, 'space', 0, 0, tiled=True)  13.8 us
    ppermute x8, starting transfers between devices, swap(): lax.ppermute(value, 'member', [(i, i ^ flip) for i in range(lax.axis_size...  11.7 us
    pallas_call x1, Pallas kernels, shards(): pl.pallas_call(node_term_kernel, grid=(width // TILE,), in_specs=[smem, s...  10.4 us
    pallas_call x1, Pallas kernels, shards(): pl.pallas_call(loss_kernel, grid=(chunks,), in_specs=[pl.BlockSpec(memory...  9.71 us
  transfers between devices with their start and end apart: 14, of which 6 were waited for; matrix products, arithmetic and copies ran while one was open for 7% of the time, Pallas kernels for 11%

profile of v6, /device:TPU:1, one launch (start us, length us, event | category | flops | bytes accessed | tf_op | source)
XLA Modules:
  0.0 187.6 jit_solution(11330016559344443865)
XLA Ops:
  0.6 1.3 fusion.11
  2.0 4.4 %collective-permute-start = (bf16[4,16,1024]{2,1,0:T(8,128)(2,1)S(1)}, bf16[4,16,1024]{2,1,0:T(8,128)(2,1)S(1)}, u32[]{:S(2)}, u32[]{:S(2)}) collective-permute-start(bf16[4,16,1024]{2,1,0:T(8,128)(2,1)S(1)} %get-tuple-element.66), channel_id=1, source_target_pairs={{0,1},{1,2},{2,3},{3,4},{4,5},{5,6},{6,7},{7,8},{8,9},{9,10},{10,1... | collective-permute-start | bytes 393224 | tf_op jit(solution)/shard_map/ppermute | solution.py:333
  6.4 1.3 collective-permute-start.1
  8.3 0.7 fusion.23
  9.0 0.8 convert_add_fusion
  9.8 0.8 add_select_fusion
  10.6 0.1 iota_compare_fusion.5
  10.8 1.3 fusion.5.pick_ref
  12.1 0.0 collective-permute-done.left_ref
  12.1 0.0 collective-permute-done.1.right_ref
  12.1 0.0 copy-start.8
  12.1 0.6 copy-done.7
  12.8 0.0 copy-done.8
  12.8 27.1 %forward.1 = (f32[4,104,512]{2,1,0:T(8,128)}, bf16[4,512,1024]{2,1,0:T(8,128)(2,1)}, bf16[4,512,1024]{2,1,0:T(8,128)(2,1)}, bf16[4,512,1024]{2,1,0:T(8,128)(2,1)...) custom-call(bf16[4,64,1024]{2,1,0:T(8,128)(2,1)} %own_ref.1, bf16[4,16,1024]{2,1,0:T(8,128)(2,1)} %copy-done.7, ...), custom_call_target="tpu_custom_call" | custom-call | tf_op jit(solution)/shard_map/forward/pallas_call | solution.py:369
  39.9 3.4 %collective-permute-start.2 = (f32[4,104,512]{2,1,0:T(8,128)}, f32[4,104,512]{2,1,0:T(8,128)S(1)}, u32[]{:S(2)}, u32[]{:S(2)}) collective-permute-start(f32[4,104,512]{2,1,0:T(8,128)} %get-tuple-element.33.own_ref), channel_id=1, source_target_pairs={{0,64},{32,96},{64,0},{96,32},{1,65},{33,97},{65,1},{97,33},{2,66}... | collective-permute-start | bytes 2555912 | tf_op jit(solution)/shard_map/ppermute | solution.py:398
  43.3 2.3 %collective-permute-start.3 = (f32[4,104,512]{2,1,0:T(8,128)}, f32[4,104,512]{2,1,0:T(8,128)S(1)}, u32[]{:S(2)}, u32[]{:S(2)}) collective-permute-start(f32[4,104,512]{2,1,0:T(8,128)} %get-tuple-element.33.own_ref), channel_id=1, source_target_pairs={{0,32},{32,0},{64,96},{96,64},{1,33},{33,1},{65,97},{97,65},{2,34}... | collective-permute-start | bytes 2555912 | tf_op jit(solution)/shard_map/ppermute | solution.py:398
  45.7 21.1 %edge_slopes.1.slope_ref = bf16[4,4,512,1024]{3,2,1,0:T(8,128)(2,1)} custom-call(bf16[4,128,1024]{2,1,0:T(8,128)(2,1)} %get-tuple-element.34.comb_ref, bf16[4,512,256]{2,1,0:T(8,128)(2,1)} %fusion.5.pick_ref, bf16[512,1024]{1,0:T(8,128)(2,1)} %grid_ref.3), custom_call_target="tpu_custom_call" | custom-call | flops 4462739456 | bytes 16777216 | tf_op jit(solution)/shard_map/edge_slopes/pallas_call | solution.py:403
  66.8 0.0 collective-permute-done.2.chip_ref
  66.8 0.0 collective-permute-done.3.core_ref
  66.8 0.0 copy-start.4
  66.8 0.1 collective-permute-start.4
  66.9 0.0 copy-done.6
  66.9 0.9 pad.9.output_ref
  67.8 0.0 copy-done.10
  67.8 0.8 broadcast_multiply_fusion.weight_ref
  68.6 0.7 collective-permute-done.4.far_ref
  69.3 0.0 copy-done.3
  69.3 0.9 copy-done.5
  70.2 9.7 %loss.1 = (bf16[4,512,128]{2,1,0:T(8,128)(2,1)}, bf16[4,512,1024]{2,1,0:T(8,128)(2,1)}, f32[1,128]{1,0:T(1,128)}) custom-call(s32[1]{0:T(128)} %bitcast.core_index_ref.core_ref, f32[4,104,512]{2,1,0:T(8,128)} %get-tuple-element.33.own_ref, f32[4,104,512]{2,1,0:T(8,128)} %copy-done.4, f32[4,104,512]{2,1,0:T(8,128)} %copy-done.3, f32[4,104,512]{2,1,0:T(8,128)} %copy-done.5, ...), custom_call_target="tpu_custom_call" | custom-call | tf_op jit(solution)/shard_map/loss/pallas_call | solution.py:423
  79.9 10.4 %node_terms.1 = (bf16[32,16,1152]{2,1,0:T(8,128)(2,1)}, bf16[32,16,1152]{2,1,0:T(8,128)(2,1)}) custom-call(s32[1]{0:T(128)} %bitcast.core_index_ref.core_ref, bf16[4,512,1024]{2,1,0:T(8,128)(2,1)} %get-tuple-element.42.summed_ref, bf16[4,512,1024]{2,1,0:T(8,128)(2,1)} %get-tuple-element.43.out_ref, bf16[4,512,1024]{2,1,0:T(8,128)(2,1)} %get-tuple-element.48.pre_ref, ...), custom_call_target="tpu_custom_call" | custom-call | flops 4296015872 | bytes 2097152 | tf_op jit(solution)/shard_map/node_terms/pallas_call | solution.py:468
  90.3 0.1 collective-permute-start.5
  90.4 0.6 copy.19
  91.0 2.3 %collective-permute-done.5 = bf16[32,16,1152]{2,1,0:T(8,128)(2,1)S(1)} collective-permute-done((bf16[32,16,1152]{2,1,0:T(8,128)(2,1)}, bf16[32,16,1152]{2,1,0:T(8,128)(2,1)S(1)}, u32[]{:S(2)}, u32[]{:S(2)}) %collective-permute-start.5) | collective-permute-done | bytes 1179680 | tf_op jit(solution)/shard_map/ppermute | solution.py:398
  93.4 2.6 %add_convert_fusion = bf16[32,16,1152]{2,1,0:T(8,128)(2,1)} fusion(bf16[32,16,1152]{2,1,0:T(8,128)(2,1)S(1)} %collective-permute-done.5, bf16[32,16,1152]{2,1,0:T(8,128)(2,1)} %get-tuple-element.46), kind=kLoop, calls=%fused_computation.3 | loop fusion | flops 2359296 | bytes 3538944 | tf_op jit(solution)/shard_map/convert_element_type | solution.py:449
  96.0 20.6 %table.1 = (f32[4,96,1024]{2,1,0:T(8,128)}, bf16[32,16,1024]{2,1,0:T(8,128)(2,1)}, bf16[32,16,1024]{2,1,0:T(8,128)(2,1)}) custom-call(s32[1]{0:T(128)} %bitcast.core_index_ref.core_ref, bf16[4,512,1024]{2,1,0:T(8,128)(2,1)} %get-tuple-element.48.pre_ref, bf16[1024,1024]{1,0:T(8,128)(2,1)} %node_ref.3, bf16[4,4,512,1024]{3,2,1,0:T(8,128)(2,1)} %edge_slopes.1.slope_ref, ...), custom_call_target="tpu_custom_call" | custom-call | flops 17196646400 | bytes 4194304 | tf_op jit(solution)/shard_map/table/pallas_call | solution.py:487
  116.6 0.2 collective-permute-start.6
  116.7 9.8 %all-to-all-start = ((bf16[32,16,1152]{2,1,0:T(8,128)(2,1)}), bf16[32,16,1152]{2,1,0:T(8,128)(2,1)S(1)}, u32[]{:S(2)}, u32[]{:S(2)}) async-start(bf16[32,16,1152]{2,1,0:T(8,128)(2,1)} %add_convert_fusion), calls=%async_computation | async-start | bytes 2359296 | tf_op jit(solution)/shard_map/all_to_all | solution.py:452
  126.5 0.0 copy-start.2
  126.5 0.0 copy-done.1
  126.5 0.1 convert.4
  126.7 1.6 collective-permute-start.7
  128.3 4.4 %collective-permute-start.8 = (bf16[4,16,1024]{2,1,0:T(8,128)(2,1)S(1)}, bf16[4,16,1024]{2,1,0:T(8,128)(2,1)}, u32[]{:S(2)}, u32[]{:S(2)}) collective-permute-start(bf16[4,16,1024]{2,1,0:T(8,128)(2,1)S(1)} %get-tuple-element.61), channel_id=1, source_target_pairs={{0,1},{1,2},{2,3},{3,4},{4,5},{5,6},{6,7},{7,8},{8,9},{9,10},{10,1... | collective-permute-start | bytes 393224 | tf_op jit(solution)/shard_map/ppermute | solution.py:515
  132.7 0.0 collective-permute-done.6
  132.7 0.0 copy-done.2
  132.7 2.7 %add_convert_fusion.1 = bf16[32,16,1024]{2,1,0:T(8,128)(2,1)} fusion(bf16[32,16,1024]{2,1,0:T(8,128)(2,1)} %collective-permute-done.6, bf16[32,16,1024]{2,1,0:T(8,128)(2,1)S(1)} %copy-done.2), kind=kLoop, calls=%fused_computation.7 | loop fusion | flops 2097152 | bytes 3145728 | tf_op jit(solution)/shard_map/convert_element_type | solution.py:449
  135.4 8.4 %collective-permute-done.7 = bf16[4,16,1024]{2,1,0:T(8,128)(2,1)S(1)} collective-permute-done((bf16[4,16,1024]{2,1,0:T(8,128)(2,1)S(1)}, bf16[4,16,1024]{2,1,0:T(8,128)(2,1)S(1)}, u32[]{:S(2)}, u32[]{:S(2)}) %collective-permute-start.7) | collective-permute-done | bytes 131104 | tf_op jit(solution)/shard_map/ppermute | solution.py:512
  143.8 0.0 collective-permute-done.8
  143.8 1.1 all-to-all-done
  144.9 9.6 %all-to-all-start.1 = ((bf16[32,16,1024]{2,1,0:T(8,128)(2,1)}), bf16[32,16,1024]{2,1,0:T(8,128)(2,1)}, u32[]{:S(2)}, u32[]{:S(2)}) async-start(bf16[32,16,1024]{2,1,0:T(8,128)(2,1)} %add_convert_fusion.1), calls=%async_computation.1 | async-start | bytes 2097152 | tf_op jit(solution)/shard_map/all_to_all | solution.py:452
  154.6 0.1 iota_compare_fusion.7
  154.6 0.2 convert_reduce_fusion
  154.8 0.3 convolution_bitcast_fusion.1
  155.2 3.2 %fusion.7 = bf16[4,64,1024]{2,1,0:T(8,128)(2,1)} fusion(bf16[1024,1024]{1,0:T(8,128)(2,1)S(1)} %copy-done, bf16[4,16,1024]{2,1,0:T(8,128)(2,1)} %collective-permute-done.8, f32[4,64,1024]{2,1,0:T(8,128)S(1)} %convolution_bitcast_fusion.1, f32[4,96,1024]{2,1,0:T(8,128)} %get-tuple-element.54, pred[2,16,64]{2,1,0:T(8,128)(4,1)S(1)} %iota_compare_fusion.7), kind=kOutput, calls=%fused_computation.15 | convolution fusion | flops 546308096 | bytes 4851712 | tf_op jit(solution)/shard_map/mnk,hk->mnh/dot_general | solution.py:531
  158.3 12.7 %all-to-all-done.1 = bf16[32,16,1024]{2,1,0:T(8,128)(2,1)} async-done(((bf16[32,16,1024]{2,1,0:T(8,128)(2,1)}), bf16[32,16,1024]{2,1,0:T(8,128)(2,1)}, u32[]{:S(2)}, u32[]{:S(2)}) %all-to-all-start.1) | async-done | bytes 1048608 | tf_op jit(solution)/shard_map/all_to_all | solution.py:452
  171.0 1.4 convert_reduce_fusion.1
  172.4 0.7 collective-permute-start.9
  173.1 2.7 %collective-permute-start.10 = (f32[16,2176]{1,0:T(8,128)S(1)}, f32[16,2176]{1,0:T(8,128)S(1)}, u32[]{:S(2)}, u32[]{:S(2)}) collective-permute-start(f32[16,2176]{1,0:T(8,128)S(1)} %pad_maximum_fusion), channel_id=1, source_target_pairs={{0,32},{32,0},{64,96},{96,64},{1,33},{33,1},{65,97},{97,65},{2,34}... | collective-permute-start | bytes 417800 | tf_op jit(solution)/shard_map/ppermute | solution.py:398
  175.8 2.3 %collective-permute-start.11 = (f32[16,2176]{1,0:T(8,128)S(1)}, f32[16,2176]{1,0:T(8,128)S(1)}, u32[]{:S(2)}, u32[]{:S(2)}) collective-permute-start(f32[16,2176]{1,0:T(8,128)S(1)} %pad_maximum_fusion), channel_id=1, source_target_pairs={{0,96},{32,64},{64,32},{96,0},{1,97},{33,65},{65,33},{97,1},{2,98}... | collective-permute-start | bytes 417800 | tf_op jit(solution)/shard_map/ppermute | solution.py:398
  178.1 0.0 collective-permute-done.9
  178.1 0.0 collective-permute-done.10
  178.1 5.7 %collective-permute-done.11 = f32[16,2176]{1,0:T(8,128)S(1)} collective-permute-done((f32[16,2176]{1,0:T(8,128)S(1)}, f32[16,2176]{1,0:T(8,128)S(1)}, u32[]{:S(2)}, u32[]{:S(2)}) %collective-permute-start.11) | collective-permute-done | bytes 139296 | tf_op jit(solution)/shard_map/ppermute | solution.py:398
  183.8 0.7 slice_multiply_fusion
  184.5 0.6 slice_multiply_fusion.2
  185.2 0.7 slice_reduce_fusion
  (22 shorter events, 0.2 us)
Async XLA Ops:
  2.0 10.1 %collective-permute-start = (bf16[4,16,1024]{2,1,0:T(8,128)(2,1)S(1)}, bf16[4,16,1024]{2,1,0:T(8,128)(2,1)S(1)}, u32[]{:S(2)}, u32[]{:S(2)}) collective-permute-start(bf16[4,16,1024]{2,1,0:T(8,128)(2,1)S(1)} %get-tuple-element.66), channel_id=1, source_target_pairs={{0,1},{1,2},{2,3},{3,4},{4,5},{5,6},{6,7},{7,8},{8,9},{9,10},{10,1... | collective-permute-start | bytes 393224 | tf_op jit(solution)/shard_map/ppermute | solution.py:333
  6.4 5.7 %collective-permute-start.1 = (bf16[4,16,1024]{2,1,0:T(8,128)(2,1)S(1)}, bf16[4,16,1024]{2,1,0:T(8,128)(2,1)S(1)}, u32[]{:S(2)}, u32[]{:S(2)}) collective-permute-start(bf16[4,16,1024]{2,1,0:T(8,128)(2,1)S(1)} %get-tuple-element.65), channel_id=1, source_target_pairs={{1,0},{2,1},{3,2},{4,3},{5,4},{6,5},{7,6},{8,7},{9,8},{10,9},{11,1... | collective-permute-start | bytes 393224 | tf_op jit(solution)/shard_map/ppermute | solution.py:334
  12.1 0.7 copy-start.7
  12.1 0.7 copy-start.8
  39.9 26.9 %collective-permute-start.2 = (f32[4,104,512]{2,1,0:T(8,128)}, f32[4,104,512]{2,1,0:T(8,128)S(1)}, u32[]{:S(2)}, u32[]{:S(2)}) collective-permute-start(f32[4,104,512]{2,1,0:T(8,128)} %get-tuple-element.33.own_ref), channel_id=1, source_target_pairs={{0,64},{32,96},{64,0},{96,32},{1,65},{33,97},{65,1},{97,33},{2,66}... | collective-permute-start | bytes 2555912 | tf_op jit(solution)/shard_map/ppermute | solution.py:398
  43.3 23.5 %collective-permute-start.3 = (f32[4,104,512]{2,1,0:T(8,128)}, f32[4,104,512]{2,1,0:T(8,128)S(1)}, u32[]{:S(2)}, u32[]{:S(2)}) collective-permute-start(f32[4,104,512]{2,1,0:T(8,128)} %get-tuple-element.33.own_ref), channel_id=1, source_target_pairs={{0,32},{32,0},{64,96},{96,64},{1,33},{33,1},{65,97},{97,65},{2,34}... | collective-permute-start | bytes 2555912 | tf_op jit(solution)/shard_map/ppermute | solution.py:398
  45.7 21.3 %copy-start.6 = (bf16[1024,100]{0,1:T(8,128)(2,1)S(1)}, bf16[1024,100]{0,1:T(8,128)(2,1)}, u32[]{:S(2)}) copy-start(bf16[1024,100]{0,1:T(8,128)(2,1)} %param.17) | copy-start | bytes 614404
  45.7 22.1 %copy-start.10 = (f32[512]{0:T(512)S(1)}, f32[512]{0:T(512)}, u32[]{:S(2)}) copy-start(f32[512]{0:T(512)} %param.20) | copy-start | bytes 6148
  45.7 22.1 %copy-start.11 = (f32[100]{0:T(128)S(1)}, f32[100]{0:T(128)}, u32[]{:S(2)}) copy-start(f32[100]{0:T(128)} %param.21) | copy-start | bytes 1204
  66.8 2.5 %copy-start.3 = (f32[4,104,512]{2,1,0:T(8,128)}, f32[4,104,512]{2,1,0:T(8,128)S(1)}, u32[]{:S(2)}) copy-start(f32[4,104,512]{2,1,0:T(8,128)S(1)} %collective-permute-done.2.chip_ref) | copy-start | bytes 2555908
  66.8 2.5 %copy-start.4 = (f32[4,104,512]{2,1,0:T(8,128)}, f32[4,104,512]{2,1,0:T(8,128)S(1)}, u32[]{:S(2)}) copy-start(f32[4,104,512]{2,1,0:T(8,128)S(1)} %collective-permute-done.3.core_ref) | copy-start | bytes 2555908
  66.8 2.5 %collective-permute-start.4 = (f32[4,104,512]{2,1,0:T(8,128)S(1)}, f32[4,104,512]{2,1,0:T(8,128)S(1)}, u32[]{:S(2)}, u32[]{:S(2)}) collective-permute-start(f32[4,104,512]{2,1,0:T(8,128)S(1)} %collective-permute-done.2.chip_ref), channel_id=1, source_target_pairs={{0,32},{32,0},{64,96},{96,64},{1,33},{33,1},{65,97},{97,65},{2,34}... | collective-permute-start | bytes 2555912 | tf_op jit(solution)/shard_map/ppermute | solution.py:398
  69.3 0.9 copy-start.5
  90.3 3.1 %collective-permute-start.5 = (bf16[32,16,1152]{2,1,0:T(8,128)(2,1)}, bf16[32,16,1152]{2,1,0:T(8,128)(2,1)S(1)}, u32[]{:S(2)}, u32[]{:S(2)}) collective-permute-start(bf16[32,16,1152]{2,1,0:T(8,128)(2,1)} %get-tuple-element.47), channel_id=1, source_target_pairs={{0,32},{32,0},{64,96},{96,64},{1,33},{33,1},{65,97},{97,65},{2,34}... | collective-permute-start | bytes 3538952 | tf_op jit(solution)/shard_map/ppermute | solution.py:398
  116.6 10.0 %copy-start.1 = (f32[4,96,1024]{2,1,0:T(8,128)S(1)}, f32[4,96,1024]{2,1,0:T(8,128)}, u32[]{:S(2)}) copy-start(f32[4,96,1024]{2,1,0:T(8,128)} %get-tuple-element.54) | copy-start | bytes 4718596
  116.6 16.2 %collective-permute-start.6 = (bf16[32,16,1024]{2,1,0:T(8,128)(2,1)}, bf16[32,16,1024]{2,1,0:T(8,128)(2,1)}, u32[]{:S(2)}, u32[]{:S(2)}) collective-permute-start(bf16[32,16,1024]{2,1,0:T(8,128)(2,1)} %get-tuple-element.52), channel_id=1, source_target_pairs={{0,32},{32,0},{64,96},{96,64},{1,33},{33,1},{65,97},{97,65},{2,34}... | collective-permute-start | bytes 3145736 | tf_op jit(solution)/shard_map/ppermute | solution.py:398
  116.7 28.2 %all-to-all-start = ((bf16[32,16,1152]{2,1,0:T(8,128)(2,1)}), bf16[32,16,1152]{2,1,0:T(8,128)(2,1)S(1)}, u32[]{:S(2)}, u32[]{:S(2)}) async-start(bf16[32,16,1152]{2,1,0:T(8,128)(2,1)} %add_convert_fusion), calls=%async_computation | async-start | bytes 2359296 | tf_op jit(solution)/shard_map/all_to_all | solution.py:452
  126.5 6.2 %copy-start.2 = (bf16[32,16,1024]{2,1,0:T(8,128)(2,1)S(1)}, bf16[32,16,1024]{2,1,0:T(8,128)(2,1)}, u32[]{:S(2)}) copy-start(bf16[32,16,1024]{2,1,0:T(8,128)(2,1)} %get-tuple-element.51) | copy-start | bytes 3145732
  126.7 17.1 %collective-permute-start.7 = (bf16[4,16,1024]{2,1,0:T(8,128)(2,1)S(1)}, bf16[4,16,1024]{2,1,0:T(8,128)(2,1)S(1)}, u32[]{:S(2)}, u32[]{:S(2)}) collective-permute-start(bf16[4,16,1024]{2,1,0:T(8,128)(2,1)S(1)} %get-tuple-element.62), channel_id=1, source_target_pairs={{1,0},{2,1},{3,2},{4,3},{5,4},{6,5},{7,6},{8,7},{9,8},{10,9},{11,1... | collective-permute-start | bytes 393224 | tf_op jit(solution)/shard_map/ppermute | solution.py:512
  128.3 15.5 %collective-permute-start.8 = (bf16[4,16,1024]{2,1,0:T(8,128)(2,1)S(1)}, bf16[4,16,1024]{2,1,0:T(8,128)(2,1)}, u32[]{:S(2)}, u32[]{:S(2)}) collective-permute-start(bf16[4,16,1024]{2,1,0:T(8,128)(2,1)S(1)} %get-tuple-element.61), channel_id=1, source_target_pairs={{0,1},{1,2},{2,3},{3,4},{4,5},{5,6},{6,7},{7,8},{8,9},{9,10},{10,1... | collective-permute-start | bytes 393224 | tf_op jit(solution)/shard_map/ppermute | solution.py:515
  132.7 21.8 %copy-start.9 = (s32[2,16]{1,0:T(2,128)S(1)}, s32[2,16]{1,0:T(2,128)}, u32[]{:S(2)}) copy-start(s32[2,16]{1,0:T(2,128)} %param.25) | copy-start | bytes 388
  135.4 19.7 %copy-start = (bf16[1024,1024]{1,0:T(8,128)(2,1)S(1)}, bf16[1024,1024]{1,0:T(8,128)(2,1)}, u32[]{:S(2)}) copy-start(bf16[1024,1024]{1,0:T(8,128)(2,1)} %project_ref.1) | copy-start | bytes 6291460
  144.9 26.1 %all-to-all-start.1 = ((bf16[32,16,1024]{2,1,0:T(8,128)(2,1)}), bf16[32,16,1024]{2,1,0:T(8,128)(2,1)}, u32[]{:S(2)}, u32[]{:S(2)}) async-start(bf16[32,16,1024]{2,1,0:T(8,128)(2,1)} %add_convert_fusion.1), calls=%async_computation.1 | async-start | bytes 2097152 | tf_op jit(solution)/shard_map/all_to_all | solution.py:452
  172.4 5.6 %collective-permute-start.9 = (f32[16,2176]{1,0:T(8,128)S(1)}, f32[16,2176]{1,0:T(8,128)S(1)}, u32[]{:S(2)}, u32[]{:S(2)}) collective-permute-start(f32[16,2176]{1,0:T(8,128)S(1)} %pad_maximum_fusion), channel_id=1, source_target_pairs={{0,64},{32,96},{64,0},{96,32},{1,65},{33,97},{65,1},{97,33},{2,66}... | collective-permute-start | bytes 417800 | tf_op jit(solution)/shard_map/ppermute | solution.py:398
  173.1 5.0 %collective-permute-start.10 = (f32[16,2176]{1,0:T(8,128)S(1)}, f32[16,2176]{1,0:T(8,128)S(1)}, u32[]{:S(2)}, u32[]{:S(2)}) collective-permute-start(f32[16,2176]{1,0:T(8,128)S(1)} %pad_maximum_fusion), channel_id=1, source_target_pairs={{0,32},{32,0},{64,96},{96,64},{1,33},{33,1},{65,97},{97,65},{2,34}... | collective-permute-start | bytes 417800 | tf_op jit(solution)/shard_map/ppermute | solution.py:398
  175.8 8.0 %collective-permute-start.11 = (f32[16,2176]{1,0:T(8,128)S(1)}, f32[16,2176]{1,0:T(8,128)S(1)}, u32[]{:S(2)}, u32[]{:S(2)}) collective-permute-start(f32[16,2176]{1,0:T(8,128)S(1)} %pad_maximum_fusion), channel_id=1, source_target_pairs={{0,96},{32,64},{64,32},{96,0},{1,97},{33,65},{65,33},{97,1},{2,98}... | collective-permute-start | bytes 417800 | tf_op jit(solution)/shard_map/ppermute | solution.py:398

commit v7 on v6

--- a/solution.py
+++ b/solution.py
@@ -507,6 +507,9 @@
         cost_estimate=cost(members * points * width, 4 * width, 8),
         name="table",
     )(core[None], pre_grad, node_weight, edge_slope, slot_row, source_columns)
+    table_grad, project_mine, project_other, node_moved = lax.optimization_barrier(
+        (table_grad, project_mine, project_other, node_moved)
+    )
     project_half = add_partner(project_mine, project_other)
 
     left_back = lax.ppermute(
@@ -515,8 +518,8 @@
     right_back = lax.ppermute(
         table_grad[:, own_nodes + send_rows :].astype(jnp.bfloat16), "space", forward
     )
-    project_half, node_moved, left_back, right_back = lax.optimization_barrier(
-        (project_half, node_moved, left_back, right_back)
+    project_half, left_back, right_back = lax.optimization_barrier(
+        (project_half, left_back, right_back)
     )
     project_moved = across_space(project_half)
     projected_grad = (

time: 188 us -> 182 us (0.968)
  waiting for transfers between devices: 30.9 us -> 24.5 us
    ppermute x1, waiting for transfers between devices: 8.39 us -> 0.44 us  [shards(): lax.ppermute(table_grad[:, own_nodes:own_nodes + send_rows].astype(jnp.bf...]
    ppermute x1, waiting for transfers between devices: 0.01 us -> 2.96 us  [shards(): lax.ppermute(table_grad[:, own_nodes + send_rows:].astype(jnp.bfloat16),...]
  transfers between devices with their start and end apart: 14 -> 14, of which waited for: 6 -> 6; matrix products, arithmetic and copies ran while one was open for 7% -> 7% of each run, Pallas kernels for 11% -> 23%
where the time goes in v7:
time: 182 us; the launch traced here: 181 us
  Pallas kernels  88.9 us (49%)
  starting transfers between devices  42.4 us (23%)
  waiting for transfers between devices  24.5 us (13%)
  other arithmetic  12.9 us (7%)
  matrix products  5.86 us (3%)
  between operations  3.3 us (2%)
  local copies, waits for them, and re-layouts  3.2 us (2%)
    pallas_call x1, Pallas kernels, shards(): pl.pallas_call(forward_kernel, grid=(chunks,), in_specs=[whole(hidden), w...  27.1 us
    pallas_call x1, Pallas kernels, shards(): pl.pallas_call(edge_slope_kernel, grid=(chunks,), in_specs=[whole(comb),...  21.1 us
    pallas_call x1, Pallas kernels, shards(): pl.pallas_call(table_kernel, grid=(width // TILE,), in_specs=[smem, whole...  20.6 us
    all_to_all x2, starting transfers between devices, across_space(): return lax.all_to_all(half, 'space', 0, 0, tiled=True)  19 us
    all_to_all x2, waiting for transfers between devices, across_space(): return lax.all_to_all(half, 'space', 0, 0, tiled=True)  12.4 us
    ppermute x8, starting transfers between devices, swap(): lax.ppermute(value, 'member', [(i, i ^ flip) for i in range(lax.axis_size...  12.2 us
    pallas_call x1, Pallas kernels, shards(): pl.pallas_call(node_term_kernel, grid=(width // TILE,), in_specs=[smem, s...  10.4 us
    pallas_call x1, Pallas kernels, shards(): pl.pallas_call(loss_kernel, grid=(chunks,), in_specs=[pl.BlockSpec(memory...  9.69 us
  transfers between devices with their start and end apart: 14, of which 6 were waited for; matrix products, arithmetic and copies ran while one was open for 7% of the time, Pallas kernels for 23%

profile of v7, /device:TPU:1, one launch (start us, length us, event | category | flops | bytes accessed | tf_op | source)
XLA Modules:
  0.0 181.1 jit_solution(10711619901692097944)
XLA Ops:
  0.6 1.3 fusion.12
  2.0 4.4 %collective-permute-start = (bf16[4,16,1024]{2,1,0:T(8,128)(2,1)S(1)}, bf16[4,16,1024]{2,1,0:T(8,128)(2,1)S(1)}, u32[]{:S(2)}, u32[]{:S(2)}) collective-permute-start(bf16[4,16,1024]{2,1,0:T(8,128)(2,1)S(1)} %get-tuple-element.72), channel_id=1, source_target_pairs={{0,1},{1,2},{2,3},{3,4},{4,5},{5,6},{6,7},{7,8},{8,9},{9,10},{10,1... | collective-permute-start | bytes 393224 | tf_op jit(solution)/shard_map/ppermute | solution.py:333
  6.4 1.3 collective-permute-start.1
  8.3 0.7 fusion.22
  9.0 0.8 convert_add_fusion
  9.8 0.8 add_select_fusion
  10.6 0.1 iota_compare_fusion.5
  10.8 1.3 fusion.5.pick_ref
  12.1 0.0 collective-permute-done.left_ref
  12.1 0.0 collective-permute-done.1.right_ref
  12.1 0.0 copy-start.7
  12.1 0.6 copy-done.6
  12.8 0.0 copy-done.7
  12.8 27.1 %forward.1 = (f32[4,104,512]{2,1,0:T(8,128)}, bf16[4,512,1024]{2,1,0:T(8,128)(2,1)}, bf16[4,512,1024]{2,1,0:T(8,128)(2,1)}, bf16[4,512,1024]{2,1,0:T(8,128)(2,1)...) custom-call(bf16[4,64,1024]{2,1,0:T(8,128)(2,1)} %own_ref.1, bf16[4,16,1024]{2,1,0:T(8,128)(2,1)} %copy-done.6, ...), custom_call_target="tpu_custom_call" | custom-call | tf_op jit(solution)/shard_map/forward/pallas_call | solution.py:369
  40.0 3.4 %collective-permute-start.2 = (f32[4,104,512]{2,1,0:T(8,128)}, f32[4,104,512]{2,1,0:T(8,128)S(1)}, u32[]{:S(2)}, u32[]{:S(2)}) collective-permute-start(f32[4,104,512]{2,1,0:T(8,128)} %get-tuple-element.36.own_ref), channel_id=1, source_target_pairs={{0,64},{32,96},{64,0},{96,32},{1,65},{33,97},{65,1},{97,33},{2,66}... | collective-permute-start | bytes 2555912 | tf_op jit(solution)/shard_map/ppermute | solution.py:398
  43.3 2.3 %collective-permute-start.3 = (f32[4,104,512]{2,1,0:T(8,128)}, f32[4,104,512]{2,1,0:T(8,128)S(1)}, u32[]{:S(2)}, u32[]{:S(2)}) collective-permute-start(f32[4,104,512]{2,1,0:T(8,128)} %get-tuple-element.36.own_ref), channel_id=1, source_target_pairs={{0,32},{32,0},{64,96},{96,64},{1,33},{33,1},{65,97},{97,65},{2,34}... | collective-permute-start | bytes 2555912 | tf_op jit(solution)/shard_map/ppermute | solution.py:398
  45.7 21.1 %edge_slopes.1.slope_ref = bf16[4,4,512,1024]{3,2,1,0:T(8,128)(2,1)} custom-call(bf16[4,128,1024]{2,1,0:T(8,128)(2,1)} %get-tuple-element.37.comb_ref, bf16[4,512,256]{2,1,0:T(8,128)(2,1)} %fusion.5.pick_ref, bf16[512,1024]{1,0:T(8,128)(2,1)} %grid_ref.3), custom_call_target="tpu_custom_call" | custom-call | flops 4462739456 | bytes 16777216 | tf_op jit(solution)/shard_map/edge_slopes/pallas_call | solution.py:403
  66.8 0.0 collective-permute-done.2.chip_ref
  66.8 0.0 collective-permute-done.3.core_ref
  66.8 0.0 copy-start.3
  66.9 0.1 collective-permute-start.4
  67.0 0.0 copy-done.5
  67.0 0.9 pad.9.output_ref
  67.8 0.0 copy-done.9
  67.8 0.0 copy-done.10
  67.8 0.8 broadcast_multiply_fusion.weight_ref
  68.6 0.7 collective-permute-done.4.far_ref
  69.3 0.0 copy-done.2
  69.3 0.9 copy-done.4
  70.2 9.7 %loss.1 = (bf16[4,512,128]{2,1,0:T(8,128)(2,1)}, bf16[4,512,1024]{2,1,0:T(8,128)(2,1)}, f32[1,128]{1,0:T(1,128)}) custom-call(s32[1]{0:T(128)} %bitcast.core_index_ref.core_ref, f32[4,104,512]{2,1,0:T(8,128)} %get-tuple-element.36.own_ref, f32[4,104,512]{2,1,0:T(8,128)} %copy-done.3, f32[4,104,512]{2,1,0:T(8,128)} %copy-done.2, f32[4,104,512]{2,1,0:T(8,128)} %copy-done.4, ...), custom_call_target="tpu_custom_call" | custom-call | tf_op jit(solution)/shard_map/loss/pallas_call | solution.py:423
  79.9 10.4 %node_terms.1 = (bf16[32,16,1152]{2,1,0:T(8,128)(2,1)}, bf16[32,16,1152]{2,1,0:T(8,128)(2,1)}) custom-call(s32[1]{0:T(128)} %bitcast.core_index_ref.core_ref, bf16[4,512,1024]{2,1,0:T(8,128)(2,1)} %get-tuple-element.45.summed_ref, bf16[4,512,1024]{2,1,0:T(8,128)(2,1)} %get-tuple-element.46.out_ref, bf16[4,512,1024]{2,1,0:T(8,128)(2,1)} %get-tuple-element.51.pre_ref, ...), custom_call_target="tpu_custom_call" | custom-call | flops 4296015872 | bytes 2097152 | tf_op jit(solution)/shard_map/node_terms/pallas_call | solution.py:468
  90.3 0.1 collective-permute-start.5
  90.4 0.6 copy.19
  91.0 2.3 %collective-permute-done.5 = bf16[32,16,1152]{2,1,0:T(8,128)(2,1)S(1)} collective-permute-done((bf16[32,16,1152]{2,1,0:T(8,128)(2,1)}, bf16[32,16,1152]{2,1,0:T(8,128)(2,1)S(1)}, u32[]{:S(2)}, u32[]{:S(2)}) %collective-permute-start.5) | collective-permute-done | bytes 1179680 | tf_op jit(solution)/shard_map/ppermute | solution.py:398
  93.4 2.6 %add_convert_fusion = bf16[32,16,1152]{2,1,0:T(8,128)(2,1)} fusion(bf16[32,16,1152]{2,1,0:T(8,128)(2,1)S(1)} %collective-permute-done.5, bf16[32,16,1152]{2,1,0:T(8,128)(2,1)} %get-tuple-element.49), kind=kLoop, calls=%fused_computation.3 | loop fusion | flops 2359296 | bytes 3538944 | tf_op jit(solution)/shard_map/convert_element_type | solution.py:449
  96.0 9.6 %all-to-all-start = ((bf16[32,16,1152]{2,1,0:T(8,128)(2,1)}), bf16[32,16,1152]{2,1,0:T(8,128)(2,1)S(1)}, u32[]{:S(2)}, u32[]{:S(2)}) async-start(bf16[32,16,1152]{2,1,0:T(8,128)(2,1)} %add_convert_fusion), calls=%async_computation | async-start | bytes 2359296 | tf_op jit(solution)/shard_map/all_to_all | solution.py:452
  105.7 20.6 %table.1 = (f32[4,96,1024]{2,1,0:T(8,128)}, bf16[32,16,1024]{2,1,0:T(8,128)(2,1)}, bf16[32,16,1024]{2,1,0:T(8,128)(2,1)}) custom-call(s32[1]{0:T(128)} %bitcast.core_index_ref.core_ref, bf16[4,512,1024]{2,1,0:T(8,128)(2,1)} %get-tuple-element.51.pre_ref, bf16[1024,1024]{1,0:T(8,128)(2,1)} %node_ref.3, bf16[4,4,512,1024]{3,2,1,0:T(8,128)(2,1)} %edge_slopes.1.slope_ref, ...), custom_call_target="tpu_custom_call" | custom-call | flops 17196646400 | bytes 4194304 | tf_op jit(solution)/shard_map/table/pallas_call | solution.py:487
  126.2 0.0 all-to-all-done
  126.3 0.5 collective-permute-start.6
  126.8 1.5 convert.4
  128.3 1.5 collective-permute-start.7
  129.8 0.0 copy-start.8
  129.9 4.0 %collective-permute-start.8 = (bf16[4,16,1024]{2,1,0:T(8,128)(2,1)S(1)}, bf16[4,16,1024]{2,1,0:T(8,128)(2,1)S(1)}, u32[]{:S(2)}, u32[]{:S(2)}) collective-permute-start(bf16[4,16,1024]{2,1,0:T(8,128)(2,1)S(1)} %get-tuple-element.67), channel_id=1, source_target_pairs={{0,1},{1,2},{2,3},{3,4},{4,5},{5,6},{6,7},{7,8},{8,9},{9,10},{10,1... | collective-permute-start | bytes 393224 | tf_op jit(solution)/shard_map/ppermute | solution.py:518
  133.9 0.0 collective-permute-done.6
  133.9 1.4 add_convert_fusion.1
  135.3 0.4 collective-permute-done.7
  135.7 3.0 %collective-permute-done.8 = bf16[4,16,1024]{2,1,0:T(8,128)(2,1)S(1)} collective-permute-done((bf16[4,16,1024]{2,1,0:T(8,128)(2,1)S(1)}, bf16[4,16,1024]{2,1,0:T(8,128)(2,1)S(1)}, u32[]{:S(2)}, u32[]{:S(2)}) %collective-permute-start.8) | collective-permute-done | bytes 131104 | tf_op jit(solution)/shard_map/ppermute | solution.py:518
  138.7 9.3 %all-to-all-start.1 = ((bf16[32,16,1024]{2,1,0:T(8,128)(2,1)}), bf16[32,16,1024]{2,1,0:T(8,128)(2,1)}, u32[]{:S(2)}, u32[]{:S(2)}) async-start(bf16[32,16,1024]{2,1,0:T(8,128)(2,1)} %add_convert_fusion.1), calls=%async_computation.1 | async-start | bytes 2097152 | tf_op jit(solution)/shard_map/all_to_all | solution.py:452
  148.1 0.1 iota_compare_fusion.7
  148.1 0.2 convert_reduce_fusion
  148.3 0.0 copy-done
  148.3 0.4 fusion.7
  148.7 3.4 %fusion.8 = bf16[4,64,1024]{2,1,0:T(8,128)(2,1)} fusion(bf16[1024,1024]{1,0:T(8,128)(2,1)} %project_ref.1, f32[4,64,1024]{2,1,0:T(8,128)S(1)} %fusion.7, bf16[4,16,1024]{2,1,0:T(8,128)(2,1)S(1)} %collective-permute-done.8, pred[2,16,64]{2,1,0:T(8,128)(4,1)S(1)} %iota_compare_fusion.7), kind=kOutput, calls=%fused_computation.16 | convolution fusion | flops 546045952 | bytes 3803136 | tf_op jit(solution)/shard_map/mnk,hk->mnh/dot_general | solution.py:534
  152.1 12.4 %all-to-all-done.1 = bf16[32,16,1024]{2,1,0:T(8,128)(2,1)} async-done(((bf16[32,16,1024]{2,1,0:T(8,128)(2,1)}), bf16[32,16,1024]{2,1,0:T(8,128)(2,1)}, u32[]{:S(2)}, u32[]{:S(2)}) %all-to-all-start.1) | async-done | bytes 1048608 | tf_op jit(solution)/shard_map/all_to_all | solution.py:452
  164.4 1.4 convert_reduce_fusion.1
  165.8 0.7 collective-permute-start.9
  166.5 2.8 %collective-permute-start.10 = (f32[16,2176]{1,0:T(8,128)S(1)}, f32[16,2176]{1,0:T(8,128)S(1)}, u32[]{:S(2)}, u32[]{:S(2)}) collective-permute-start(f32[16,2176]{1,0:T(8,128)S(1)} %pad_maximum_fusion), channel_id=1, source_target_pairs={{0,32},{32,0},{64,96},{96,64},{1,33},{33,1},{65,97},{97,65},{2,34}... | collective-permute-start | bytes 417800 | tf_op jit(solution)/shard_map/ppermute | solution.py:398
  169.3 2.3 %collective-permute-start.11 = (f32[16,2176]{1,0:T(8,128)S(1)}, f32[16,2176]{1,0:T(8,128)S(1)}, u32[]{:S(2)}, u32[]{:S(2)}) collective-permute-start(f32[16,2176]{1,0:T(8,128)S(1)} %pad_maximum_fusion), channel_id=1, source_target_pairs={{0,96},{32,64},{64,32},{96,0},{1,97},{33,65},{65,33},{97,1},{2,98}... | collective-permute-start | bytes 417800 | tf_op jit(solution)/shard_map/ppermute | solution.py:398
  171.6 0.0 collective-permute-done.9
  171.6 0.0 collective-permute-done.10
  171.6 5.7 %collective-permute-done.11 = f32[16,2176]{1,0:T(8,128)S(1)} collective-permute-done((f32[16,2176]{1,0:T(8,128)S(1)}, f32[16,2176]{1,0:T(8,128)S(1)}, u32[]{:S(2)}, u32[]{:S(2)}) %collective-permute-start.11) | collective-permute-done | bytes 139296 | tf_op jit(solution)/shard_map/ppermute | solution.py:398
  177.3 0.7 slice_multiply_fusion
  178.1 0.6 slice_multiply_fusion.2
  178.7 0.7 slice_reduce_fusion
  (20 shorter events, 0.2 us)
Async XLA Ops:
  2.0 10.1 %collective-permute-start = (bf16[4,16,1024]{2,1,0:T(8,128)(2,1)S(1)}, bf16[4,16,1024]{2,1,0:T(8,128)(2,1)S(1)}, u32[]{:S(2)}, u32[]{:S(2)}) collective-permute-start(bf16[4,16,1024]{2,1,0:T(8,128)(2,1)S(1)} %get-tuple-element.72), channel_id=1, source_target_pairs={{0,1},{1,2},{2,3},{3,4},{4,5},{5,6},{6,7},{7,8},{8,9},{9,10},{10,1... | collective-permute-start | bytes 393224 | tf_op jit(solution)/shard_map/ppermute | solution.py:333
  6.4 5.7 %collective-permute-start.1 = (bf16[4,16,1024]{2,1,0:T(8,128)(2,1)S(1)}, bf16[4,16,1024]{2,1,0:T(8,128)(2,1)S(1)}, u32[]{:S(2)}, u32[]{:S(2)}) collective-permute-start(bf16[4,16,1024]{2,1,0:T(8,128)(2,1)S(1)} %get-tuple-element.71), channel_id=1, source_target_pairs={{1,0},{2,1},{3,2},{4,3},{5,4},{6,5},{7,6},{8,7},{9,8},{10,9},{11,1... | collective-permute-start | bytes 393224 | tf_op jit(solution)/shard_map/ppermute | solution.py:334
  12.1 0.7 copy-start.6
  12.1 0.7 copy-start.7
  40.0 26.9 %collective-permute-start.2 = (f32[4,104,512]{2,1,0:T(8,128)}, f32[4,104,512]{2,1,0:T(8,128)S(1)}, u32[]{:S(2)}, u32[]{:S(2)}) collective-permute-start(f32[4,104,512]{2,1,0:T(8,128)} %get-tuple-element.36.own_ref), channel_id=1, source_target_pairs={{0,64},{32,96},{64,0},{96,32},{1,65},{33,97},{65,1},{97,33},{2,66}... | collective-permute-start | bytes 2555912 | tf_op jit(solution)/shard_map/ppermute | solution.py:398
  43.3 23.5 %collective-permute-start.3 = (f32[4,104,512]{2,1,0:T(8,128)}, f32[4,104,512]{2,1,0:T(8,128)S(1)}, u32[]{:S(2)}, u32[]{:S(2)}) collective-permute-start(f32[4,104,512]{2,1,0:T(8,128)} %get-tuple-element.36.own_ref), channel_id=1, source_target_pairs={{0,32},{32,0},{64,96},{96,64},{1,33},{33,1},{65,97},{97,65},{2,34}... | collective-permute-start | bytes 2555912 | tf_op jit(solution)/shard_map/ppermute | solution.py:398
  45.7 21.3 %copy-start.5 = (bf16[1024,100]{0,1:T(8,128)(2,1)S(1)}, bf16[1024,100]{0,1:T(8,128)(2,1)}, u32[]{:S(2)}) copy-start(bf16[1024,100]{0,1:T(8,128)(2,1)} %param.17) | copy-start | bytes 614404
  45.7 22.2 %copy-start.9 = (f32[512]{0:T(512)S(1)}, f32[512]{0:T(512)}, u32[]{:S(2)}) copy-start(f32[512]{0:T(512)} %param.20) | copy-start | bytes 6148
  45.7 22.2 %copy-start.10 = (f32[100]{0:T(128)S(1)}, f32[100]{0:T(128)}, u32[]{:S(2)}) copy-start(f32[100]{0:T(128)} %param.21) | copy-start | bytes 1204
  66.8 2.5 %copy-start.2 = (f32[4,104,512]{2,1,0:T(8,128)}, f32[4,104,512]{2,1,0:T(8,128)S(1)}, u32[]{:S(2)}) copy-start(f32[4,104,512]{2,1,0:T(8,128)S(1)} %collective-permute-done.2.chip_ref) | copy-start | bytes 2555908
  66.8 2.5 %copy-start.3 = (f32[4,104,512]{2,1,0:T(8,128)}, f32[4,104,512]{2,1,0:T(8,128)S(1)}, u32[]{:S(2)}) copy-start(f32[4,104,512]{2,1,0:T(8,128)S(1)} %collective-permute-done.3.core_ref) | copy-start | bytes 2555908
  66.9 2.5 %collective-permute-start.4 = (f32[4,104,512]{2,1,0:T(8,128)S(1)}, f32[4,104,512]{2,1,0:T(8,128)S(1)}, u32[]{:S(2)}, u32[]{:S(2)}) collective-permute-start(f32[4,104,512]{2,1,0:T(8,128)S(1)} %collective-permute-done.2.chip_ref), channel_id=1, source_target_pairs={{0,32},{32,0},{64,96},{96,64},{1,33},{33,1},{65,97},{97,65},{2,34}... | collective-permute-start | bytes 2555912 | tf_op jit(solution)/shard_map/ppermute | solution.py:398
  69.3 0.9 copy-start.4
  90.3 3.1 %collective-permute-start.5 = (bf16[32,16,1152]{2,1,0:T(8,128)(2,1)}, bf16[32,16,1152]{2,1,0:T(8,128)(2,1)S(1)}, u32[]{:S(2)}, u32[]{:S(2)}) collective-permute-start(bf16[32,16,1152]{2,1,0:T(8,128)(2,1)} %get-tuple-element.50), channel_id=1, source_target_pairs={{0,32},{32,0},{64,96},{96,64},{1,33},{33,1},{65,97},{97,65},{2,34}... | collective-permute-start | bytes 3538952 | tf_op jit(solution)/shard_map/ppermute | solution.py:398
  96.0 30.2 %all-to-all-start = ((bf16[32,16,1152]{2,1,0:T(8,128)(2,1)}), bf16[32,16,1152]{2,1,0:T(8,128)(2,1)S(1)}, u32[]{:S(2)}, u32[]{:S(2)}) async-start(bf16[32,16,1152]{2,1,0:T(8,128)(2,1)} %add_convert_fusion), calls=%async_computation | async-start | bytes 2359296 | tf_op jit(solution)/shard_map/all_to_all | solution.py:452
  126.2 7.7 %copy-start.1 = (bf16[32,16,1024]{2,1,0:T(8,128)(2,1)S(1)}, bf16[32,16,1024]{2,1,0:T(8,128)(2,1)}, u32[]{:S(2)}) copy-start(bf16[32,16,1024]{2,1,0:T(8,128)(2,1)} %get-tuple-element.58) | copy-start | bytes 3145732
  126.3 7.7 %collective-permute-start.6 = (bf16[32,16,1024]{2,1,0:T(8,128)(2,1)}, bf16[32,16,1024]{2,1,0:T(8,128)(2,1)S(1)}, u32[]{:S(2)}, u32[]{:S(2)}) collective-permute-start(bf16[32,16,1024]{2,1,0:T(8,128)(2,1)} %get-tuple-element.59), channel_id=1, source_target_pairs={{0,32},{32,0},{64,96},{96,64},{1,33},{33,1},{65,97},{97,65},{2,34}... | collective-permute-start | bytes 3145736 | tf_op jit(solution)/shard_map/ppermute | solution.py:398
  128.3 7.4 %collective-permute-start.7 = (bf16[4,16,1024]{2,1,0:T(8,128)(2,1)S(1)}, bf16[4,16,1024]{2,1,0:T(8,128)(2,1)S(1)}, u32[]{:S(2)}, u32[]{:S(2)}) collective-permute-start(bf16[4,16,1024]{2,1,0:T(8,128)(2,1)S(1)} %get-tuple-element.68), channel_id=1, source_target_pairs={{1,0},{2,1},{3,2},{4,3},{5,4},{6,5},{7,6},{8,7},{9,8},{10,9},{11,1... | collective-permute-start | bytes 393224 | tf_op jit(solution)/shard_map/ppermute | solution.py:515
  129.8 18.2 %copy-start.8 = (s32[2,16]{1,0:T(2,128)S(1)}, s32[2,16]{1,0:T(2,128)}, u32[]{:S(2)}) copy-start(s32[2,16]{1,0:T(2,128)} %param.25) | copy-start | bytes 388
  129.9 8.8 %collective-permute-start.8 = (bf16[4,16,1024]{2,1,0:T(8,128)(2,1)S(1)}, bf16[4,16,1024]{2,1,0:T(8,128)(2,1)S(1)}, u32[]{:S(2)}, u32[]{:S(2)}) collective-permute-start(bf16[4,16,1024]{2,1,0:T(8,128)(2,1)S(1)} %get-tuple-element.67), channel_id=1, source_target_pairs={{0,1},{1,2},{2,3},{3,4},{4,5},{5,6},{6,7},{7,8},{8,9},{9,10},{10,1... | collective-permute-start | bytes 393224 | tf_op jit(solution)/shard_map/ppermute | solution.py:518
  135.3 13.0 %copy-start = (f32[4,96,1024]{2,1,0:T(8,128)S(1)}, f32[4,96,1024]{2,1,0:T(8,128)}, u32[]{:S(2)}) copy-start(f32[4,96,1024]{2,1,0:T(8,128)} %get-tuple-element.60) | copy-start | bytes 4718596
  138.7 25.7 %all-to-all-start.1 = ((bf16[32,16,1024]{2,1,0:T(8,128)(2,1)}), bf16[32,16,1024]{2,1,0:T(8,128)(2,1)}, u32[]{:S(2)}, u32[]{:S(2)}) async-start(bf16[32,16,1024]{2,1,0:T(8,128)(2,1)} %add_convert_fusion.1), calls=%async_computation.1 | async-start | bytes 2097152 | tf_op jit(solution)/shard_map/all_to_all | solution.py:452
  165.8 5.7 %collective-permute-start.9 = (f32[16,2176]{1,0:T(8,128)S(1)}, f32[16,2176]{1,0:T(8,128)S(1)}, u32[]{:S(2)}, u32[]{:S(2)}) collective-permute-start(f32[16,2176]{1,0:T(8,128)S(1)} %pad_maximum_fusion), channel_id=1, source_target_pairs={{0,64},{32,96},{64,0},{96,32},{1,65},{33,97},{65,1},{97,33},{2,66}... | collective-permute-start | bytes 417800 | tf_op jit(solution)/shard_map/ppermute | solution.py:398
  166.5 5.1 %collective-permute-start.10 = (f32[16,2176]{1,0:T(8,128)S(1)}, f32[16,2176]{1,0:T(8,128)S(1)}, u32[]{:S(2)}, u32[]{:S(2)}) collective-permute-start(f32[16,2176]{1,0:T(8,128)S(1)} %pad_maximum_fusion), channel_id=1, source_target_pairs={{0,32},{32,0},{64,96},{96,64},{1,33},{33,1},{65,97},{97,65},{2,34}... | collective-permute-start | bytes 417800 | tf_op jit(solution)/shard_map/ppermute | solution.py:398
  169.3 8.0 %collective-permute-start.11 = (f32[16,2176]{1,0:T(8,128)S(1)}, f32[16,2176]{1,0:T(8,128)S(1)}, u32[]{:S(2)}, u32[]{:S(2)}) collective-permute-start(f32[16,2176]{1,0:T(8,128)S(1)} %pad_maximum_fusion), channel_id=1, source_target_pairs={{0,96},{32,64},{64,32},{96,0},{1,97},{33,65},{65,33},{97,1},{2,98}... | collective-permute-start | bytes 417800 | tf_op jit(solution)/shard_map/ppermute | solution.py:398

commit v8 on v7

--- a/solution.py
+++ b/solution.py
@@ -245,20 +245,24 @@
 def node_term_kernel(
     core_ref, summed_ref, out_ref, pre_ref, grad_ref, loss_ref, mine_ref, other_ref,
 ):
-    members, _, width = pre_ref.shape
+    width = pre_ref.shape[2]
     core = core_ref[0]
-    node = sum(dot_tn(summed_ref[m], pre_ref[m]) for m in range(members))
+    def flat(ref):
+        return ref[...].reshape(ref.shape[0] * ref.shape[1], ref.shape[2])
+
+    node = dot_tn(flat(summed_ref), flat(pre_ref))
     split_rows(node, core, mine_ref, other_ref, slice(0, width))
-    output = sum(dot_tn(out_ref[m], grad_ref[m]) for m in range(members)) + loss_ref[...]
+    output = dot_tn(flat(out_ref), flat(grad_ref)) + loss_ref[...]
     split_rows(output, core, mine_ref, other_ref, slice(width, width + TABLE))
 
 
 def table_kernel(
-    core_ref, pre_ref, node_ref, slope_ref, slot_ref, rows_ref, grad_ref, mine_ref, other_ref,
-    place_ref,
+    core_ref, pre_ref, node_ref, slope_ref, slot_ref, rows_ref,
+    own_ref, left_ref, right_ref, mine_ref, other_ref, place_ref,
 ):
-    members, points, _ = pre_ref.shape
-    table_rows = grad_ref.shape[1]
+    members, points, width = pre_ref.shape
+    own_nodes, send_rows = own_ref.shape[1], left_ref.shape[1]
+    table_rows = own_nodes + 2 * send_rows
 
     @pl.when(pl.program_id(0) == 0)
     def _():
@@ -268,15 +272,20 @@
             picked = jnp.where(slot_ref[:, columns] == row, 1.0, 0.0)
             place_ref[:, columns] = picked.astype(jnp.bfloat16)
 
+    summed_grads = dot_nt(pre_ref[...].reshape(members * points, width), node_ref[...])
+    summed_grads = summed_grads.astype(jnp.bfloat16)
     cast = []
     for m in range(members):
-        summed_grad = dot_nt(pre_ref[m], node_ref[...]).astype(jnp.bfloat16)
+        summed_grad = summed_grads[m * points : (m + 1) * points]
         table = sum(
             dot(place_ref[:, k * points : (k + 1) * points], summed_grad * slope_ref[m, k])
             for k in range(DEGREE)
         )[:table_rows]
-        grad_ref[m] = table
-        cast.append(table.astype(jnp.bfloat16))
+        own_ref[m] = table[:own_nodes]
+        rounded = table.astype(jnp.bfloat16)
+        left_ref[m] = rounded[own_nodes : own_nodes + send_rows]
+        right_ref[m] = rounded[own_nodes + send_rows :]
+        cast.append(rounded)
     term = dot(rows_ref[...], jnp.concatenate(cast, axis=0))
     split_rows(term, core_ref[0], mine_ref, other_ref, slice(0, term.shape[1]))
 
@@ -483,8 +492,10 @@
     pre_grad, node_half = lax.optimization_barrier((node_pre_grad, node_half))
     node_moved = across_space(node_half)
     columns = pl.BlockSpec((space, own_rows, TILE), lambda c: (0, 0, c))
+    halo_columns = pl.BlockSpec((members, send_rows, TILE), lambda c: (0, 0, c))
+    halo_shape = jax.ShapeDtypeStruct((members, send_rows, width), jnp.bfloat16)
     columns_shape = jax.ShapeDtypeStruct((space, own_rows, width), jnp.bfloat16)
-    table_grad, project_mine, project_other = pl.pallas_call(
+    own_grad, left_grad, right_grad, project_mine, project_other = pl.pallas_call(
         table_kernel,
         grid=(width // TILE,),
         in_specs=[
@@ -496,10 +507,11 @@
             whole(source_columns),
         ],
         out_specs=[
-            pl.BlockSpec((members, table_rows, TILE), lambda c: (0, 0, c)), columns, columns,
+            pl.BlockSpec((members, own_nodes, TILE), lambda c: (0, 0, c)), halo_columns,
+            halo_columns, columns, columns,
         ],
         out_shape=[
-            jax.ShapeDtypeStruct((members, table_rows, width), jnp.float32),
+            jax.ShapeDtypeStruct((members, own_nodes, width), jnp.float32), halo_shape, halo_shape,
             columns_shape, columns_shape,
         ],
         scratch_shapes=[pltpu.VMEM((TABLE, DEGREE * points), jnp.bfloat16)],
@@ -507,23 +519,19 @@
         cost_estimate=cost(members * points * width, 4 * width, 8),
         name="table",
     )(core[None], pre_grad, node_weight, edge_slope, slot_row, source_columns)
-    table_grad, project_mine, project_other, node_moved = lax.optimization_barrier(
-        (table_grad, project_mine, project_other, node_moved)
+    left_grad, right_grad, project_mine, project_other, node_moved = lax.optimization_barrier(
+        (left_grad, right_grad, project_mine, project_other, node_moved)
     )
     project_half = add_partner(project_mine, project_other)
 
-    left_back = lax.ppermute(
-        table_grad[:, own_nodes : own_nodes + send_rows].astype(jnp.bfloat16), "space", backward
-    )
-    right_back = lax.ppermute(
-        table_grad[:, own_nodes + send_rows :].astype(jnp.bfloat16), "space", forward
-    )
+    left_back = lax.ppermute(left_grad, "space", backward)
+    right_back = lax.ppermute(right_grad, "space", forward)
     project_half, left_back, right_back = lax.optimization_barrier(
         (project_half, left_back, right_back)
     )
     project_moved = across_space(project_half)
     projected_grad = (
-        table_grad[:, :own_nodes]
+        own_grad
         + jnp.einsum(
             "sn,msh->mnh", chosen[1], left_back, preferred_element_type=jnp.float32
         )

time: 182 us -> 179 us (0.984)
  waiting for transfers between devices: 24.5 us -> 21.1 us
  starting transfers between devices: 42.4 us -> 44.5 us
  Pallas kernels: 88.9 us -> 87 us
    ppermute x2, waiting for transfers between devices: 3.39 us -> 0.55 us  [the longest x1 0.55 us: shards(): right_back = lax.ppermute(right_grad, 'space', forward)]
    pallas_call x1, Pallas kernels: 20.6 us -> 18.6 us  [shards(): pl.pallas_call(table_kernel, grid=(width // TILE,), in_specs=[smem, whole...]
  transfers between devices with their start and end apart: 14 -> 14, of which waited for: 6 -> 5; matrix products, arithmetic and copies ran while one was open for 7% -> 7% of each run, Pallas kernels for 23% -> 22%
where the time goes in v8:
time: 179 us; the launch traced here: 178 us
  Pallas kernels  87 us (49%)
  starting transfers between devices  44.5 us (25%)
  waiting for transfers between devices  21.1 us (12%)
  other arithmetic  12.6 us (7%)
  matrix products  6.49 us (4%)
  between operations  3.25 us (2%)
  local copies, waits for them, and re-layouts  3.15 us (2%)
    pallas_call x1, Pallas kernels, shards(): pl.pallas_call(forward_kernel, grid=(chunks,), in_specs=[whole(hidden), w...  27.2 us
    pallas_call x1, Pallas kernels, shards(): pl.pallas_call(edge_slope_kernel, grid=(chunks,), in_specs=[whole(comb),...  21.2 us
    all_to_all x2, starting transfers between devices, across_space(): return lax.all_to_all(half, 'space', 0, 0, tiled=True)  19.5 us
    pallas_call x1, Pallas kernels, shards(): pl.pallas_call(table_kernel, grid=(width // TILE,), in_specs=[smem, whole...  18.6 us
    ppermute x8, starting transfers between devices, swap(): lax.ppermute(value, 'member', [(i, i ^ flip) for i in range(lax.axis_size...  13.2 us
    all_to_all x2, waiting for transfers between devices, across_space(): return lax.all_to_all(half, 'space', 0, 0, tiled=True)  11.8 us
    pallas_call x1, Pallas kernels, shards(): pl.pallas_call(node_term_kernel, grid=(width // TILE,), in_specs=[smem, s...  10.4 us
    pallas_call x1, Pallas kernels, shards(): pl.pallas_call(loss_kernel, grid=(chunks,), in_specs=[pl.BlockSpec(memory...  9.7 us
  transfers between devices with their start and end apart: 14, of which 5 were waited for; matrix products, arithmetic and copies ran while one was open for 7% of the time, Pallas kernels for 22%

profile of v8, /device:TPU:1, one launch (start us, length us, event | category | flops | bytes accessed | tf_op | source)
XLA Modules:
  0.0 178.1 jit_solution(2269211743088527133)
XLA Ops:
  0.6 1.3 fusion.9
  2.0 4.4 %collective-permute-start = (bf16[4,16,1024]{2,1,0:T(8,128)(2,1)S(1)}, bf16[4,16,1024]{2,1,0:T(8,128)(2,1)S(1)}, u32[]{:S(2)}, u32[]{:S(2)}) collective-permute-start(bf16[4,16,1024]{2,1,0:T(8,128)(2,1)S(1)} %get-tuple-element.76), channel_id=1, source_target_pairs={{0,1},{1,2},{2,3},{3,4},{4,5},{5,6},{6,7},{7,8},{8,9},{9,10},{10,1... | collective-permute-start | bytes 393224 | tf_op jit(solution)/shard_map/ppermute | solution.py:342
  6.4 1.3 collective-permute-start.1
  8.3 0.7 fusion.19
  9.0 0.8 convert_add_fusion
  9.8 0.8 add_select_fusion
  10.6 0.1 iota_compare_fusion.5
  10.8 1.3 fusion.5.pick_ref
  12.1 0.0 collective-permute-done.left_ref
  12.1 0.0 collective-permute-done.1.right_ref
  12.1 0.0 copy-start.6
  12.1 0.6 copy-done.5
  12.7 0.0 copy-done.6
  12.8 27.2 %forward.1 = (f32[4,104,512]{2,1,0:T(8,128)}, bf16[4,512,1024]{2,1,0:T(8,128)(2,1)}, bf16[4,512,1024]{2,1,0:T(8,128)(2,1)}, bf16[4,512,1024]{2,1,0:T(8,128)(2,1)...) custom-call(bf16[4,64,1024]{2,1,0:T(8,128)(2,1)} %own_ref.1, bf16[4,16,1024]{2,1,0:T(8,128)(2,1)} %copy-done.5, ...), custom_call_target="tpu_custom_call" | custom-call | tf_op jit(solution)/shard_map/forward/pallas_call | solution.py:378
  40.0 3.4 %collective-permute-start.2 = (f32[4,104,512]{2,1,0:T(8,128)}, f32[4,104,512]{2,1,0:T(8,128)S(1)}, u32[]{:S(2)}, u32[]{:S(2)}) collective-permute-start(f32[4,104,512]{2,1,0:T(8,128)} %get-tuple-element.39.own_ref), channel_id=1, source_target_pairs={{0,64},{32,96},{64,0},{96,32},{1,65},{33,97},{65,1},{97,33},{2,66}... | collective-permute-start | bytes 2555912 | tf_op jit(solution)/shard_map/ppermute | solution.py:407
  43.3 2.3 %collective-permute-start.3 = (f32[4,104,512]{2,1,0:T(8,128)}, f32[4,104,512]{2,1,0:T(8,128)S(1)}, u32[]{:S(2)}, u32[]{:S(2)}) collective-permute-start(f32[4,104,512]{2,1,0:T(8,128)} %get-tuple-element.39.own_ref), channel_id=1, source_target_pairs={{0,32},{32,0},{64,96},{96,64},{1,33},{33,1},{65,97},{97,65},{2,34}... | collective-permute-start | bytes 2555912 | tf_op jit(solution)/shard_map/ppermute | solution.py:407
  45.7 21.2 %edge_slopes.1.slope_ref = bf16[4,4,512,1024]{3,2,1,0:T(8,128)(2,1)} custom-call(bf16[4,128,1024]{2,1,0:T(8,128)(2,1)} %get-tuple-element.40.comb_ref, bf16[4,512,256]{2,1,0:T(8,128)(2,1)} %fusion.5.pick_ref, bf16[512,1024]{1,0:T(8,128)(2,1)} %grid_ref.3), custom_call_target="tpu_custom_call" | custom-call | flops 4462739456 | bytes 16777216 | tf_op jit(solution)/shard_map/edge_slopes/pallas_call | solution.py:412
  66.8 0.0 collective-permute-done.2.chip_ref
  66.8 0.0 collective-permute-done.3.core_ref
  66.9 0.0 copy-start.2
  66.9 0.1 collective-permute-start.4
  67.0 0.0 copy-done.4
  67.0 0.9 pad.9.output_ref
  67.9 0.0 copy-done.8
  67.9 0.0 copy-done.9
  67.9 0.8 broadcast_multiply_fusion.weight_ref
  68.6 0.7 collective-permute-done.4.far_ref
  69.3 0.0 copy-done.1
  69.3 0.0 copy-done.2
  69.3 0.9 copy-done.3
  70.2 9.7 %loss.1 = (bf16[4,512,128]{2,1,0:T(8,128)(2,1)}, bf16[4,512,1024]{2,1,0:T(8,128)(2,1)}, f32[1,128]{1,0:T(1,128)}) custom-call(s32[1]{0:T(128)} %bitcast.core_index_ref.core_ref, f32[4,104,512]{2,1,0:T(8,128)} %get-tuple-element.39.own_ref, f32[4,104,512]{2,1,0:T(8,128)} %copy-done.2, f32[4,104,512]{2,1,0:T(8,128)} %copy-done.1, f32[4,104,512]{2,1,0:T(8,128)} %copy-done.3, ...), custom_call_target="tpu_custom_call" | custom-call | tf_op jit(solution)/shard_map/loss/pallas_call | solution.py:432
  79.9 10.4 %node_terms.1 = (bf16[32,16,1152]{2,1,0:T(8,128)(2,1)}, bf16[32,16,1152]{2,1,0:T(8,128)(2,1)}) custom-call(s32[1]{0:T(128)} %bitcast.core_index_ref.core_ref, bf16[4,512,1024]{2,1,0:T(8,128)(2,1)} %get-tuple-element.48.summed_ref, bf16[4,512,1024]{2,1,0:T(8,128)(2,1)} %get-tuple-element.49.out_ref, bf16[4,512,1024]{2,1,0:T(8,128)(2,1)} %get-tuple-element.54.pre_ref, ...), custom_call_target="tpu_custom_call" | custom-call | flops 4296015872 | bytes 2097152 | tf_op jit(solution)/shard_map/node_terms/pallas_call | solution.py:477
  90.3 0.1 collective-permute-start.5
  90.4 0.6 copy.19
  91.1 2.3 %collective-permute-done.5 = bf16[32,16,1152]{2,1,0:T(8,128)(2,1)S(1)} collective-permute-done((bf16[32,16,1152]{2,1,0:T(8,128)(2,1)}, bf16[32,16,1152]{2,1,0:T(8,128)(2,1)S(1)}, u32[]{:S(2)}, u32[]{:S(2)}) %collective-permute-start.5) | collective-permute-done | bytes 1179680 | tf_op jit(solution)/shard_map/ppermute | solution.py:407
  93.4 2.6 %add_convert_fusion = bf16[32,16,1152]{2,1,0:T(8,128)(2,1)} fusion(bf16[32,16,1152]{2,1,0:T(8,128)(2,1)S(1)} %collective-permute-done.5, bf16[32,16,1152]{2,1,0:T(8,128)(2,1)} %get-tuple-element.52), kind=kLoop, calls=%fused_computation.3 | loop fusion | flops 2359296 | bytes 3538944 | tf_op jit(solution)/shard_map/convert_element_type | solution.py:458
  96.0 9.6 %all-to-all-start = ((bf16[32,16,1152]{2,1,0:T(8,128)(2,1)}), bf16[32,16,1152]{2,1,0:T(8,128)(2,1)S(1)}, u32[]{:S(2)}, u32[]{:S(2)}) async-start(bf16[32,16,1152]{2,1,0:T(8,128)(2,1)} %add_convert_fusion), calls=%async_computation | async-start | bytes 2359296 | tf_op jit(solution)/shard_map/all_to_all | solution.py:461
  105.7 18.6 %table.1 = (f32[4,64,1024]{2,1,0:T(8,128)}, bf16[4,16,1024]{2,1,0:T(8,128)(2,1)}, bf16[4,16,1024]{2,1,0:T(8,128)(2,1)}, bf16[32,16,1024]{2,1,0:T(8,128)(2,1)}, bf16[32,16,1024]{2,1,0:T(8,128)(2,1)}) custom-call(s32[1]{0:T(128)} %bitcast.core_index_ref.core_ref, bf16[4,512,1024]{2,1,0:T(8,128)(2,1)} %get-tuple-element.54.pre_ref, ...), custom_call_target="tpu_custom_call" | custom-call | flops 17196646400 | bytes 4194304 | tf_op jit(solution)/shard_map/table/pallas_call | solution.py:498
  124.3 0.0 all-to-all-done
  124.3 1.6 collective-permute-start.6
  125.9 1.5 collective-permute-start.7
  127.4 4.7 %collective-permute-start.8 = (bf16[4,16,1024]{2,1,0:T(8,128)(2,1)}, bf16[4,16,1024]{2,1,0:T(8,128)(2,1)}, u32[]{:S(2)}, u32[]{:S(2)}) collective-permute-start(bf16[4,16,1024]{2,1,0:T(8,128)(2,1)} %get-tuple-element.65), channel_id=1, source_target_pairs={{0,1},{1,2},{2,3},{3,4},{4,5},{5,6},{6,7},{7,8},{8,9},{9,10},{10,1... | collective-permute-start | bytes 393224 | tf_op jit(solution)/shard_map/ppermute | solution.py:528
  132.0 0.0 collective-permute-done.6
  132.0 2.6 %add_convert_fusion.1 = bf16[32,16,1024]{2,1,0:T(8,128)(2,1)} fusion(bf16[32,16,1024]{2,1,0:T(8,128)(2,1)S(1)} %collective-permute-done.6, bf16[32,16,1024]{2,1,0:T(8,128)(2,1)} %get-tuple-element.62), kind=kLoop, calls=%fused_computation.7 | loop fusion | flops 2097152 | bytes 3145728 | tf_op jit(solution)/shard_map/convert_element_type | solution.py:458
  134.6 0.0 collective-permute-done.7
  134.6 0.5 collective-permute-done.8
  135.2 9.9 %all-to-all-start.1 = ((bf16[32,16,1024]{2,1,0:T(8,128)(2,1)}), bf16[32,16,1024]{2,1,0:T(8,128)(2,1)}, u32[]{:S(2)}, u32[]{:S(2)}) async-start(bf16[32,16,1024]{2,1,0:T(8,128)(2,1)} %add_convert_fusion.1), calls=%async_computation.1 | async-start | bytes 2097152 | tf_op jit(solution)/shard_map/all_to_all | solution.py:461
  145.1 0.0 copy-done.7
  145.1 0.1 iota_compare_fusion.7
  145.2 0.2 convert_reduce_fusion
  145.3 1.2 convolution_bitcast_fusion
  146.6 0.0 copy-done
  146.6 3.1 %fusion.6 = bf16[4,64,1024]{2,1,0:T(8,128)(2,1)} fusion(bf16[1024,1024]{1,0:T(8,128)(2,1)S(1)} %copy-done, f32[4,64,1024]{2,1,0:T(8,128)S(1)} %convolution_bitcast_fusion, f32[4,64,1024]{2,1,0:T(8,128)} %get-tuple-element.67, bf16[4,16,1024]{2,1,0:T(8,128)(2,1)S(1)} %collective-permute-done.7, pred[2,16,64]{2,1,0:T(8,128)(4,1)S(1)} %iota_compare_fusion.7), kind=kOutput, calls=%fused_computation.14 | convolution fusion | flops 546308096 | bytes 4851712 | tf_op jit(solution)/shard_map/mnk,hk->mnh/dot_general | solution.py:542
  149.7 11.8 %all-to-all-done.1 = bf16[32,16,1024]{2,1,0:T(8,128)(2,1)} async-done(((bf16[32,16,1024]{2,1,0:T(8,128)(2,1)}), bf16[32,16,1024]{2,1,0:T(8,128)(2,1)}, u32[]{:S(2)}, u32[]{:S(2)}) %all-to-all-start.1) | async-done | bytes 1048608 | tf_op jit(solution)/shard_map/all_to_all | solution.py:461
  161.5 1.4 convert_reduce_fusion.1
  162.9 0.7 collective-permute-start.9
  163.6 2.7 %collective-permute-start.10 = (f32[16,2176]{1,0:T(8,128)S(1)}, f32[16,2176]{1,0:T(8,128)S(1)}, u32[]{:S(2)}, u32[]{:S(2)}) collective-permute-start(f32[16,2176]{1,0:T(8,128)S(1)} %pad_maximum_fusion), channel_id=1, source_target_pairs={{0,32},{32,0},{64,96},{96,64},{1,33},{33,1},{65,97},{97,65},{2,34}... | collective-permute-start | bytes 417800 | tf_op jit(solution)/shard_map/ppermute | solution.py:407
  166.3 2.3 %collective-permute-start.11 = (f32[16,2176]{1,0:T(8,128)S(1)}, f32[16,2176]{1,0:T(8,128)S(1)}, u32[]{:S(2)}, u32[]{:S(2)}) collective-permute-start(f32[16,2176]{1,0:T(8,128)S(1)} %pad_maximum_fusion), channel_id=1, source_target_pairs={{0,96},{32,64},{64,32},{96,0},{1,97},{33,65},{65,33},{97,1},{2,98}... | collective-permute-start | bytes 417800 | tf_op jit(solution)/shard_map/ppermute | solution.py:407
  168.6 0.0 collective-permute-done.9
  168.6 0.0 collective-permute-done.10
  168.6 5.7 %collective-permute-done.11 = f32[16,2176]{1,0:T(8,128)S(1)} collective-permute-done((f32[16,2176]{1,0:T(8,128)S(1)}, f32[16,2176]{1,0:T(8,128)S(1)}, u32[]{:S(2)}, u32[]{:S(2)}) %collective-permute-start.11) | collective-permute-done | bytes 139296 | tf_op jit(solution)/shard_map/ppermute | solution.py:407
  174.4 0.7 slice_multiply_fusion
  175.1 0.6 slice_multiply_fusion.2
  175.7 0.7 slice_reduce_fusion
  (16 shorter events, 0.2 us)
Async XLA Ops:
  2.0 10.1 %collective-permute-start = (bf16[4,16,1024]{2,1,0:T(8,128)(2,1)S(1)}, bf16[4,16,1024]{2,1,0:T(8,128)(2,1)S(1)}, u32[]{:S(2)}, u32[]{:S(2)}) collective-permute-start(bf16[4,16,1024]{2,1,0:T(8,128)(2,1)S(1)} %get-tuple-element.76), channel_id=1, source_target_pairs={{0,1},{1,2},{2,3},{3,4},{4,5},{5,6},{6,7},{7,8},{8,9},{9,10},{10,1... | collective-permute-start | bytes 393224 | tf_op jit(solution)/shard_map/ppermute | solution.py:342
  6.4 5.7 %collective-permute-start.1 = (bf16[4,16,1024]{2,1,0:T(8,128)(2,1)S(1)}, bf16[4,16,1024]{2,1,0:T(8,128)(2,1)S(1)}, u32[]{:S(2)}, u32[]{:S(2)}) collective-permute-start(bf16[4,16,1024]{2,1,0:T(8,128)(2,1)S(1)} %get-tuple-element.75), channel_id=1, source_target_pairs={{1,0},{2,1},{3,2},{4,3},{5,4},{6,5},{7,6},{8,7},{9,8},{10,9},{11,1... | collective-permute-start | bytes 393224 | tf_op jit(solution)/shard_map/ppermute | solution.py:343
  12.1 0.7 copy-start.5
  12.1 0.7 copy-start.6
  40.0 26.9 %collective-permute-start.2 = (f32[4,104,512]{2,1,0:T(8,128)}, f32[4,104,512]{2,1,0:T(8,128)S(1)}, u32[]{:S(2)}, u32[]{:S(2)}) collective-permute-start(f32[4,104,512]{2,1,0:T(8,128)} %get-tuple-element.39.own_ref), channel_id=1, source_target_pairs={{0,64},{32,96},{64,0},{96,32},{1,65},{33,97},{65,1},{97,33},{2,66}... | collective-permute-start | bytes 2555912 | tf_op jit(solution)/shard_map/ppermute | solution.py:407
  43.3 23.5 %collective-permute-start.3 = (f32[4,104,512]{2,1,0:T(8,128)}, f32[4,104,512]{2,1,0:T(8,128)S(1)}, u32[]{:S(2)}, u32[]{:S(2)}) collective-permute-start(f32[4,104,512]{2,1,0:T(8,128)} %get-tuple-element.39.own_ref), channel_id=1, source_target_pairs={{0,32},{32,0},{64,96},{96,64},{1,33},{33,1},{65,97},{97,65},{2,34}... | collective-permute-start | bytes 2555912 | tf_op jit(solution)/shard_map/ppermute | solution.py:407
  45.7 21.3 %copy-start.4 = (bf16[1024,100]{0,1:T(8,128)(2,1)S(1)}, bf16[1024,100]{0,1:T(8,128)(2,1)}, u32[]{:S(2)}) copy-start(bf16[1024,100]{0,1:T(8,128)(2,1)} %param.17) | copy-start | bytes 614404
  45.7 22.2 %copy-start.8 = (f32[512]{0:T(512)S(1)}, f32[512]{0:T(512)}, u32[]{:S(2)}) copy-start(f32[512]{0:T(512)} %param.20) | copy-start | bytes 6148
  45.7 22.2 %copy-start.9 = (f32[100]{0:T(128)S(1)}, f32[100]{0:T(128)}, u32[]{:S(2)}) copy-start(f32[100]{0:T(128)} %param.21) | copy-start | bytes 1204
  66.8 2.5 %copy-start.1 = (f32[4,104,512]{2,1,0:T(8,128)}, f32[4,104,512]{2,1,0:T(8,128)S(1)}, u32[]{:S(2)}) copy-start(f32[4,104,512]{2,1,0:T(8,128)S(1)} %collective-permute-done.2.chip_ref) | copy-start | bytes 2555908
  66.9 2.5 %copy-start.2 = (f32[4,104,512]{2,1,0:T(8,128)}, f32[4,104,512]{2,1,0:T(8,128)S(1)}, u32[]{:S(2)}) copy-start(f32[4,104,512]{2,1,0:T(8,128)S(1)} %collective-permute-done.3.core_ref) | copy-start | bytes 2555908
  66.9 2.5 %collective-permute-start.4 = (f32[4,104,512]{2,1,0:T(8,128)S(1)}, f32[4,104,512]{2,1,0:T(8,128)S(1)}, u32[]{:S(2)}, u32[]{:S(2)}) collective-permute-start(f32[4,104,512]{2,1,0:T(8,128)S(1)} %collective-permute-done.2.chip_ref), channel_id=1, source_target_pairs={{0,32},{32,0},{64,96},{96,64},{1,33},{33,1},{65,97},{97,65},{2,34}... | collective-permute-start | bytes 2555912 | tf_op jit(solution)/shard_map/ppermute | solution.py:407
  69.3 0.9 copy-start.3
  90.3 3.1 %collective-permute-start.5 = (bf16[32,16,1152]{2,1,0:T(8,128)(2,1)}, bf16[32,16,1152]{2,1,0:T(8,128)(2,1)S(1)}, u32[]{:S(2)}, u32[]{:S(2)}) collective-permute-start(bf16[32,16,1152]{2,1,0:T(8,128)(2,1)} %get-tuple-element.53), channel_id=1, source_target_pairs={{0,32},{32,0},{64,96},{96,64},{1,33},{33,1},{65,97},{97,65},{2,34}... | collective-permute-start | bytes 3538952 | tf_op jit(solution)/shard_map/ppermute | solution.py:407
  96.0 28.3 %all-to-all-start = ((bf16[32,16,1152]{2,1,0:T(8,128)(2,1)}), bf16[32,16,1152]{2,1,0:T(8,128)(2,1)S(1)}, u32[]{:S(2)}, u32[]{:S(2)}) async-start(bf16[32,16,1152]{2,1,0:T(8,128)(2,1)} %add_convert_fusion), calls=%async_computation | async-start | bytes 2359296 | tf_op jit(solution)/shard_map/all_to_all | solution.py:461
  124.3 20.8 %copy-start.7 = (s32[2,16]{1,0:T(2,128)S(1)}, s32[2,16]{1,0:T(2,128)}, u32[]{:S(2)}) copy-start(s32[2,16]{1,0:T(2,128)} %param.25) | copy-start | bytes 388
  124.3 7.7 %collective-permute-start.6 = (bf16[32,16,1024]{2,1,0:T(8,128)(2,1)}, bf16[32,16,1024]{2,1,0:T(8,128)(2,1)S(1)}, u32[]{:S(2)}, u32[]{:S(2)}) collective-permute-start(bf16[32,16,1024]{2,1,0:T(8,128)(2,1)} %get-tuple-element.63), channel_id=1, source_target_pairs={{0,32},{32,0},{64,96},{96,64},{1,33},{33,1},{65,97},{97,65},{2,34}... | collective-permute-start | bytes 3145736 | tf_op jit(solution)/shard_map/ppermute | solution.py:407
  125.9 8.8 %collective-permute-start.7 = (bf16[4,16,1024]{2,1,0:T(8,128)(2,1)}, bf16[4,16,1024]{2,1,0:T(8,128)(2,1)S(1)}, u32[]{:S(2)}, u32[]{:S(2)}) collective-permute-start(bf16[4,16,1024]{2,1,0:T(8,128)(2,1)} %get-tuple-element.64), channel_id=1, source_target_pairs={{1,0},{2,1},{3,2},{4,3},{5,4},{6,5},{7,6},{8,7},{9,8},{10,9},{11,1... | collective-permute-start | bytes 393224 | tf_op jit(solution)/shard_map/ppermute | solution.py:527
  127.4 7.8 %collective-permute-start.8 = (bf16[4,16,1024]{2,1,0:T(8,128)(2,1)}, bf16[4,16,1024]{2,1,0:T(8,128)(2,1)}, u32[]{:S(2)}, u32[]{:S(2)}) collective-permute-start(bf16[4,16,1024]{2,1,0:T(8,128)(2,1)} %get-tuple-element.65), channel_id=1, source_target_pairs={{0,1},{1,2},{2,3},{3,4},{4,5},{5,6},{6,7},{7,8},{8,9},{9,10},{10,1... | collective-permute-start | bytes 393224 | tf_op jit(solution)/shard_map/ppermute | solution.py:528
  134.6 11.9 %copy-start = (bf16[1024,1024]{1,0:T(8,128)(2,1)S(1)}, bf16[1024,1024]{1,0:T(8,128)(2,1)}, u32[]{:S(2)}) copy-start(bf16[1024,1024]{1,0:T(8,128)(2,1)} %project_ref.1) | copy-start | bytes 6291460
  135.2 26.3 %all-to-all-start.1 = ((bf16[32,16,1024]{2,1,0:T(8,128)(2,1)}), bf16[32,16,1024]{2,1,0:T(8,128)(2,1)}, u32[]{:S(2)}, u32[]{:S(2)}) async-start(bf16[32,16,1024]{2,1,0:T(8,128)(2,1)} %add_convert_fusion.1), calls=%async_computation.1 | async-start | bytes 2097152 | tf_op jit(solution)/shard_map/all_to_all | solution.py:461
  162.9 5.7 %collective-permute-start.9 = (f32[16,2176]{1,0:T(8,128)S(1)}, f32[16,2176]{1,0:T(8,128)S(1)}, u32[]{:S(2)}, u32[]{:S(2)}) collective-permute-start(f32[16,2176]{1,0:T(8,128)S(1)} %pad_maximum_fusion), channel_id=1, source_target_pairs={{0,64},{32,96},{64,0},{96,32},{1,65},{33,97},{65,1},{97,33},{2,66}... | collective-permute-start | bytes 417800 | tf_op jit(solution)/shard_map/ppermute | solution.py:407
  163.6 5.0 %collective-permute-start.10 = (f32[16,2176]{1,0:T(8,128)S(1)}, f32[16,2176]{1,0:T(8,128)S(1)}, u32[]{:S(2)}, u32[]{:S(2)}) collective-permute-start(f32[16,2176]{1,0:T(8,128)S(1)} %pad_maximum_fusion), channel_id=1, source_target_pairs={{0,32},{32,0},{64,96},{96,64},{1,33},{33,1},{65,97},{97,65},{2,34}... | collective-permute-start | bytes 417800 | tf_op jit(solution)/shard_map/ppermute | solution.py:407
  166.3 8.0 %collective-permute-start.11 = (f32[16,2176]{1,0:T(8,128)S(1)}, f32[16,2176]{1,0:T(8,128)S(1)}, u32[]{:S(2)}, u32[]{:S(2)}) collective-permute-start(f32[16,2176]{1,0:T(8,128)S(1)} %pad_maximum_fusion), channel_id=1, source_target_pairs={{0,96},{32,64},{64,32},{96,0},{1,97},{33,65},{65,33},{97,1},{2,98}... | collective-permute-start | bytes 417800 | tf_op jit(solution)/shard_map/ppermute | solution.py:407

commit v9 on v8

--- a/solution.py
+++ b/solution.py
@@ -19,6 +19,7 @@
 PART = 32
 PIECES = 1
 VMEM_LIMIT = 56 * 1024 * 1024
+BACKWARD_VMEM_LIMIT = 46 * 1024 * 1024
 LANES = 128
 
 
@@ -290,9 +291,9 @@
     split_rows(term, core_ref[0], mine_ref, other_ref, slice(0, term.shape[1]))
 
 
-def params():
+def params(limit=VMEM_LIMIT):
     return pltpu.CompilerParams(
-        dimension_semantics=("arbitrary",), vmem_limit_bytes=VMEM_LIMIT
+        dimension_semantics=("arbitrary",), vmem_limit_bytes=limit
     )
 
 
@@ -447,7 +448,7 @@
         scratch_shapes=[
             pltpu.VMEM((members, TABLE, CHUNK), jnp.float32), pltpu.VMEM((1, CHUNK), jnp.float32),
         ],
-        compiler_params=params(),
+        compiler_params=params(BACKWARD_VMEM_LIMIT),
         name="loss",
     )(core[None], pred, core_pred, chip_pred, far_pred, target, weight_map, node_slope, output_padded)
 
@@ -483,7 +484,7 @@
         ],
         out_specs=[terms_block, terms_block],
         out_shape=[terms_shape, terms_shape],
-        compiler_params=params(),
+        compiler_params=params(BACKWARD_VMEM_LIMIT),
         cost_estimate=cost(width * width, members * points, 1),
         name="node_terms",
     )(core[None], summed, node_out, node_pre_grad, grad_rows, loss_row)
@@ -515,7 +516,7 @@
             columns_shape, columns_shape,
         ],
         scratch_shapes=[pltpu.VMEM((TABLE, DEGREE * points), jnp.bfloat16)],
-        compiler_params=params(),
+        compiler_params=params(BACKWARD_VMEM_LIMIT),
         cost_estimate=cost(members * points * width, 4 * width, 8),
         name="table",
     )(core[None], pre_grad, node_weight, edge_slope, slot_row, source_columns)

time: 179 us -> 177 us (0.989)
  Pallas kernels: 87 us -> 84.5 us
  waiting for transfers between devices: 21.1 us -> 23.3 us
  other arithmetic: 12.6 us -> 10.6 us
    convert_element_type x2, other arithmetic: 5.25 us -> 2.69 us  [add_partner(): (mine.astype(jnp.float32) + swap(other, 1).astype(jnp.float32)).astype(jn...]
    ppermute x1, waiting for transfers between devices: 0.55 us -> 2.92 us  [shards(): right_back = lax.ppermute(right_grad, 'space', forward)]
    all_to_all x2, waiting for transfers between devices: 11.8 us -> 9.63 us  [across_space(): return lax.all_to_all(half, 'space', 0, 0, tiled=True)]
    ppermute x8, waiting for transfers between devices: 8.71 us -> 10.7 us  [swap(): lax.ppermute(value, 'member', [(i, i ^ flip) for i in range(lax.axis_size...]
    unnamed x21 -> x31, local copies, waits for them, and re-layouts: 2.2 us -> 3.79 us
where the time goes in v9:
time: 177 us; the launch traced here: 176 us
  Pallas kernels  84.5 us (48%)
  starting transfers between devices  43 us (24%)
  waiting for transfers between devices  23.3 us (13%)
  other arithmetic  10.6 us (6%)
  matrix products  7.43 us (4%)
  local copies, waits for them, and re-layouts  3.89 us (2%)
  between operations  3.31 us (2%)
    pallas_call x1, Pallas kernels, shards(): pl.pallas_call(forward_kernel, grid=(chunks,), in_specs=[whole(hidden), w...  27.2 us
    pallas_call x1, Pallas kernels, shards(): pl.pallas_call(edge_slope_kernel, grid=(chunks,), in_specs=[whole(comb),...  21.2 us
    all_to_all x2, starting transfers between devices, across_space(): return lax.all_to_all(half, 'space', 0, 0, tiled=True)  19.3 us
    pallas_call x1, Pallas kernels, shards(): pl.pallas_call(table_kernel, grid=(width // TILE,), in_specs=[smem, whole...  17.6 us
    ppermute x8, starting transfers between devices, swap(): lax.ppermute(value, 'member', [(i, i ^ flip) for i in range(lax.axis_size...  12.1 us
    ppermute x8, waiting for transfers between devices, swap(): lax.ppermute(value, 'member', [(i, i ^ flip) for i in range(lax.axis_size...  10.7 us
    all_to_all x2, waiting for transfers between devices, across_space(): return lax.all_to_all(half, 'space', 0, 0, tiled=True)  9.63 us
    pallas_call x1, Pallas kernels, shards(): pl.pallas_call(loss_kernel, grid=(chunks,), in_specs=[pl.BlockSpec(memory...  9.33 us
  transfers between devices with their start and end apart: 14, of which 5 were waited for; matrix products, arithmetic and copies ran while one was open for 7% of the time, Pallas kernels for 22%

profile of v9, /device:TPU:1, one launch (start us, length us, event | category | flops | bytes accessed | tf_op | source)
XLA Modules:
  0.0 176.1 jit_solution(10262969232571936772)
XLA Ops:
  0.6 1.3 fusion.9
  2.0 4.4 %collective-permute-start = (bf16[4,16,1024]{2,1,0:T(8,128)(2,1)S(1)}, bf16[4,16,1024]{2,1,0:T(8,128)(2,1)S(1)}, u32[]{:S(2)}, u32[]{:S(2)}) collective-permute-start(bf16[4,16,1024]{2,1,0:T(8,128)(2,1)S(1)} %get-tuple-element.76), channel_id=1, source_target_pairs={{0,1},{1,2},{2,3},{3,4},{4,5},{5,6},{6,7},{7,8},{8,9},{9,10},{10,1... | collective-permute-start | bytes 393224 | tf_op jit(solution)/shard_map/ppermute | solution.py:343
  6.4 1.3 collective-permute-start.1
  8.3 0.7 fusion.19
  9.0 0.8 convert_add_fusion
  9.8 0.8 add_select_fusion
  10.6 0.1 iota_compare_fusion.5
  10.8 1.3 fusion.5.pick_ref
  12.1 0.0 collective-permute-done.left_ref
  12.1 0.0 collective-permute-done.1.right_ref
  12.1 0.6 copy-done.10
  12.7 0.0 copy-done.11
  12.8 27.2 %forward.1 = (f32[4,104,512]{2,1,0:T(8,128)}, bf16[4,512,1024]{2,1,0:T(8,128)(2,1)}, bf16[4,512,1024]{2,1,0:T(8,128)(2,1)}, bf16[4,512,1024]{2,1,0:T(8,128)(2,1)...) custom-call(bf16[4,64,1024]{2,1,0:T(8,128)(2,1)} %own_ref.1, bf16[4,16,1024]{2,1,0:T(8,128)(2,1)} %copy-done.10, ...), custom_call_target="tpu_custom_call" | custom-call | tf_op jit(solution)/shard_map/forward/pallas_call | solution.py:379
  39.9 3.4 %collective-permute-start.2 = (f32[4,104,512]{2,1,0:T(8,128)}, f32[4,104,512]{2,1,0:T(8,128)S(1)}, u32[]{:S(2)}, u32[]{:S(2)}) collective-permute-start(f32[4,104,512]{2,1,0:T(8,128)} %get-tuple-element.39.own_ref), channel_id=1, source_target_pairs={{0,64},{32,96},{64,0},{96,32},{1,65},{33,97},{65,1},{97,33},{2,66}... | collective-permute-start | bytes 2555912 | tf_op jit(solution)/shard_map/ppermute | solution.py:408
  43.3 2.4 %collective-permute-start.3 = (f32[4,104,512]{2,1,0:T(8,128)}, f32[4,104,512]{2,1,0:T(8,128)S(1)}, u32[]{:S(2)}, u32[]{:S(2)}) collective-permute-start(f32[4,104,512]{2,1,0:T(8,128)} %get-tuple-element.39.own_ref), channel_id=1, source_target_pairs={{0,32},{32,0},{64,96},{96,64},{1,33},{33,1},{65,97},{97,65},{2,34}... | collective-permute-start | bytes 2555912 | tf_op jit(solution)/shard_map/ppermute | solution.py:408
  45.7 0.0 copy-start.4
  45.7 21.2 %edge_slopes.1.slope_ref = bf16[4,4,512,1024]{3,2,1,0:T(8,128)(2,1)} custom-call(bf16[4,128,1024]{2,1,0:T(8,128)(2,1)} %get-tuple-element.40.comb_ref, bf16[4,512,256]{2,1,0:T(8,128)(2,1)} %fusion.5.pick_ref, bf16[512,1024]{1,0:T(8,128)(2,1)} %grid_ref.3), custom_call_target="tpu_custom_call" | custom-call | flops 4462739456 | bytes 16777216 | tf_op jit(solution)/shard_map/edge_slopes/pallas_call | solution.py:413
  66.9 0.0 collective-permute-done.2.chip_ref
  66.9 0.0 collective-permute-done.3.core_ref
  66.9 0.1 collective-permute-start.4
  67.0 0.0 copy-done.9
  67.0 0.0 copy-done.13
  67.1 0.0 copy-done.14
  67.1 0.1 broadcast_multiply_fusion.weight_ref
  67.2 2.3 %collective-permute-done.4.far_ref = f32[4,104,512]{2,1,0:T(8,128)} collective-permute-done((f32[4,104,512]{2,1,0:T(8,128)S(1)}, f32[4,104,512]{2,1,0:T(8,128)}, u32[]{:S(2)}, u32[]{:S(2)}) %collective-permute-start.4) | collective-permute-done | bytes 852000 | tf_op jit(solution)/shard_map/ppermute | solution.py:408
  69.5 0.0 copy-done.4
  69.5 9.3 %loss.1 = (bf16[4,512,128]{2,1,0:T(8,128)(2,1)S(1)}, bf16[4,512,1024]{2,1,0:T(8,128)(2,1)}, f32[1,128]{1,0:T(1,128)S(1)}) custom-call(s32[1]{0:T(128)} %bitcast.core_index_ref.core_ref, f32[4,104,512]{2,1,0:T(8,128)S(1)} %copy-done.3, f32[4,104,512]{2,1,0:T(8,128)S(1)} %collective-permute-done.3.core_ref, ...), custom_call_target="tpu_custom_call" | custom-call | tf_op jit(solution)/shard_map/loss/pallas_call | solution.py:433
  78.8 9.2 %node_terms.1 = (bf16[32,16,1152]{2,1,0:T(8,128)(2,1)S(1)}, bf16[32,16,1152]{2,1,0:T(8,128)(2,1)S(1)}) custom-call(s32[1]{0:T(128)} %bitcast.core_index_ref.core_ref, bf16[4,512,1024]{2,1,0:T(8,128)(2,1)S(1)} %copy-done.5, bf16[4,512,1024]{2,1,0:T(8,128)(2,1)} %get-tuple-element.49.out_ref, bf16[4,512,1024]{2,1,0:T(8,128)(2,1)} %get-tuple-element.54.pre_ref, ...), custom_call_target="tpu_custom_call" | custom-call | flops 4296015872 | bytes 2097152 | tf_op jit(solution)/shard_map/node_terms/pallas_call | solution.py:478
  88.1 0.2 collective-permute-start.5
  88.3 2.7 %collective-permute-done.5 = bf16[32,16,1152]{2,1,0:T(8,128)(2,1)S(1)} collective-permute-done((bf16[32,16,1152]{2,1,0:T(8,128)(2,1)S(1)}, bf16[32,16,1152]{2,1,0:T(8,128)(2,1)S(1)}, u32[]{:S(2)}, u32[]{:S(2)}) %collective-permute-start.5) | collective-permute-done | bytes 1179680 | tf_op jit(solution)/shard_map/ppermute | solution.py:408
  91.0 1.3 add_convert_fusion
  92.3 9.8 %all-to-all-start = ((bf16[32,16,1152]{2,1,0:T(8,128)(2,1)}), bf16[32,16,1152]{2,1,0:T(8,128)(2,1)}, u32[]{:S(2)}, u32[]{:S(2)}) async-start(bf16[32,16,1152]{2,1,0:T(8,128)(2,1)} %add_convert_fusion), calls=%async_computation | async-start | bytes 2359296 | tf_op jit(solution)/shard_map/all_to_all | solution.py:462
  102.0 0.0 copy-done
  102.1 0.0 copy-start.7
  102.1 1.1 copy-done.7
  103.2 17.6 %table.1 = (f32[4,64,1024]{2,1,0:T(8,128)S(1)}, bf16[4,16,1024]{2,1,0:T(8,128)(2,1)S(1)}, bf16[4,16,1024]{2,1,0:T(8,128)(2,1)S(1)}, bf16[32,16,1024]{2,1,0:T(8,128)(2,1)S(1)}, bf16[32,16,1024]{2,1,0:T(8,128)(2,1)S(1)}) custom-call(s32[1]{0:T(128)} %bitcast.core_index_ref.core_ref, bf16[4,512,1024]{2,1,0:T(8,128)(2,1)} %get-tuple-element.54.pre_ref, ...), custom_call_target="tpu_custom_call" | custom-call | flops 17196646400 | bytes 4194304 | tf_op jit(solution)/shard_map/table/pallas_call | solution.py:499
  120.8 0.0 copy-start.1
  120.8 1.0 copy-done.1
  121.8 1.0 copy-done.6
  122.8 0.0 all-to-all-done
  122.8 0.4 collective-permute-start.6
  123.2 1.3 collective-permute-start.7
  124.5 4.7 %collective-permute-start.8 = (bf16[4,16,1024]{2,1,0:T(8,128)(2,1)S(1)}, bf16[4,16,1024]{2,1,0:T(8,128)(2,1)}, u32[]{:S(2)}, u32[]{:S(2)}) collective-permute-start(bf16[4,16,1024]{2,1,0:T(8,128)(2,1)S(1)} %get-tuple-element.65), channel_id=1, source_target_pairs={{0,1},{1,2},{2,3},{3,4},{4,5},{5,6},{6,7},{7,8},{8,9},{9,10},{10,1... | collective-permute-start | bytes 393224 | tf_op jit(solution)/shard_map/ppermute | solution.py:529
  129.1 0.0 collective-permute-done.6
  129.2 1.4 add_convert_fusion.1
  130.5 0.0 collective-permute-done.7
  130.6 2.9 %collective-permute-done.8 = bf16[4,16,1024]{2,1,0:T(8,128)(2,1)} collective-permute-done((bf16[4,16,1024]{2,1,0:T(8,128)(2,1)S(1)}, bf16[4,16,1024]{2,1,0:T(8,128)(2,1)}, u32[]{:S(2)}, u32[]{:S(2)}) %collective-permute-start.8) | collective-permute-done | bytes 131104 | tf_op jit(solution)/shard_map/ppermute | solution.py:529
  133.5 9.5 %all-to-all-start.1 = ((bf16[32,16,1024]{2,1,0:T(8,128)(2,1)}), bf16[32,16,1024]{2,1,0:T(8,128)(2,1)}, u32[]{:S(2)}, u32[]{:S(2)}) async-start(bf16[32,16,1024]{2,1,0:T(8,128)(2,1)} %add_convert_fusion.1), calls=%async_computation.1 | async-start | bytes 2097152 | tf_op jit(solution)/shard_map/all_to_all | solution.py:462
  143.0 0.0 copy-done.12
  143.0 0.1 iota_compare_fusion.7
  143.1 1.4 convert_reduce_fusion
  144.5 2.2 %convolution_bitcast_fusion = f32[4,64,1024]{2,1,0:T(8,128)} fusion(bf16[4,16,1024]{2,1,0:T(8,128)(2,1)} %collective-permute-done.8, pred[2,16,64]{2,1,0:T(8,128)(4,1)S(1)} %iota_compare_fusion.7), kind=kOutput, calls=%fused_computation.12 | convolution fusion | flops 8388608 | bytes 1181696 | tf_op jit(solution)/shard_map/sn,msh->mnh/dot_general | solution.py:539
  146.7 3.1 %fusion.6 = bf16[4,64,1024]{2,1,0:T(8,128)(2,1)} fusion(bf16[1024,1024]{1,0:T(8,128)(2,1)S(1)} %copy-done.8, f32[4,64,1024]{2,1,0:T(8,128)} %convolution_bitcast_fusion, f32[4,64,1024]{2,1,0:T(8,128)S(1)} %copy-done.2, bf16[4,16,1024]{2,1,0:T(8,128)(2,1)S(1)} %collective-permute-done.7, pred[2,16,64]{2,1,0:T(8,128)(4,1)S(1)} %iota_compare_fusion.7), kind=kOutput, calls=%fused_computation.14 | convolution fusion | flops 546308096 | bytes 4851712 | tf_op jit(solution)/shard_map/mnk,hk->mnh/dot_general | solution.py:543
  149.8 9.6 %all-to-all-done.1 = bf16[32,16,1024]{2,1,0:T(8,128)(2,1)} async-done(((bf16[32,16,1024]{2,1,0:T(8,128)(2,1)}), bf16[32,16,1024]{2,1,0:T(8,128)(2,1)}, u32[]{:S(2)}, u32[]{:S(2)}) %all-to-all-start.1) | async-done | bytes 1048608 | tf_op jit(solution)/shard_map/all_to_all | solution.py:462
  159.4 1.4 convert_reduce_fusion.1
  160.9 0.7 collective-permute-start.9
  161.5 2.7 %collective-permute-start.10 = (f32[16,2176]{1,0:T(8,128)S(1)}, f32[16,2176]{1,0:T(8,128)S(1)}, u32[]{:S(2)}, u32[]{:S(2)}) collective-permute-start(f32[16,2176]{1,0:T(8,128)S(1)} %pad_maximum_fusion), channel_id=1, source_target_pairs={{0,32},{32,0},{64,96},{96,64},{1,33},{33,1},{65,97},{97,65},{2,34}... | collective-permute-start | bytes 417800 | tf_op jit(solution)/shard_map/ppermute | solution.py:408
  164.3 2.3 %collective-permute-start.11 = (f32[16,2176]{1,0:T(8,128)S(1)}, f32[16,2176]{1,0:T(8,128)S(1)}, u32[]{:S(2)}, u32[]{:S(2)}) collective-permute-start(f32[16,2176]{1,0:T(8,128)S(1)} %pad_maximum_fusion), channel_id=1, source_target_pairs={{0,96},{32,64},{64,32},{96,0},{1,97},{33,65},{65,33},{97,1},{2,98}... | collective-permute-start | bytes 417800 | tf_op jit(solution)/shard_map/ppermute | solution.py:408
  166.5 0.0 collective-permute-done.9
  166.5 0.0 collective-permute-done.10
  166.6 5.7 %collective-permute-done.11 = f32[16,2176]{1,0:T(8,128)S(1)} collective-permute-done((f32[16,2176]{1,0:T(8,128)S(1)}, f32[16,2176]{1,0:T(8,128)S(1)}, u32[]{:S(2)}, u32[]{:S(2)}) %collective-permute-start.11) | collective-permute-done | bytes 139296 | tf_op jit(solution)/shard_map/ppermute | solution.py:408
  172.3 0.7 slice_multiply_fusion
  173.0 0.6 slice_multiply_fusion.2
  173.6 0.7 slice_reduce_fusion
  (26 shorter events, 0.2 us)
Async XLA Ops:
  2.0 10.1 %collective-permute-start = (bf16[4,16,1024]{2,1,0:T(8,128)(2,1)S(1)}, bf16[4,16,1024]{2,1,0:T(8,128)(2,1)S(1)}, u32[]{:S(2)}, u32[]{:S(2)}) collective-permute-start(bf16[4,16,1024]{2,1,0:T(8,128)(2,1)S(1)} %get-tuple-element.76), channel_id=1, source_target_pairs={{0,1},{1,2},{2,3},{3,4},{4,5},{5,6},{6,7},{7,8},{8,9},{9,10},{10,1... | collective-permute-start | bytes 393224 | tf_op jit(solution)/shard_map/ppermute | solution.py:343
  6.4 5.7 %collective-permute-start.1 = (bf16[4,16,1024]{2,1,0:T(8,128)(2,1)S(1)}, bf16[4,16,1024]{2,1,0:T(8,128)(2,1)S(1)}, u32[]{:S(2)}, u32[]{:S(2)}) collective-permute-start(bf16[4,16,1024]{2,1,0:T(8,128)(2,1)S(1)} %get-tuple-element.75), channel_id=1, source_target_pairs={{1,0},{2,1},{3,2},{4,3},{5,4},{6,5},{7,6},{8,7},{9,8},{10,9},{11,1... | collective-permute-start | bytes 393224 | tf_op jit(solution)/shard_map/ppermute | solution.py:344
  12.1 0.7 copy-start.10
  12.1 0.7 copy-start.11
  39.9 26.9 %collective-permute-start.2 = (f32[4,104,512]{2,1,0:T(8,128)}, f32[4,104,512]{2,1,0:T(8,128)S(1)}, u32[]{:S(2)}, u32[]{:S(2)}) collective-permute-start(f32[4,104,512]{2,1,0:T(8,128)} %get-tuple-element.39.own_ref), channel_id=1, source_target_pairs={{0,64},{32,96},{64,0},{96,32},{1,65},{33,97},{65,1},{97,33},{2,66}... | collective-permute-start | bytes 2555912 | tf_op jit(solution)/shard_map/ppermute | solution.py:408
  43.3 23.6 %collective-permute-start.3 = (f32[4,104,512]{2,1,0:T(8,128)}, f32[4,104,512]{2,1,0:T(8,128)S(1)}, u32[]{:S(2)}, u32[]{:S(2)}) collective-permute-start(f32[4,104,512]{2,1,0:T(8,128)} %get-tuple-element.39.own_ref), channel_id=1, source_target_pairs={{0,32},{32,0},{64,96},{96,64},{1,33},{33,1},{65,97},{97,65},{2,34}... | collective-permute-start | bytes 2555912 | tf_op jit(solution)/shard_map/ppermute | solution.py:408
  45.7 21.3 %copy-start.9 = (bf16[1024,100]{0,1:T(8,128)(2,1)S(1)}, bf16[1024,100]{0,1:T(8,128)(2,1)}, u32[]{:S(2)}) copy-start(bf16[1024,100]{0,1:T(8,128)(2,1)} %param.17) | copy-start | bytes 614404
  45.7 21.4 %copy-start.13 = (f32[512]{0:T(512)S(1)}, f32[512]{0:T(512)}, u32[]{:S(2)}) copy-start(f32[512]{0:T(512)} %param.20) | copy-start | bytes 6148
  45.7 21.4 %copy-start.14 = (f32[100]{0:T(128)S(1)}, f32[100]{0:T(128)}, u32[]{:S(2)}) copy-start(f32[100]{0:T(128)} %param.21) | copy-start | bytes 1204
  45.7 23.8 %copy-start.3 = (f32[4,104,512]{2,1,0:T(8,128)S(1)}, f32[4,104,512]{2,1,0:T(8,128)}, u32[]{:S(2)}) copy-start(f32[4,104,512]{2,1,0:T(8,128)} %get-tuple-element.39.own_ref) | copy-start | bytes 2555908
  45.7 23.8 %copy-start.4 = (f32[100,512]{1,0:T(8,128)S(1)}, f32[100,512]{1,0:T(8,128)}, u32[]{:S(2)}) copy-start(f32[100,512]{1,0:T(8,128)} %truth_ref.1) | copy-start | bytes 614404
  66.9 2.6 %collective-permute-start.4 = (f32[4,104,512]{2,1,0:T(8,128)S(1)}, f32[4,104,512]{2,1,0:T(8,128)}, u32[]{:S(2)}, u32[]{:S(2)}) collective-permute-start(f32[4,104,512]{2,1,0:T(8,128)S(1)} %collective-permute-done.2.chip_ref), channel_id=1, source_target_pairs={{0,32},{32,0},{64,96},{96,64},{1,33},{33,1},{65,97},{97,65},{2,34}... | collective-permute-start | bytes 2555912 | tf_op jit(solution)/shard_map/ppermute | solution.py:408
  69.5 9.3 %copy-start.5 = (bf16[4,512,1024]{2,1,0:T(8,128)(2,1)S(1)}, bf16[4,512,1024]{2,1,0:T(8,128)(2,1)}, u32[]{:S(2)}) copy-start(bf16[4,512,1024]{2,1,0:T(8,128)(2,1)} %get-tuple-element.48.summed_ref) | copy-start | bytes 12582916
  88.1 2.9 %collective-permute-start.5 = (bf16[32,16,1152]{2,1,0:T(8,128)(2,1)S(1)}, bf16[32,16,1152]{2,1,0:T(8,128)(2,1)S(1)}, u32[]{:S(2)}, u32[]{:S(2)}) collective-permute-start(bf16[32,16,1152]{2,1,0:T(8,128)(2,1)S(1)} %get-tuple-element.53), channel_id=1, source_target_pairs={{0,32},{32,0},{64,96},{96,64},{1,33},{33,1},{65,97},{97,65},{2,34}... | collective-permute-start | bytes 3538952 | tf_op jit(solution)/shard_map/ppermute | solution.py:408
  91.0 11.1 %copy-start = (bf16[1024,1024]{1,0:T(8,128)(2,1)S(1)}, bf16[1024,1024]{1,0:T(8,128)(2,1)}, u32[]{:S(2)}) copy-start(bf16[1024,1024]{1,0:T(8,128)(2,1)} %node_ref.3) | copy-start | bytes 6291460
  92.3 30.5 %all-to-all-start = ((bf16[32,16,1152]{2,1,0:T(8,128)(2,1)}), bf16[32,16,1152]{2,1,0:T(8,128)(2,1)}, u32[]{:S(2)}, u32[]{:S(2)}) async-start(bf16[32,16,1152]{2,1,0:T(8,128)(2,1)} %add_convert_fusion), calls=%async_computation | async-start | bytes 2359296 | tf_op jit(solution)/shard_map/all_to_all | solution.py:462
  102.1 1.1 copy-start.7
  120.8 1.0 copy-start.1
  121.8 1.0 copy-start.6
  122.8 20.2 %copy-start.12 = (s32[2,16]{1,0:T(2,128)S(1)}, s32[2,16]{1,0:T(2,128)}, u32[]{:S(2)}) copy-start(s32[2,16]{1,0:T(2,128)} %param.25) | copy-start | bytes 388
  122.8 6.4 %collective-permute-start.6 = (bf16[32,16,1024]{2,1,0:T(8,128)(2,1)}, bf16[32,16,1024]{2,1,0:T(8,128)(2,1)S(1)}, u32[]{:S(2)}, u32[]{:S(2)}) collective-permute-start(bf16[32,16,1024]{2,1,0:T(8,128)(2,1)} %copy-done.6), channel_id=1, source_target_pairs={{0,32},{32,0},{64,96},{96,64},{1,33},{33,1},{65,97},{97,65},{2,34}... | collective-permute-start | bytes 3145736 | tf_op jit(solution)/shard_map/ppermute | solution.py:408
  123.2 7.4 %collective-permute-start.7 = (bf16[4,16,1024]{2,1,0:T(8,128)(2,1)S(1)}, bf16[4,16,1024]{2,1,0:T(8,128)(2,1)S(1)}, u32[]{:S(2)}, u32[]{:S(2)}) collective-permute-start(bf16[4,16,1024]{2,1,0:T(8,128)(2,1)S(1)} %get-tuple-element.64), channel_id=1, source_target_pairs={{1,0},{2,1},{3,2},{4,3},{5,4},{6,5},{7,6},{8,7},{9,8},{10,9},{11,1... | collective-permute-start | bytes 393224 | tf_op jit(solution)/shard_map/ppermute | solution.py:528
  124.5 9.0 %collective-permute-start.8 = (bf16[4,16,1024]{2,1,0:T(8,128)(2,1)S(1)}, bf16[4,16,1024]{2,1,0:T(8,128)(2,1)}, u32[]{:S(2)}, u32[]{:S(2)}) collective-permute-start(bf16[4,16,1024]{2,1,0:T(8,128)(2,1)S(1)} %get-tuple-element.65), channel_id=1, source_target_pairs={{0,1},{1,2},{2,3},{3,4},{4,5},{5,6},{6,7},{7,8},{8,9},{9,10},{10,1... | collective-permute-start | bytes 393224 | tf_op jit(solution)/shard_map/ppermute | solution.py:529
  130.5 16.2 %copy-start.2 = (f32[4,64,1024]{2,1,0:T(8,128)S(1)}, f32[4,64,1024]{2,1,0:T(8,128)}, u32[]{:S(2)}) copy-start(f32[4,64,1024]{2,1,0:T(8,128)} %copy-done.1) | copy-start | bytes 3145732
  130.5 16.2 %copy-start.8 = (bf16[1024,1024]{1,0:T(8,128)(2,1)S(1)}, bf16[1024,1024]{1,0:T(8,128)(2,1)}, u32[]{:S(2)}) copy-start(bf16[1024,1024]{1,0:T(8,128)(2,1)} %project_ref.1) | copy-start | bytes 6291460
  133.5 26.0 %all-to-all-start.1 = ((bf16[32,16,1024]{2,1,0:T(8,128)(2,1)}), bf16[32,16,1024]{2,1,0:T(8,128)(2,1)}, u32[]{:S(2)}, u32[]{:S(2)}) async-start(bf16[32,16,1024]{2,1,0:T(8,128)(2,1)} %add_convert_fusion.1), calls=%async_computation.1 | async-start | bytes 2097152 | tf_op jit(solution)/shard_map/all_to_all | solution.py:462
  160.9 5.7 %collective-permute-start.9 = (f32[16,2176]{1,0:T(8,128)S(1)}, f32[16,2176]{1,0:T(8,128)S(1)}, u32[]{:S(2)}, u32[]{:S(2)}) collective-permute-start(f32[16,2176]{1,0:T(8,128)S(1)} %pad_maximum_fusion), channel_id=1, source_target_pairs={{0,64},{32,96},{64,0},{96,32},{1,65},{33,97},{65,1},{97,33},{2,66}... | collective-permute-start | bytes 417800 | tf_op jit(solution)/shard_map/ppermute | solution.py:408
  161.5 5.0 %collective-permute-start.10 = (f32[16,2176]{1,0:T(8,128)S(1)}, f32[16,2176]{1,0:T(8,128)S(1)}, u32[]{:S(2)}, u32[]{:S(2)}) collective-permute-start(f32[16,2176]{1,0:T(8,128)S(1)} %pad_maximum_fusion), channel_id=1, source_target_pairs={{0,32},{32,0},{64,96},{96,64},{1,33},{33,1},{65,97},{97,65},{2,34}... | collective-permute-start | bytes 417800 | tf_op jit(solution)/shard_map/ppermute | solution.py:408
  164.3 8.0 %collective-permute-start.11 = (f32[16,2176]{1,0:T(8,128)S(1)}, f32[16,2176]{1,0:T(8,128)S(1)}, u32[]{:S(2)}, u32[]{:S(2)}) collective-permute-start(f32[16,2176]{1,0:T(8,128)S(1)} %pad_maximum_fusion), channel_id=1, source_target_pairs={{0,96},{32,64},{64,32},{96,0},{1,97},{33,65},{65,33},{97,1},{2,98}... | collective-permute-start | bytes 417800 | tf_op jit(solution)/shard_map/ppermute | solution.py:408
